TPU v7x, 32 devices: a whole 2x2x4 slice. The times are simulated.
32 devices in a mesh: frag: 2 (over y), space: 4 (over z), aux: 2 (over x), sub: 2 (over core).
Axes of the slice: x: 2, y: 2, z: 4, core: 2. Of those that a mesh axis runs over, the one named last changes fastest.
Arguments:
- densities: bfloat16 [128, 128, 256], P(('frag', 'space', 'sub')), parts along dimension 0, may hold values from -6 to 6
- three_centre: bfloat16 [128, 24, 128, 128], P(('frag', 'space', 'sub'), 'aux'), parts along dimension 0, may hold values from -0.0625 to 0.0625
- block_tile: int32 [128, 24], P(('frag', 'space', 'sub'), 'aux'), parts along dimension 0, may hold values from 0 to 31
- owner_domain: int32 [16, 2, 32, 1], P(('frag', 'space', 'sub'), 'aux'), parts along dimension 0, may hold values from 0 to 3; in each aligned block of 32 rows (0 to 31, 32 to 63, ..., all dimensions but the last counted through in order) at most 16 rows name the same one
- owner_tile: int32 [16, 2, 32], P(('frag', 'space', 'sub'), 'aux'), parts along dimension 0, may hold values from 0 to 2
- metric_inverse: bfloat16 [48, 8, 128, 128], P(('frag', 'space', 'aux'), 'sub'), parts along dimension 0, may hold values from -0.1875 to 0.1875
- metric_columns: int32 [48, 8], P(('frag', 'space', 'aux'), 'sub'), parts along dimension 0, may hold values from 0 to 17
Outputs:
- coulomb: bfloat16 [128, 128, 256], P(('frag', 'space', 'sub'), 'aux'), parts along dimension 0
There are 2 independent parts, one for each index of `frag`. A program takes and returns all parts, laid end to end along the dimension named above; each array names one. Nothing has to cross between parts.
Inputs may be any that keep to these rules, and one draw needn't show every extreme that they name: `block_tile`: index into the 32 touched tiles of the device holding the block. `owner_domain`: among the 32 touched tiles of one device at most 16 name the same domain; some device has exactly 16.
All inputs are finite; a program needn't handle non-finite values.
Results may differ from a plain program's by a relative error of at most 0.019.
Values may be sent and summed in bfloat16 or wider, within the bound.
No kernel may reach another device: no remote copies, remote signals or barrier semaphores. Data moves between devices by JAX's collectives and lax.ppermute only.
A program may use at most 64 MiB of HBM per device.

v0:
```python
import jax
import jax.numpy as jnp
from jax import lax
from jax.sharding import PartitionSpec as P


def with_halo(block, sides, width):
    for axis, dim in sides:
        count = lax.axis_size(axis)
        forward = [(i, i + 1) for i in range(count - 1)]
        backward = [(target, source) for source, target in forward]
        low = lax.ppermute(
            lax.slice_in_dim(block, block.shape[dim] - width, None, axis=dim), axis, forward
        )
        high = lax.ppermute(lax.slice_in_dim(block, 0, width, axis=dim), axis, backward)
        block = jnp.concatenate([low, block, high], axis=dim)
    return block


def shards(
    densities, three_centre, block_tile, owner_domain, owner_tile, metric_inverse, metric_columns
):
    domains = lax.axis_size("space")
    touched = owner_tile.shape[-1]
    owned_tiles = metric_inverse.shape[0]
    tile_width = densities.shape[1]
    columns = densities.shape[2]
    capacity = 2 * touched // domains
    slot_count = domains * capacity
    contrib = jnp.einsum(
        "pkrc,prn->pkcn", three_centre, densities, preferred_element_type=jnp.float32
    )
    contrib_high = contrib.astype(jnp.bfloat16)
    contrib_low = (contrib - contrib_high.astype(jnp.float32)).astype(jnp.bfloat16)
    touched_range = jnp.arange(touched, dtype=jnp.int32)
    chooser = (block_tile[:, :, None] == touched_range[None, None, :]).astype(jnp.bfloat16)
    partial_high = jnp.einsum(
        "pkt,pkcn->tcn", chooser, contrib_high, preferred_element_type=jnp.float32
    )
    partial_low = jnp.einsum(
        "pkt,pkcn->tcn", chooser, contrib_low, preferred_element_type=jnp.float32
    )
    partial_sum = (partial_high + partial_low).astype(jnp.bfloat16)
    target = owner_domain.reshape(touched)
    own_tile = owner_tile.reshape(touched)
    earlier = (target[:, None] == target[None, :]) & (
        touched_range[None, :] < touched_range[:, None]
    )
    position = target * capacity + jnp.sum(earlier.astype(jnp.int32), axis=1)
    placing = (position[:, None] == jnp.arange(slot_count, dtype=jnp.int32)[None, :]).astype(
        jnp.bfloat16
    )
    tile_marks = (own_tile[:, None] == jnp.arange(owned_tiles, dtype=jnp.int32)[None, :]).astype(
        jnp.bfloat16
    )
    outgoing = jnp.einsum(
        "ts,tcn->scn", placing, partial_sum, preferred_element_type=jnp.float32
    ).astype(jnp.bfloat16)
    labels = jnp.einsum(
        "ts,tu->su", placing, tile_marks, preferred_element_type=jnp.float32
    ).astype(jnp.bfloat16)
    arrived, arrived_labels = (
        lax.all_to_all(
            outgoing.reshape(domains, capacity, tile_width, columns),
            "space",
            split_axis=0,
            concat_axis=0,
            tiled=True,
        ),
        lax.all_to_all(
            labels.reshape(domains, capacity, owned_tiles),
            "space",
            split_axis=0,
            concat_axis=0,
            tiled=True,
        ),
    )
    own_sum = jnp.einsum(
        "scu,scrn->urn", arrived_labels, arrived, preferred_element_type=jnp.float32
    )
    fitted = lax.psum(own_sum.astype(jnp.bfloat16), "sub")
    domain_tiles = lax.all_gather(fitted, "aux", axis=0, tiled=True)
    window = with_halo(domain_tiles[None], (("space", 0),), 1)
    window = window.reshape(-1, tile_width, columns)
    chosen = window[metric_columns]
    metric_terms = jnp.einsum(
        "qjcr,qjrn->qcn", metric_inverse, chosen, preferred_element_type=jnp.float32
    )
    coefficients = lax.psum(metric_terms.astype(jnp.bfloat16), "sub")
    every_tile = lax.all_gather(coefficients, "space", axis=0, tiled=True)
    needed = every_tile[target * owned_tiles + own_tile]
    picked = needed[block_tile]
    coulomb = jnp.einsum("pkrc,pkcn->prn", three_centre, picked, preferred_element_type=jnp.float32)
    return lax.psum_scatter(coulomb.astype(jnp.bfloat16), "aux", scatter_dimension=1, tiled=True)


def solution(mesh):
    placed = (
        P(("frag", "space", "sub"), None, None),
        P(("frag", "space", "sub"), "aux", None, None),
        P(("frag", "space", "sub"), "aux"),
        P(("frag", "space", "sub"), "aux", None, None),
        P(("frag", "space", "sub"), "aux", None),
        P(("frag", "space", "aux"), "sub", None, None),
        P(("frag", "space", "aux"), "sub"),
    )
    return jax.shard_map(
        shards,
        mesh=mesh,
        in_specs=placed,
        out_specs=P(("frag", "space", "sub"), "aux", None),
        check_vma=False,
    )
```

profile of v0, /device:TPU:0, one launch (start us, length us, event | category | flops | bytes accessed | tf_op | source)
XLA Modules:
  0.0 273.4 jit_solution(1166276536944532797)
XLA Ops:
  9.8 6.3 %all-to-all-start = ((bf16[4,16,3]{1,2,0:T(4,128)(2,1)}), bf16[4,16,3]{1,2,0:T(4,128)(2,1)S(1)}, u32[]{:S(2)}, u32[]{:S(2)}) async-start(bf16[4,16,3]{1,2,0:T(4,128)(2,1)} %copy.28), calls=%async_computation | async-start | bytes 8192 | tf_op jit(solution)/shard_map/all_to_all | solution.py:70
  16.1 5.5 %subtract_convert_fusion = (bf16[8,12,128,256]{3,2,1,0:T(8,128)(2,1)S(1)}, bf16[8,12,128,256]{3,2,1,0:T(8,128)(2,1)}) fusion(bf16[8,12,128,128]{3,2,1,0:T(8,128)(2,1)S(1)} %copy-done, bf16[8,128,256]{2,1,0:T(8,128)(2,1)} %param.7), kind=kOutput, calls=%fused_computation.3 | convolution fusion | flops 817889280 | bytes 16252928 | tf_op jit(solution)/shard_map/pkrc,prn->pkcn/dot_general | solution.py:30
  21.7 6.2 %fusion = f32[32,128,256,1]{2,0,3,1:T(8,128)} fusion(bf16[8,12,128,256]{3,2,1,0:T(8,128)(2,1)S(1)} %get-tuple-element.5, s32[8,12]{1,0:T(8,128)S(1)} %copy-done.1), kind=kOutput, calls=%fused_computation.4 | convolution fusion | flops 201329664 | bytes 10486144 | tf_op jit(solution)/shard_map/pkt,pkcn->tcn/dot_general | solution.py:40
  27.9 11.6 %convolution_convert_fusion = bf16[64,128,256]{2,0,1:T(8,128)(2,1)} fusion(f32[32,128,256,1]{2,0,3,1:T(8,128)} %fusion, bf16[8,12,128,256]{3,2,1,0:T(8,128)(2,1)} %get-tuple-element.6, s32[8,12]{1,0:T(8,128)S(1)} %copy-done.1, s32[32]{0:T(128)S(1)} %multiply_add_fusion), kind=kOutput, calls=%fused_computation.10 | convolution fusion | flops 339743744 | bytes 14680576 | tf_op jit(solution)/shard_map/ts,tcn->scn/dot_general | solution.py:56
  39.5 4.5 %copy.32 = bf16[4,16,128,256]{3,1,2,0:T(8,128)(2,1)} copy(bf16[4,16,128,256]{3,1,0,2:T(8,128)(2,1)} %bitcast.82) | data formatting | bytes 8388608 | tf_op jit(solution)/shard_map/reshape | solution.py:64
  44.1 97.9 %all_to_all.10 = bf16[4,16,128,256]{3,1,2,0:T(8,128)(2,1)S(1)} all-to-all(bf16[4,16,128,256]{3,1,2,0:T(8,128)(2,1)} %copy.32), channel_id=1, replica_groups=mesh['frag'=2,'space'=4,'aux'=2,'sub'=2] {'space'}, dimensions={0} | all-to-all | bytes 8388608 | tf_op jit(solution)/shard_map/all_to_all | solution.py:63
  141.9 1.4 fusion.11
  143.4 17.3 %all-reduce.3.cloned.1.call-done = bf16[3,128,256]{2,0,1:T(4,128)(2,1)} async-done(((bf16[3,128,256]{2,0,1:T(4,128)(2,1)}), bf16[3,128,256]{2,0,1:T(4,128)(2,1)}) %all-reduce.3.cloned.1.call-update) | async-done | bytes 196624 | tf_op jit(solution)/shard_map/psum | solution.py:81
  161.7 7.8 %all_gather.6 = bf16[6,128,256]{2,1,0:T(8,128)(2,1)S(1)} all-gather(bf16[3,128,256]{2,1,0:T(8,128)(2,1)S(1)} %copy.34), channel_id=1, replica_groups=mesh['frag'=2,'space'=4,'aux'=2,'sub'=2] {'aux'}, dimensions={0}, use_global_device_ids=true | all-gather | bytes 589824 | tf_op jit(solution)/shard_map/all_gather | solution.py:82
  169.4 4.4 %collective-permute-start = (bf16[1,6,128,256]{3,2,1,0:T(8,128)(2,1)S(1)}, bf16[1,6,128,256]{3,2,1,0:T(8,128)(2,1)}, u32[]{:S(2)}, u32[]{:S(2)}) collective-permute-start(bf16[1,6,128,256]{3,2,1,0:T(8,128)(2,1)S(1)} %bitcast.85), channel_id=1, source_target_pairs={{0,4},{4,8},{8,12},{1,5},{5,9},{9,13},{2,6},{6,10},{10,14},{3,7},{... | collective-permute-start | bytes 1179656 | tf_op jit(solution)/shard_map/ppermute | solution.py:12
  173.9 1.3 collective-permute-start.1
  176.0 5.1 %collective-permute-done = bf16[1,6,128,256]{3,2,1,0:T(8,128)(2,1)} collective-permute-done((bf16[1,6,128,256]{3,2,1,0:T(8,128)(2,1)S(1)}, bf16[1,6,128,256]{3,2,1,0:T(8,128)(2,1)}, u32[]{:S(2)}, u32[]{:S(2)}) %collective-permute-start) | collective-permute-done | bytes 393248 | tf_op jit(solution)/shard_map/ppermute | solution.py:12
  181.1 5.0 %collective-permute-done.1 = bf16[1,6,128,256]{3,2,1,0:T(8,128)(2,1)} collective-permute-done((bf16[1,6,128,256]{3,2,1,0:T(8,128)(2,1)S(1)}, bf16[1,6,128,256]{3,2,1,0:T(8,128)(2,1)}, u32[]{:S(2)}, u32[]{:S(2)}) %collective-permute-start.1) | collective-permute-done | bytes 393248 | tf_op jit(solution)/shard_map/ppermute | solution.py:15
  186.1 2.3 pad_maximum_fusion
  188.4 2.8 %gather_fusion = bf16[12,128,256]{2,1,0:T(8,128)(2,1)} fusion(bf16[18,128,256]{2,1,0:T(8,128)(2,1)} %bitcast.83, s32[1024]{0:T(1024)S(1)} %pad_clamp_fusion.2), kind=kCustom, calls=%fused_computation | custom fusion | bytes 1572912 | tf_op jit(solution)/shard_map/gather | solution.py:85
  191.2 2.3 fusion.13
  193.6 17.4 %all-reduce.5.cloned.1.call-done = bf16[3,128,256]{1,2,0:T(8,128)(2,1)} async-done(((bf16[3,128,256]{1,2,0:T(8,128)(2,1)}), bf16[3,128,256]{1,2,0:T(8,128)(2,1)}) %all-reduce.5.cloned.1.call-update) | async-done | bytes 196624 | tf_op jit(solution)/shard_map/psum | solution.py:89
  212.1 20.2 %all_gather.7 = bf16[12,128,256]{2,1,0:T(8,128)(2,1)} all-gather(bf16[3,128,256]{2,1,0:T(8,128)(2,1)S(1)} %copy.36), channel_id=1, replica_groups=mesh['frag'=2,'space'=4,'aux'=2,'sub'=2] {'space'}, dimensions={0}, use_global_device_ids=true | all-gather | bytes 983040 | tf_op jit(solution)/shard_map/all_gather | solution.py:90
  232.3 3.2 %gather_fusion.1 = bf16[32,128,256]{2,1,0:T(8,128)(2,1)} fusion(bf16[12,128,256]{2,1,0:T(8,128)(2,1)} %all_gather.7, s32[1024]{0:T(1024)S(1)} %pad_clamp_fusion.1), kind=kCustom, calls=%fused_computation.1 | custom fusion | bytes 4194432 | tf_op jit(solution)/shard_map/gather | solution.py:91
  235.5 7.6 %gather_fusion.2 = bf16[96,128,256]{2,1,0:T(8,128)(2,1)} fusion(bf16[32,128,256]{2,1,0:T(8,128)(2,1)} %gather_fusion.1, s32[1024]{0:T(1024)S(1)} %pad_clamp_fusion), kind=kCustom, calls=%fused_computation.2 | custom fusion | bytes 12583296 | tf_op jit(solution)/shard_map/gather | solution.py:92
  243.1 5.6 %fusion.10 = bf16[8,128,256]{1,2,0:T(8,128)(2,1)} fusion(bf16[8,12,128,256]{3,2,1,0:T(8,128)(2,1)} %bitcast.81, bf16[8,12,128,128]{3,2,1,0:T(8,128)(2,1)S(1)} %copy-done), kind=kOutput, calls=%fused_computation.14 | convolution fusion | flops 805568512 | bytes 9961472 | tf_op jit(solution)/shard_map/pkrc,pkcn->prn/dot_general | solution.py:93
  248.7 2.2 copy.38
  250.9 14.3 %reduce-scatter.2.cloned.1.call-done = bf16[8,64,256]{2,0,1:T(8,128)(2,1)} async-done(((bf16[8,128,256]{2,0,1:T(8,128)(2,1)}), bf16[8,64,256]{2,0,1:T(8,128)(2,1)}) %reduce-scatter.2.cloned.1.call-update) | async-done | bytes 262160 | tf_op jit(solution)/shard_map/reduce_scatter | solution.py:94
  265.2 1.7 copy.39
  (30 shorter events, 6.3 us)
Async XLA Ops:
  6.5 9.6 %copy-start = (bf16[8,12,128,128]{3,2,1,0:T(8,128)(2,1)S(1)}, bf16[8,12,128,128]{3,2,1,0:T(8,128)(2,1)}, u32[]{:S(2)}) copy-start(bf16[8,12,128,128]{3,2,1,0:T(8,128)(2,1)} %param.8) | copy-start | bytes 9437188
  9.8 34.3 %all-to-all-start = ((bf16[4,16,3]{1,2,0:T(4,128)(2,1)}), bf16[4,16,3]{1,2,0:T(4,128)(2,1)S(1)}, u32[]{:S(2)}, u32[]{:S(2)}) async-start(bf16[4,16,3]{1,2,0:T(4,128)(2,1)} %copy.28), calls=%async_computation | async-start | bytes 8192 | tf_op jit(solution)/shard_map/all_to_all | solution.py:70
  16.1 5.6 %copy-start.1 = (s32[8,12]{1,0:T(8,128)S(1)}, s32[8,12]{1,0:T(8,128)}, u32[]{:S(2)}) copy-start(s32[8,12]{1,0:T(8,128)} %param.9) | copy-start | bytes 1156
  16.1 144.6 %all-reduce.3.cloned.1.call-start = ((), (), s32[]{:S(2)}) async-start(), calls=%async_computation.3 | async-start | bytes 524288 | tf_op jit(solution)/shard_map/psum | solution.py:81
  141.9 33.3 %copy-start.2 = (s32[3,4]{1,0:T(4,128)S(1)}, s32[3,4]{1,0:T(4,128)}, u32[]{:S(2)}) copy-start(s32[3,4]{1,0:T(4,128)} %param.13) | copy-start | bytes 148
  141.9 33.4 %copy-start.3 = (s32[1,1,32,1]{2,3,1,0:T(1,128)S(1)}, s32[1,1,32,1]{2,3,1,0:T(1,128)}, u32[]{:S(2)}) copy-start(s32[1,1,32,1]{2,3,1,0:T(1,128)} %param.10) | copy-start | bytes 388
  143.4 67.7 %all-reduce.5.cloned.1.call-start = ((), (), s32[]{:S(2)}) async-start(), calls=%async_computation.4 | async-start | bytes 393216 | tf_op jit(solution)/shard_map/psum | solution.py:89
  169.4 11.7 %collective-permute-start = (bf16[1,6,128,256]{3,2,1,0:T(8,128)(2,1)S(1)}, bf16[1,6,128,256]{3,2,1,0:T(8,128)(2,1)}, u32[]{:S(2)}, u32[]{:S(2)}) collective-permute-start(bf16[1,6,128,256]{3,2,1,0:T(8,128)(2,1)S(1)} %bitcast.85), channel_id=1, source_target_pairs={{0,4},{4,8},{8,12},{1,5},{5,9},{9,13},{2,6},{6,10},{10,14},{3,7},{... | collective-permute-start | bytes 1179656 | tf_op jit(solution)/shard_map/ppermute | solution.py:12
  173.9 12.2 %collective-permute-start.1 = (bf16[1,6,128,256]{3,2,1,0:T(8,128)(2,1)S(1)}, bf16[1,6,128,256]{3,2,1,0:T(8,128)(2,1)}, u32[]{:S(2)}, u32[]{:S(2)}) collective-permute-start(bf16[1,6,128,256]{3,2,1,0:T(8,128)(2,1)S(1)} %bitcast.86), channel_id=1, source_target_pairs={{4,0},{8,4},{12,8},{5,1},{9,5},{13,9},{6,2},{10,6},{14,10},{7,3},{... | collective-permute-start | bytes 1179656 | tf_op jit(solution)/shard_map/ppermute | solution.py:15
  193.6 71.6 %reduce-scatter.2.cloned.1.call-start = ((), (), s32[]{:S(2)}) async-start(), calls=%async_computation.5 | async-start | bytes 786432 | tf_op jit(solution)/shard_map/reduce_scatter | solution.py:94
Sparse Core Ops, SparseCore 0:
  143.5 17.1 all-reduce.2
  193.7 17.3 all-reduce.4
  251.0 14.1 reduce-scatter.1
where the time goes:
time: 274 us; the launch traced here: 273 us
  blocking collectives  126 us (46%)
  waiting for transfers between devices  59.1 us (22%)
  matrix products  33.7 us (12%)
  local copies, waits for them, and re-layouts  24.9 us (9%)
  between operations  13.2 us (5%)
  starting transfers between devices  12.1 us (4%)
  other arithmetic  4.62 us (2%)
    all_to_all x1, blocking collectives, shards(): lax.all_to_all(outgoing.reshape(domains, capacity, tile_width, columns),...  97.9 us
    all_gather x1, blocking collectives, shards(): every_tile = lax.all_gather(coefficients, 'space', axis=0, tiled=True)  20.2 us
    psum x1, waiting for transfers between devices, shards(): coefficients = lax.psum(metric_terms.astype(jnp.bfloat16), 'sub')  17.4 us
    psum x1, waiting for transfers between devices, shards(): fitted = lax.psum(own_sum.astype(jnp.bfloat16), 'sub')  17.3 us
    reduce_scatter x1, waiting for transfers between devices, shards(): lax.psum_scatter(coulomb.astype(jnp.bfloat16), 'aux', scatter_dimension=1...  14.3 us
    dot_general x1, matrix products, shards(): jnp.einsum('ts,tcn->scn', placing, partial_sum, preferred_element_type=jn...  11.6 us
    all_gather x1, blocking collectives, shards(): domain_tiles = lax.all_gather(fitted, 'aux', axis=0, tiled=True)  7.75 us
    gather x1, local copies, waits for them, and re-layouts, shards(): picked = needed[block_tile]  7.6 us
  transfers between devices with their start and end apart: 6, of which 5 were waited for; matrix products, arithmetic and copies ran while one was open for 11% of the time, Pallas kernels for 0%

commit v1 on v0

v1 whole, which is shorter than its diff:
```python
import functools

import jax
import jax.numpy as jnp
from jax import lax
from jax.experimental import pallas as pl
from jax.experimental.pallas import tpu as pltpu
from jax.sharding import PartitionSpec as P

BF16 = jnp.bfloat16
F32 = jnp.float32
NT = (((1,), (1,)), ((), ()))
VMEM_LIMIT = 48 * 1024 * 1024


def fit_kernel(owned, half, tile_ref, domain_ref, number_ref, d_ref, t_ref, keep_ref, send_ref, acc):
    step = pl.program_id(0)
    me = lax.axis_index("space")
    mine = lax.axis_index("sub")
    listed = t_ref.shape[1]

    @pl.when(step == 0)
    def _():
        acc[...] = jnp.zeros_like(acc)

    rows = jnp.transpose(d_ref[0])
    for k in range(listed):
        touched = tile_ref[step, k]
        slot = jnp.bitwise_xor(domain_ref[touched], me) * owned + number_ref[touched]
        acc[slot] += jnp.dot(rows, t_ref[0, k], preferred_element_type=F32)

    @pl.when(step == pl.num_programs(0) - 1)
    def _():
        keep_ref[...] = acc[:, pl.ds(pl.multiple_of(mine * half, half), half), :].astype(BF16)
        send_ref[...] = acc[:, pl.ds(pl.multiple_of((1 - mine) * half, half), half), :].astype(BF16)


def fit(block_tile, domain, number, densities, three_centre, domains, owned):
    blocks, listed, width, _ = three_centre.shape
    columns = densities.shape[2]
    half = columns // 2
    slots = domains * owned
    out = jax.ShapeDtypeStruct((slots, half, width), BF16)
    return pl.pallas_call(
        functools.partial(fit_kernel, owned, half),
        grid_spec=pltpu.PrefetchScalarGridSpec(
            num_scalar_prefetch=3,
            grid=(blocks,),
            in_specs=[
                pl.BlockSpec((1, width, columns), lambda p, *_: (p, 0, 0)),
                pl.BlockSpec((1, listed, width, width), lambda p, *_: (p, 0, 0, 0)),
            ],
            out_specs=[pl.BlockSpec((slots, half, width), lambda p, *_: (0, 0, 0))] * 2,
            scratch_shapes=[pltpu.VMEM((slots, columns, width), F32)],
        ),
        out_shape=[out, out],
        compiler_params=pltpu.CompilerParams(vmem_limit_bytes=VMEM_LIMIT),
        cost_estimate=pl.CostEstimate(
            flops=2 * blocks * listed * width * width * columns,
            bytes_accessed=2 * (three_centre.size + densities.size),
            transcendentals=0,
        ),
        name="fit",
    )(block_tile, domain, number, densities, three_centre)


def metric_kernel(owned, count, mine_cols, peer_cols, near_ref, even_ref, odd_ref, m_ref, pm_ref, out_ref, window):
    me = lax.axis_index("space")
    aux = lax.axis_index("aux")
    own = owned * count
    window[:own] = near_ref[...]
    window[own : 2 * own] = even_ref[...]
    window[2 * own :] = odd_ref[...]

    def place(column):
        zone = column // own
        rest = column % own
        side = jnp.where((zone == 2) == (me % 2 == 0), 1, 2)
        block = jnp.where(zone == 1, 0, side)
        turned = (rest // owned + count - aux) % count
        return block * own + turned * owned + rest % owned

    for q in range(m_ref.shape[0]):
        picked, blocks = [], []
        for cols, mat in ((mine_cols, m_ref), (peer_cols, pm_ref)):
            for m in range(mat.shape[1]):
                picked.append(window[place(cols[q, m])])
                blocks.append(mat[q, m])
        out_ref[q] = lax.dot_general(
            jnp.concatenate(picked, axis=1),
            jnp.concatenate(blocks, axis=1),
            NT,
            preferred_element_type=F32,
        ).astype(BF16)


def metric(mine_cols, peer_cols, near, even, odd, m, pm, count):
    owned, listed, width, _ = m.shape
    half = near.shape[1]
    return pl.pallas_call(
        functools.partial(metric_kernel, owned, count),
        in_specs=[pl.BlockSpec(memory_space=pltpu.SMEM)] * 2 + [pl.BlockSpec(memory_space=pltpu.VMEM)] * 5,
        out_specs=pl.BlockSpec(memory_space=pltpu.VMEM),
        out_shape=jax.ShapeDtypeStruct((owned, half, width), BF16),
        scratch_shapes=[pltpu.VMEM((3 * owned * count, half, width), BF16)],
        compiler_params=pltpu.CompilerParams(vmem_limit_bytes=VMEM_LIMIT),
        cost_estimate=pl.CostEstimate(
            flops=4 * owned * listed * width * width * half,
            bytes_accessed=4 * m.size + 6 * near.size,
            transcendentals=0,
        ),
        name="metric",
    )(mine_cols, peer_cols, near, even, odd, m, pm)


def build_kernel(owned, half, pieces, tile_ref, domain_ref, number_ref, t_ref, *rest):
    piece_refs, (out_ref, table, sems) = rest[: 2 * pieces], rest[2 * pieces :]
    step = pl.program_id(0)
    me = lax.axis_index("space")
    mine = lax.axis_index("sub")

    @pl.when(step == 0)
    def _():
        copies = []
        for k in range(pieces):
            for side in range(2):
                start = mine * half if side == 0 else (1 - mine) * half
                copies.append(
                    pltpu.make_async_copy(
                        piece_refs[side * pieces + k],
                        table.at[pl.ds(k * owned, owned), pl.ds(pl.multiple_of(start, half), half), :],
                        sems.at[side * pieces + k],
                    )
                )
        for copy in copies:
            copy.start()
        for copy in copies:
            copy.wait()

    left, right = [], []
    for k in range(t_ref.shape[1]):
        touched = tile_ref[step, k]
        slot = jnp.bitwise_xor(domain_ref[touched], me) * owned + number_ref[touched]
        left.append(t_ref[0, k])
        right.append(table[slot])
    out_ref[0] = lax.dot_general(
        jnp.concatenate(left, axis=1), jnp.concatenate(right, axis=1), NT, preferred_element_type=F32
    ).astype(out_ref.dtype)


def build(block_tile, domain, number, three_centre, pieces, ahead, parts, name):
    blocks, listed, width, _ = three_centre.shape
    owned, half, _ = pieces[0].shape
    count = len(pieces) // 2
    rows = width // parts
    columns = 2 * half
    return pl.pallas_call(
        functools.partial(build_kernel, owned, half, count),
        grid_spec=pltpu.PrefetchScalarGridSpec(
            num_scalar_prefetch=3,
            grid=(blocks,),
            in_specs=[
                pl.BlockSpec(
                    (1, listed, rows, width),
                    lambda p, *_: (p, 0, lax.rem(lax.axis_index("aux") + ahead, parts), 0),
                )
            ]
            + [pl.BlockSpec(memory_space=pl.ANY)] * len(pieces),
            out_specs=pl.BlockSpec((1, rows, columns), lambda p, *_: (p, 0, 0)),
            scratch_shapes=[
                pltpu.VMEM((count * owned, columns, width), BF16),
                pltpu.SemaphoreType.DMA((len(pieces),)),
            ],
        ),
        out_shape=jax.ShapeDtypeStruct((blocks, rows, columns), BF16),
        compiler_params=pltpu.CompilerParams(vmem_limit_bytes=VMEM_LIMIT),
        cost_estimate=pl.CostEstimate(
            flops=2 * blocks * listed * width * rows * columns,
            bytes_accessed=2 * (three_centre.size // parts + blocks * rows * columns),
            transcendentals=0,
        ),
        name=name,
    )(block_tile, domain, number, three_centre, *pieces)


def exchange(array, axis, distance):
    return lax.ppermute(array, axis, [(i, i ^ distance) for i in range(lax.axis_size(axis))])


def ahead_by(array, axis, distance):
    count = lax.axis_size(axis)
    return lax.ppermute(array, axis, [(i, (i + distance) % count) for i in range(count)])


def pairs_from(array, axis, first):
    swaps = []
    for low in range(first, lax.axis_size(axis) - 1, 2):
        swaps += [(low, low + 1), (low + 1, low)]
    return lax.ppermute(array, axis, swaps)


def shards(
    densities, three_centre, block_tile, owner_domain, owner_tile, metric_inverse, metric_columns
):
    domains = lax.axis_size("space")
    aux_count = lax.axis_size("aux")
    touched = owner_tile.shape[-1]
    owned, _, width, _ = metric_inverse.shape
    half = densities.shape[2] // 2
    domain = owner_domain.reshape(touched)
    number = owner_tile.reshape(touched)

    peer_metric = exchange(metric_inverse, "sub", 1)
    peer_columns = exchange(metric_columns, "sub", 1)

    keep, send = fit(block_tile, domain, number, densities, three_centre, domains, owned)
    got = exchange(send, "sub", 1)
    chip = (keep.astype(F32) + got.astype(F32)).astype(BF16).reshape(domains, owned, half, width)
    arrived = [exchange(chip[k], "space", k) for k in range(1, domains)]
    total = chip[0].astype(F32)
    for piece in arrived:
        total = total + piece.astype(F32)
    fitted = total.astype(BF16)

    near = jnp.concatenate(
        [fitted] + [ahead_by(fitted, "aux", aux_count - k) for k in range(1, aux_count)]
    )
    even = pairs_from(near, "space", 0)
    odd = pairs_from(near, "space", 1)
    coefficients = metric(
        metric_columns, peer_columns, near, even, odd, metric_inverse, peer_metric, aux_count
    )

    pieces = [coefficients] + [exchange(coefficients, "space", k) for k in range(1, domains)]
    pieces = pieces + [exchange(piece, "sub", 1) for piece in pieces]

    rows = []
    for ahead in list(range(1, aux_count)) + [0]:
        part = build(block_tile, domain, number, three_centre, pieces, ahead, aux_count, f"build_{ahead}")
        rows.append(ahead_by(part, "aux", ahead) if ahead else part)
    result = rows[-1].astype(F32)
    for part in rows[:-1]:
        result = result + part.astype(F32)
    return result.astype(BF16)


def solution(mesh):
    placed = (
        P(("frag", "space", "sub"), None, None),
        P(("frag", "space", "sub"), "aux", None, None),
        P(("frag", "space", "sub"), "aux"),
        P(("frag", "space", "sub"), "aux", None, None),
        P(("frag", "space", "sub"), "aux", None),
        P(("frag", "space", "aux"), "sub", None, None),
        P(("frag", "space", "aux"), "sub"),
    )
    return jax.shard_map(
        shards,
        mesh=mesh,
        in_specs=placed,
        out_specs=P(("frag", "space", "sub"), "aux", None),
        check_vma=False,
    )
```

time: 274 us -> 64.1 us (0.23)
  blocking collectives: 126 us -> 0 us
  waiting for transfers between devices: 59.1 us -> 24.6 us
  matrix products: 33.7 us -> 0 us
  local copies, waits for them, and re-layouts: 24.9 us -> 4.97 us
  Pallas kernels: 0 us -> 14.3 us
  between operations: 13.2 us -> 0.12 us
  starting transfers between devices: 12.1 us -> 18.9 us
  other arithmetic: 4.62 us -> 0.95 us
    all_to_all x1 -> x0, blocking collectives: 97.9 us -> none  [shards(): lax.all_to_all(outgoing.reshape(domains, capacity, tile_width, columns),...]
    psum x2 -> x0, waiting for transfers between devices: 34.7 us -> none  [the longest x1 17.4 us: shards(): coefficients = lax.psum(metric_terms.astype(jnp.bfloat16), 'sub')]
    dot_general x7 -> x0, matrix products: 33.7 us -> none  [the longest x1 11.6 us: shards(): jnp.einsum('ts,tcn->scn', placing, partial_sum, preferred_element_type=jn...]
    all_gather x2 -> x0, blocking collectives: 27.9 us -> none  [the longest x1 20.2 us: shards(): every_tile = lax.all_gather(coefficients, 'space', axis=0, tiled=True)]
    ppermute x2 -> x17, waiting for transfers between devices: 10.1 us -> 24.6 us  [the longest x13 16.9 us: exchange(): lax.ppermute(array, axis, [(i, i ^ distance) for i in range(lax.axis_size...]
    pallas_call x0 -> x4, Pallas kernels: none -> 14.3 us  [the longest x2 8.96 us: build(): pl.pallas_call(functools.partial(build_kernel, owned, half, count), grid_...]
    reduce_scatter x1 -> x0, waiting for transfers between devices: 14.3 us -> none  [shards(): lax.psum_scatter(coulomb.astype(jnp.bfloat16), 'aux', scatter_dimension=1...]
    gather x3 -> x0, local copies, waits for them, and re-layouts: 13.6 us -> none  [the longest x1 7.6 us: shards(): picked = needed[block_tile]]
  transfers between devices with their start and end apart: 6 -> 17, of which waited for: 5 -> 11; matrix products, arithmetic and copies ran while one was open for 11% -> 0% of each run, Pallas kernels for 0% -> 7%
where the time goes in v1:
time: 64.1 us; the launch traced here: 63.9 us
  waiting for transfers between devices  24.6 us (38%)
  starting transfers between devices  18.9 us (29%)
  Pallas kernels  14.3 us (22%)
  local copies, waits for them, and re-layouts  4.97 us (8%)
  other arithmetic  0.95 us (1%)
    ppermute x13, waiting for transfers between devices, exchange(): lax.ppermute(array, axis, [(i, i ^ distance) for i in range(lax.axis_size...  16.9 us
    ppermute x13, starting transfers between devices, exchange(): lax.ppermute(array, axis, [(i, i ^ distance) for i in range(lax.axis_size...  13.3 us
    pallas_call x2, Pallas kernels, build(): pl.pallas_call(functools.partial(build_kernel, owned, half, count), grid_...  8.96 us
    ppermute x2, waiting for transfers between devices, ahead_by(): lax.ppermute(array, axis, [(i, (i + distance) % count) for i in range(cou...  5.69 us
    unnamed x22, local copies, waits for them, and re-layouts  4.95 us
    pallas_call x1, Pallas kernels, fit(): pl.pallas_call(functools.partial(fit_kernel, owned, half), grid_spec=pltp...  4.16 us
    ppermute x2, starting transfers between devices, ahead_by(): lax.ppermute(array, axis, [(i, (i + distance) % count) for i in range(cou...  3.14 us
    ppermute x2, starting transfers between devices, pairs_from(): return lax.ppermute(array, axis, swaps)  2.45 us
  transfers between devices with their start and end apart: 17, of which 11 were waited for; matrix products, arithmetic and copies ran while one was open for 0% of the time, Pallas kernels for 7%

profile of v1, /device:TPU:0, one launch (start us, length us, event | category | flops | bytes accessed | tf_op | source)
XLA Modules:
  0.0 63.9 jit_solution(12365566759653952105)
XLA Ops:
  0.0 1.9 %copy-done = bf16[8,12,128,128]{3,2,1,0:T(8,128)(2,1)S(1)} copy-done((bf16[8,12,128,128]{3,2,1,0:T(8,128)(2,1)S(1)}, bf16[8,12,128,128]{3,2,1,0:T(8,128)(2,1)}, u32[]{:S(2)}) %copy-start) | copy-done | bytes 3145752
  1.9 1.0 %copy-done.2 = bf16[8,128,256]{2,1,0:T(8,128)(2,1)S(1)} copy-done((bf16[8,128,256]{2,1,0:T(8,128)(2,1)S(1)}, bf16[8,128,256]{2,1,0:T(8,128)(2,1)}, u32[]{:S(2)}) %copy-start.2) | copy-done | bytes 524312
  5.0 4.2 %fit.1 = (bf16[12,128,128]{2,1,0:T(8,128)(2,1)S(1)}, bf16[12,128,128]{2,1,0:T(8,128)(2,1)S(1)}) custom-call(s32[8,12]{1,0:T(8,128)S(1)} %copy-done.4, s32[32]{0:T(128)S(1)} %bitcast.2, s32[32]{0:T(128)S(1)} %bitcast.5, bf16[8,128,256]{2,1,0:T(8,128)(2,1)S(1)} %copy-done.2, bf16[8,12,128,128]{3,2,1,0:T(8,128)(2,1)S(1)} %copy-done), custom_call_target="tpu_custom_call" | custom-call | flops 805306368 | bytes 3670016 | tf_op jit(solution)/shard_map/fit/pallas_call | solution.py:44
  9.7 1.3 %collective-permute-done.1 = bf16[12,128,128]{2,1,0:T(8,128)(2,1)S(1)} collective-permute-done((bf16[12,128,128]{2,1,0:T(8,128)(2,1)S(1)}, bf16[12,128,128]{2,1,0:T(8,128)(2,1)S(1)}, u32[]{:S(2)}, u32[]{:S(2)}) %collective-permute-start.1) | collective-permute-done | bytes 393248 | tf_op jit(solution)/shard_map/ppermute | solution.py:187
  11.2 3.0 %collective-permute-start.2 = (bf16[3,128,128]{2,1,0:T(8,128)(2,1)S(1)}, bf16[3,128,128]{2,1,0:T(8,128)(2,1)S(1)}, u32[]{:S(2)}, u32[]{:S(2)}) collective-permute-start(bf16[3,128,128]{2,1,0:T(8,128)(2,1)S(1)} %get-tuple-element.9), channel_id=1, source_target_pairs={{0,4},{4,0},{8,12},{12,8},{1,5},{5,1},{9,13},{13,9},{2,6},{6,2},{1... | collective-permute-start | bytes 294920 | tf_op jit(solution)/shard_map/ppermute | solution.py:187
  14.2 2.6 %collective-permute-start.3 = (bf16[3,128,128]{2,1,0:T(8,128)(2,1)S(1)}, bf16[3,128,128]{2,1,0:T(8,128)(2,1)S(1)}, u32[]{:S(2)}, u32[]{:S(2)}) collective-permute-start(bf16[3,128,128]{2,1,0:T(8,128)(2,1)S(1)} %get-tuple-element.11), channel_id=1, source_target_pairs={{0,8},{4,12},{8,0},{12,4},{1,9},{5,13},{9,1},{13,5},{2,10},{6,14},... | collective-permute-start | bytes 294920 | tf_op jit(solution)/shard_map/ppermute | solution.py:187
  17.3 7.6 %collective-permute-done.3 = bf16[3,128,128]{2,1,0:T(8,128)(2,1)S(1)} collective-permute-done((bf16[3,128,128]{2,1,0:T(8,128)(2,1)S(1)}, bf16[3,128,128]{2,1,0:T(8,128)(2,1)S(1)}, u32[]{:S(2)}, u32[]{:S(2)}) %collective-permute-start.3) | collective-permute-done | bytes 98336 | tf_op jit(solution)/shard_map/ppermute | solution.py:187
  24.9 1.6 %collective-permute-start.5 = (bf16[3,128,128]{2,1,0:T(8,128)(2,1)S(1)}, bf16[3,128,128]{2,1,0:T(8,128)(2,1)S(1)}, u32[]{:S(2)}, u32[]{:S(2)}) collective-permute-start(bf16[3,128,128]{2,1,0:T(8,128)(2,1)S(1)} %add_convert_fusion.2), channel_id=1, source_target_pairs={{0,2},{2,0},{1,3},{3,1},{4,6},{6,4},{5,7},{7,5},{8,10},{10,8},{9,1... | collective-permute-start | bytes 294920 | tf_op jit(solution)/shard_map/ppermute | solution.py:192
  26.5 3.1 %collective-permute-done.5 = bf16[3,128,128]{2,1,0:T(8,128)(2,1)S(1)} collective-permute-done((bf16[3,128,128]{2,1,0:T(8,128)(2,1)S(1)}, bf16[3,128,128]{2,1,0:T(8,128)(2,1)S(1)}, u32[]{:S(2)}, u32[]{:S(2)}) %collective-permute-start.5) | collective-permute-done | bytes 98336 | tf_op jit(solution)/shard_map/ppermute | solution.py:192
  29.6 1.8 %collective-permute-start.6 = (bf16[6,128,128]{2,1,0:T(8,128)(2,1)S(1)}, bf16[6,128,128]{2,1,0:T(8,128)(2,1)S(1)}, u32[]{:S(2)}, u32[]{:S(2)}) collective-permute-start(bf16[6,128,128]{2,1,0:T(8,128)(2,1)S(1)} %pad_maximum_fusion.near_ref), channel_id=1, source_target_pairs={{0,4},{4,0},{8,12},{12,8},{1,5},{5,1},{9,13},{13,9},{2,6},{6,2},{1... | collective-permute-start | bytes 589832 | tf_op jit(solution)/shard_map/ppermute | solution.py:199
  32.1 1.1 %collective-permute-done.peer_cols = s32[3,4]{1,0:T(4,128)S(1)} collective-permute-done((s32[3,4]{1,0:T(4,128)S(1)}, s32[3,4]{1,0:T(4,128)S(1)}, u32[]{:S(2)}, u32[]{:S(2)}) %collective-permute-start) | collective-permute-done | bytes 80 | tf_op jit(solution)/shard_map/ppermute | solution.py:187
  33.3 2.0 %collective-permute-done.6.even_ref = bf16[6,128,128]{2,1,0:T(8,128)(2,1)S(1)} collective-permute-done((bf16[6,128,128]{2,1,0:T(8,128)(2,1)S(1)}, bf16[6,128,128]{2,1,0:T(8,128)(2,1)S(1)}, u32[]{:S(2)}, u32[]{:S(2)}) %collective-permute-start.6) | collective-permute-done | bytes 196640 | tf_op jit(solution)/shard_map/ppermute | solution.py:199
  35.3 1.2 %metric.1.rest_0_ = bf16[3,128,128]{2,1,0:T(8,128)(2,1)S(1)} custom-call(s32[3,4]{1,0:T(4,128)S(1)} %copy-done.10, s32[3,4]{1,0:T(4,128)S(1)} %collective-permute-done.peer_cols, bf16[6,128,128]{2,1,0:T(8,128)(2,1)S(1)} %pad_maximum_fusion.near_ref, bf16[6,128,128]{2,1,0:T(8,128)(2,1)S(1)} %collective-permute-done.6.even_ref, ...), custom_call_target="tpu_custom_call" | custom-call | flops 100663296 | bytes 1376256 | tf_op jit(solution)/shard_map/metric/pallas_call | solution.py:100
  36.6 4.0 %collective-permute-start.9 = (bf16[3,128,128]{2,1,0:T(8,128)(2,1)S(1)}, bf16[3,128,128]{2,1,0:T(8,128)(2,1)S(1)}, u32[]{:S(2)}, u32[]{:S(2)}) collective-permute-start(bf16[3,128,128]{2,1,0:T(8,128)(2,1)S(1)} %metric.1.rest_0_), channel_id=1, source_target_pairs={{0,4},{4,0},{8,12},{12,8},{1,5},{5,1},{9,13},{13,9},{2,6},{6,2},{1... | collective-permute-start | bytes 294920 | tf_op jit(solution)/shard_map/ppermute | solution.py:187
  40.5 1.2 %collective-permute-start.10 = (bf16[3,128,128]{2,1,0:T(8,128)(2,1)S(1)}, bf16[3,128,128]{2,1,0:T(8,128)(2,1)S(1)}, u32[]{:S(2)}, u32[]{:S(2)}) collective-permute-start(bf16[3,128,128]{2,1,0:T(8,128)(2,1)S(1)} %metric.1.rest_0_), channel_id=1, source_target_pairs={{0,8},{4,12},{8,0},{12,4},{1,9},{5,13},{9,1},{13,5},{2,10},{6,14},... | collective-permute-start | bytes 294920 | tf_op jit(solution)/shard_map/ppermute | solution.py:187
  41.7 1.4 %collective-permute-start.11 = (bf16[3,128,128]{2,1,0:T(8,128)(2,1)S(1)}, bf16[3,128,128]{2,1,0:T(8,128)(2,1)S(1)}, u32[]{:S(2)}, u32[]{:S(2)}) collective-permute-start(bf16[3,128,128]{2,1,0:T(8,128)(2,1)S(1)} %metric.1.rest_0_), channel_id=1, source_target_pairs={{0,12},{4,8},{8,4},{12,0},{1,13},{5,9},{9,5},{13,1},{2,14},{6,10},... | collective-permute-start | bytes 294920 | tf_op jit(solution)/shard_map/ppermute | solution.py:187
  43.1 2.1 %collective-permute-done.9.rest_1_ = bf16[3,128,128]{2,1,0:T(8,128)(2,1)S(1)} collective-permute-done((bf16[3,128,128]{2,1,0:T(8,128)(2,1)S(1)}, bf16[3,128,128]{2,1,0:T(8,128)(2,1)S(1)}, u32[]{:S(2)}, u32[]{:S(2)}) %collective-permute-start.9) | collective-permute-done | bytes 98336 | tf_op jit(solution)/shard_map/ppermute | solution.py:187
  45.2 3.3 %collective-permute-done.10.rest_2_ = bf16[3,128,128]{2,1,0:T(8,128)(2,1)S(1)} collective-permute-done((bf16[3,128,128]{2,1,0:T(8,128)(2,1)S(1)}, bf16[3,128,128]{2,1,0:T(8,128)(2,1)S(1)}, u32[]{:S(2)}, u32[]{:S(2)}) %collective-permute-start.10) | collective-permute-done | bytes 98336 | tf_op jit(solution)/shard_map/ppermute | solution.py:187
  49.0 0.8 %collective-permute-done.14.rest_6_ = bf16[3,128,128]{2,1,0:T(8,128)(2,1)S(1)} collective-permute-done((bf16[3,128,128]{2,1,0:T(8,128)(2,1)S(1)}, bf16[3,128,128]{2,1,0:T(8,128)(2,1)S(1)}, u32[]{:S(2)}, u32[]{:S(2)}) %collective-permute-start.14) | collective-permute-done | bytes 98336 | tf_op jit(solution)/shard_map/ppermute | solution.py:187
  50.0 4.5 %build_1.1 = bf16[8,64,256]{2,1,0:T(8,128)(2,1)S(1)} custom-call(s32[8,12]{1,0:T(8,128)S(1)} %copy-done.5, s32[32]{0:T(128)S(1)} %bitcast.3, s32[32]{0:T(128)S(1)} %bitcast.6, bf16[8,12,128,128]{3,2,1,0:T(8,128)(2,1)S(1)} %copy-done.1, bf16[3,128,128]{2,1,0:T(8,128)(2,1)S(1)} %metric.1.rest_0_, bf16[3,128,128]{2,1,0:T(8,128)(2,1)S(1)} %collective-permute-done.9.rest_1_, ...), custom_call_target="tpu_custom_call" | custom-call | flops 402653184 | bytes 1835008 | tf_op jit(solution)/shard_map/build_1/pallas_call | solution.py:157
  54.5 1.6 %collective-permute-start.16 = (bf16[8,64,256]{2,1,0:T(8,128)(2,1)S(1)}, bf16[8,64,256]{2,1,0:T(8,128)(2,1)S(1)}, u32[]{:S(2)}, u32[]{:S(2)}) collective-permute-start(bf16[8,64,256]{2,1,0:T(8,128)(2,1)S(1)} %build_1.1), channel_id=1, source_target_pairs={{0,2},{2,0},{1,3},{3,1},{4,6},{6,4},{5,7},{7,5},{8,10},{10,8},{9,1... | collective-permute-start | bytes 786440 | tf_op jit(solution)/shard_map/ppermute | solution.py:192
  56.0 4.5 %build_0.1 = bf16[8,64,256]{2,1,0:T(8,128)(2,1)S(1)} custom-call(s32[8,12]{1,0:T(8,128)S(1)} %copy-done.5, s32[32]{0:T(128)S(1)} %bitcast.4, s32[32]{0:T(128)S(1)} %bitcast.7, bf16[8,12,128,128]{3,2,1,0:T(8,128)(2,1)S(1)} %copy-done.1, bf16[3,128,128]{2,1,0:T(8,128)(2,1)S(1)} %metric.1.rest_0_, bf16[3,128,128]{2,1,0:T(8,128)(2,1)S(1)} %collective-permute-done.9.rest_1_, ...), custom_call_target="tpu_custom_call" | custom-call | flops 402653184 | bytes 1835008 | tf_op jit(solution)/shard_map/build_0/pallas_call | solution.py:157
  60.5 2.6 %collective-permute-done.16 = bf16[8,64,256]{2,1,0:T(8,128)(2,1)S(1)} collective-permute-done((bf16[8,64,256]{2,1,0:T(8,128)(2,1)S(1)}, bf16[8,64,256]{2,1,0:T(8,128)(2,1)S(1)}, u32[]{:S(2)}, u32[]{:S(2)}) %collective-permute-start.16) | collective-permute-done | bytes 262176 | tf_op jit(solution)/shard_map/ppermute | solution.py:192
  63.1 0.8 %add_convert_fusion.1 = bf16[8,64,256]{2,1,0:T(8,128)(2,1)} fusion(bf16[8,64,256]{2,1,0:T(8,128)(2,1)S(1)} %collective-permute-done.16, bf16[8,64,256]{2,1,0:T(8,128)(2,1)S(1)} %build_0.1), kind=kLoop, calls=%fused_computation.1 | loop fusion | flops 524288 | bytes 786432 | tf_op jit(solution)/shard_map/convert_element_type | solution.py:244
  (41 shorter events, 4.6 us)
Async XLA Ops:
  0.0 1.9 %copy-start = (bf16[8,12,128,128]{3,2,1,0:T(8,128)(2,1)S(1)}, bf16[8,12,128,128]{3,2,1,0:T(8,128)(2,1)}, u32[]{:S(2)}) copy-start(bf16[8,12,128,128]{3,2,1,0:T(8,128)(2,1)} %t_ref.5) | copy-start | bytes 9437188
  4.9 21.5 %copy-start.3 = (bf16[3,4,128,128]{3,2,1,0:T(8,128)(2,1)S(1)}, bf16[3,4,128,128]{3,2,1,0:T(8,128)(2,1)}, u32[]{:S(2)}) copy-start(bf16[3,4,128,128]{3,2,1,0:T(8,128)(2,1)} %m_ref.1) | copy-start | bytes 1179652
  4.9 27.1 %copy-start.10 = (s32[3,4]{1,0:T(4,128)S(1)}, s32[3,4]{1,0:T(4,128)}, u32[]{:S(2)}) copy-start(s32[3,4]{1,0:T(4,128)} %mine_cols.1) | copy-start | bytes 148
  4.9 45.0 %copy-start.1 = (bf16[8,12,128,128]{3,2,1,0:T(8,128)(2,1)S(1)}, bf16[8,12,128,128]{3,2,1,0:T(8,128)(2,1)}, u32[]{:S(2)}) copy-start(bf16[8,12,128,128]{3,2,1,0:T(8,128)(2,1)} %t_ref.5) | copy-start | bytes 9437188
  4.9 45.0 %copy-start.5 = (s32[8,12]{1,0:T(8,128)S(1)}, s32[8,12]{1,0:T(8,128)}, u32[]{:S(2)}) copy-start(s32[8,12]{1,0:T(8,128)} %tile_ref.5) | copy-start | bytes 1156
  4.9 45.0 %copy-start.7 = (s32[1,1,32,1]{2,3,1,0:T(1,128)S(1)}, s32[1,1,32,1]{2,3,1,0:T(1,128)}, u32[]{:S(2)}) copy-start(s32[1,1,32,1]{2,3,1,0:T(1,128)} %param.10) | copy-start | bytes 388
  5.0 45.0 %copy-start.9 = (s32[1,1,32]{2,1,0:T(1,128)S(1)}, s32[1,1,32]{2,1,0:T(1,128)}, u32[]{:S(2)}) copy-start(s32[1,1,32]{2,1,0:T(1,128)} %param.11) | copy-start | bytes 388
  9.1 1.9 %collective-permute-start.1 = (bf16[12,128,128]{2,1,0:T(8,128)(2,1)S(1)}, bf16[12,128,128]{2,1,0:T(8,128)(2,1)S(1)}, u32[]{:S(2)}, u32[]{:S(2)}) collective-permute-start(bf16[12,128,128]{2,1,0:T(8,128)(2,1)S(1)} %get-tuple-element.8), channel_id=1, source_target_pairs={{0,1},{1,0},{2,3},{3,2},{4,5},{5,4},{6,7},{7,6},{8,9},{9,8},{10,11... | collective-permute-start | bytes 1179656 | tf_op jit(solution)/shard_map/ppermute | solution.py:187
  11.2 6.1 %collective-permute-start.2 = (bf16[3,128,128]{2,1,0:T(8,128)(2,1)S(1)}, bf16[3,128,128]{2,1,0:T(8,128)(2,1)S(1)}, u32[]{:S(2)}, u32[]{:S(2)}) collective-permute-start(bf16[3,128,128]{2,1,0:T(8,128)(2,1)S(1)} %get-tuple-element.9), channel_id=1, source_target_pairs={{0,4},{4,0},{8,12},{12,8},{1,5},{5,1},{9,13},{13,9},{2,6},{6,2},{1... | collective-permute-start | bytes 294920 | tf_op jit(solution)/shard_map/ppermute | solution.py:187
  14.2 10.7 %collective-permute-start.3 = (bf16[3,128,128]{2,1,0:T(8,128)(2,1)S(1)}, bf16[3,128,128]{2,1,0:T(8,128)(2,1)S(1)}, u32[]{:S(2)}, u32[]{:S(2)}) collective-permute-start(bf16[3,128,128]{2,1,0:T(8,128)(2,1)S(1)} %get-tuple-element.11), channel_id=1, source_target_pairs={{0,8},{4,12},{8,0},{12,4},{1,9},{5,13},{9,1},{13,5},{2,10},{6,14},... | collective-permute-start | bytes 294920 | tf_op jit(solution)/shard_map/ppermute | solution.py:187
  16.8 8.0 %collective-permute-start.4 = (bf16[3,128,128]{2,1,0:T(8,128)(2,1)S(1)}, bf16[3,128,128]{2,1,0:T(8,128)(2,1)S(1)}, u32[]{:S(2)}, u32[]{:S(2)}) collective-permute-start(bf16[3,128,128]{2,1,0:T(8,128)(2,1)S(1)} %get-tuple-element.10), channel_id=1, source_target_pairs={{0,12},{4,8},{8,4},{12,0},{1,13},{5,9},{9,5},{13,1},{2,14},{6,10},... | collective-permute-start | bytes 294920 | tf_op jit(solution)/shard_map/ppermute | solution.py:187
  24.9 4.7 %collective-permute-start.5 = (bf16[3,128,128]{2,1,0:T(8,128)(2,1)S(1)}, bf16[3,128,128]{2,1,0:T(8,128)(2,1)S(1)}, u32[]{:S(2)}, u32[]{:S(2)}) collective-permute-start(bf16[3,128,128]{2,1,0:T(8,128)(2,1)S(1)} %add_convert_fusion.2), channel_id=1, source_target_pairs={{0,2},{2,0},{1,3},{3,1},{4,6},{6,4},{5,7},{7,5},{8,10},{10,8},{9,1... | collective-permute-start | bytes 294920 | tf_op jit(solution)/shard_map/ppermute | solution.py:192
  26.5 6.8 %collective-permute-start.8 = (bf16[3,4,128,128]{3,2,1,0:T(8,128)(2,1)S(1)}, bf16[3,4,128,128]{3,2,1,0:T(8,128)(2,1)S(1)}, u32[]{:S(2)}, u32[]{:S(2)}) collective-permute-start(bf16[3,4,128,128]{3,2,1,0:T(8,128)(2,1)S(1)} %copy-done.3), channel_id=1, source_target_pairs={{0,1},{1,0},{2,3},{3,2},{4,5},{5,4},{6,7},{7,6},{8,9},{9,8},{10,11... | collective-permute-start | bytes 1179656 | tf_op jit(solution)/shard_map/ppermute | solution.py:187
  29.6 5.7 %collective-permute-start.6 = (bf16[6,128,128]{2,1,0:T(8,128)(2,1)S(1)}, bf16[6,128,128]{2,1,0:T(8,128)(2,1)S(1)}, u32[]{:S(2)}, u32[]{:S(2)}) collective-permute-start(bf16[6,128,128]{2,1,0:T(8,128)(2,1)S(1)} %pad_maximum_fusion.near_ref), channel_id=1, source_target_pairs={{0,4},{4,0},{8,12},{12,8},{1,5},{5,1},{9,13},{13,9},{2,6},{6,2},{1... | collective-permute-start | bytes 589832 | tf_op jit(solution)/shard_map/ppermute | solution.py:199
  31.4 4.0 %collective-permute-start.7 = (bf16[6,128,128]{2,1,0:T(8,128)(2,1)S(1)}, bf16[6,128,128]{2,1,0:T(8,128)(2,1)S(1)}, u32[]{:S(2)}, u32[]{:S(2)}) collective-permute-start(bf16[6,128,128]{2,1,0:T(8,128)(2,1)S(1)} %pad_maximum_fusion.near_ref), channel_id=1, source_target_pairs={{4,8},{8,4},{5,9},{9,5},{6,10},{10,6},{7,11},{11,7},{20,24},{24,20... | collective-permute-start | bytes 589832 | tf_op jit(solution)/shard_map/ppermute | solution.py:199
  32.1 1.2 %collective-permute-start = (s32[3,4]{1,0:T(4,128)S(1)}, s32[3,4]{1,0:T(4,128)S(1)}, u32[]{:S(2)}, u32[]{:S(2)}) collective-permute-start(s32[3,4]{1,0:T(4,128)S(1)} %copy-done.10), channel_id=1, source_target_pairs={{0,1},{1,0},{2,3},{3,2},{4,5},{5,4},{6,7},{7,6},{8,9},{9,8},{10,11... | collective-permute-start | bytes 152 | tf_op jit(solution)/shard_map/ppermute | solution.py:187
  36.6 8.7 %collective-permute-start.9 = (bf16[3,128,128]{2,1,0:T(8,128)(2,1)S(1)}, bf16[3,128,128]{2,1,0:T(8,128)(2,1)S(1)}, u32[]{:S(2)}, u32[]{:S(2)}) collective-permute-start(bf16[3,128,128]{2,1,0:T(8,128)(2,1)S(1)} %metric.1.rest_0_), channel_id=1, source_target_pairs={{0,4},{4,0},{8,12},{12,8},{1,5},{5,1},{9,13},{13,9},{2,6},{6,2},{1... | collective-permute-start | bytes 294920 | tf_op jit(solution)/shard_map/ppermute | solution.py:187
  40.5 8.0 %collective-permute-start.10 = (bf16[3,128,128]{2,1,0:T(8,128)(2,1)S(1)}, bf16[3,128,128]{2,1,0:T(8,128)(2,1)S(1)}, u32[]{:S(2)}, u32[]{:S(2)}) collective-permute-start(bf16[3,128,128]{2,1,0:T(8,128)(2,1)S(1)} %metric.1.rest_0_), channel_id=1, source_target_pairs={{0,8},{4,12},{8,0},{12,4},{1,9},{5,13},{9,1},{13,5},{2,10},{6,14},... | collective-permute-start | bytes 294920 | tf_op jit(solution)/shard_map/ppermute | solution.py:187
  41.7 6.8 %collective-permute-start.11 = (bf16[3,128,128]{2,1,0:T(8,128)(2,1)S(1)}, bf16[3,128,128]{2,1,0:T(8,128)(2,1)S(1)}, u32[]{:S(2)}, u32[]{:S(2)}) collective-permute-start(bf16[3,128,128]{2,1,0:T(8,128)(2,1)S(1)} %metric.1.rest_0_), channel_id=1, source_target_pairs={{0,12},{4,8},{8,4},{12,0},{1,13},{5,9},{9,5},{13,1},{2,14},{6,10},... | collective-permute-start | bytes 294920 | tf_op jit(solution)/shard_map/ppermute | solution.py:187
  43.1 5.9 %collective-permute-start.12 = (bf16[3,128,128]{2,1,0:T(8,128)(2,1)S(1)}, bf16[3,128,128]{2,1,0:T(8,128)(2,1)S(1)}, u32[]{:S(2)}, u32[]{:S(2)}) collective-permute-start(bf16[3,128,128]{2,1,0:T(8,128)(2,1)S(1)} %metric.1.rest_0_), channel_id=1, source_target_pairs={{0,1},{1,0},{2,3},{3,2},{4,5},{5,4},{6,7},{7,6},{8,9},{9,8},{10,11... | collective-permute-start | bytes 294920 | tf_op jit(solution)/shard_map/ppermute | solution.py:187
  45.2 3.8 %collective-permute-start.13 = (bf16[3,128,128]{2,1,0:T(8,128)(2,1)S(1)}, bf16[3,128,128]{2,1,0:T(8,128)(2,1)S(1)}, u32[]{:S(2)}, u32[]{:S(2)}) collective-permute-start(bf16[3,128,128]{2,1,0:T(8,128)(2,1)S(1)} %collective-permute-done.9.rest_1_), channel_id=1, source_target_pairs={{0,1},{1,0},{2,3},{3,2},{4,5},{5,4},{6,7},{7,6},{8,9},{9,8},{10,11... | collective-permute-start | bytes 294920 | tf_op jit(solution)/shard_map/ppermute | solution.py:187
  48.5 1.3 %collective-permute-start.14 = (bf16[3,128,128]{2,1,0:T(8,128)(2,1)S(1)}, bf16[3,128,128]{2,1,0:T(8,128)(2,1)S(1)}, u32[]{:S(2)}, u32[]{:S(2)}) collective-permute-start(bf16[3,128,128]{2,1,0:T(8,128)(2,1)S(1)} %collective-permute-done.10.rest_2_), channel_id=1, source_target_pairs={{0,1},{1,0},{2,3},{3,2},{4,5},{5,4},{6,7},{7,6},{8,9},{9,8},{10,11... | collective-permute-start | bytes 294920 | tf_op jit(solution)/shard_map/ppermute | solution.py:187
  48.5 1.5 %collective-permute-start.15 = (bf16[3,128,128]{2,1,0:T(8,128)(2,1)S(1)}, bf16[3,128,128]{2,1,0:T(8,128)(2,1)S(1)}, u32[]{:S(2)}, u32[]{:S(2)}) collective-permute-start(bf16[3,128,128]{2,1,0:T(8,128)(2,1)S(1)} %collective-permute-done.11.rest_3_), channel_id=1, source_target_pairs={{0,1},{1,0},{2,3},{3,2},{4,5},{5,4},{6,7},{7,6},{8,9},{9,8},{10,11... | collective-permute-start | bytes 294920 | tf_op jit(solution)/shard_map/ppermute | solution.py:187
  54.5 8.6 %collective-permute-start.16 = (bf16[8,64,256]{2,1,0:T(8,128)(2,1)S(1)}, bf16[8,64,256]{2,1,0:T(8,128)(2,1)S(1)}, u32[]{:S(2)}, u32[]{:S(2)}) collective-permute-start(bf16[8,64,256]{2,1,0:T(8,128)(2,1)S(1)} %build_1.1), channel_id=1, source_target_pairs={{0,2},{2,0},{1,3},{3,1},{4,6},{6,4},{5,7},{7,5},{8,10},{10,8},{9,1... | collective-permute-start | bytes 786440 | tf_op jit(solution)/shard_map/ppermute | solution.py:192
  (4 other events, 3.0 us)

commit v2 on v1

v2 whole, which is shorter than its diff:
```python
import functools

import jax
import jax.numpy as jnp
from jax import lax
from jax.experimental import pallas as pl
from jax.experimental.pallas import tpu as pltpu
from jax.sharding import PartitionSpec as P

BF16 = jnp.bfloat16
F32 = jnp.float32
NT = (((1,), (1,)), ((), ()))
VMEM_LIMIT = 32 * 1024 * 1024
FIT_VMEM_LIMIT = 56 * 1024 * 1024
VMEM = pl.BlockSpec(memory_space=pltpu.VMEM)
SMEM = pl.BlockSpec(memory_space=pltpu.SMEM)


def fit_kernel(
    owned, half, tile_hbm, domain_hbm, number_hbm, d_hbm, t_hbm, keep_ref, send_ref, slot_ref,
    acc, tile_ref, domain_ref, number_ref, d_ref, t_ref, small_sem, d_sem, t_sem,
):
    me = lax.axis_index("space")
    mine = lax.axis_index("sub")
    blocks, listed = t_ref.shape[:2]
    small = [
        pltpu.make_async_copy(tile_hbm, tile_ref, small_sem.at[0]),
        pltpu.make_async_copy(domain_hbm, domain_ref, small_sem.at[1]),
        pltpu.make_async_copy(number_hbm, number_ref, small_sem.at[2]),
    ]
    d_copies = [pltpu.make_async_copy(d_hbm.at[p], d_ref.at[p], d_sem.at[p]) for p in range(blocks)]
    t_copies = [pltpu.make_async_copy(t_hbm.at[p], t_ref.at[p], t_sem.at[p]) for p in range(blocks)]
    for copy in small:
        copy.start()
    for p in range(blocks):
        d_copies[p].start()
        t_copies[p].start()
    acc[...] = jnp.zeros_like(acc)
    for copy in small:
        copy.wait()
    for p in range(blocks):
        d_copies[p].wait()
        rows = jnp.transpose(d_ref[p])
        t_copies[p].wait()
        for k in range(listed):
            touched = tile_ref[p, k]
            slot = jnp.bitwise_xor(domain_ref[touched], me) * owned + number_ref[touched]
            slot_ref[p, k] = slot
            acc[slot] += jnp.dot(rows, t_ref[p, k], preferred_element_type=F32)
    keep_ref[...] = acc[:, pl.ds(pl.multiple_of(mine * half, half), half), :].astype(BF16)
    send_ref[...] = acc[:, pl.ds(pl.multiple_of((1 - mine) * half, half), half), :].astype(BF16)


def fit(block_tile, domain, number, densities, three_centre, domains, owned):
    blocks, listed, width, _ = three_centre.shape
    columns = densities.shape[2]
    half = columns // 2
    slots = domains * owned
    out = jax.ShapeDtypeStruct((slots, half, width), BF16)
    return pl.pallas_call(
        functools.partial(fit_kernel, owned, half),
        in_specs=[pl.BlockSpec(memory_space=pltpu.HBM)] * 5,
        out_specs=[VMEM, VMEM, SMEM],
        scratch_shapes=[
            pltpu.VMEM((slots, columns, width), F32),
            pltpu.SMEM(block_tile.shape, jnp.int32),
            pltpu.SMEM(domain.shape, jnp.int32),
            pltpu.SMEM(number.shape, jnp.int32),
            pltpu.VMEM(densities.shape, BF16),
            pltpu.VMEM(three_centre.shape, BF16),
            pltpu.SemaphoreType.DMA((3,)),
            pltpu.SemaphoreType.DMA((blocks,)),
            pltpu.SemaphoreType.DMA((blocks,)),
        ],
        out_shape=[out, out, jax.ShapeDtypeStruct(block_tile.shape, jnp.int32)],
        compiler_params=pltpu.CompilerParams(vmem_limit_bytes=FIT_VMEM_LIMIT),
        cost_estimate=pl.CostEstimate(
            flops=2 * blocks * listed * width * width * columns,
            bytes_accessed=2 * (three_centre.size + densities.size),
            transcendentals=0,
        ),
        name="fit",
    )(block_tile, domain, number, densities, three_centre)


def metric_kernel(owned, count, mine_cols, peer_cols, near_ref, even_ref, odd_ref, m_ref, pm_ref, out_ref, window):
    me = lax.axis_index("space")
    aux = lax.axis_index("aux")
    own = owned * count
    window[:own] = near_ref[...]
    window[own : 2 * own] = even_ref[...]
    window[2 * own :] = odd_ref[...]

    def place(column):
        zone = column // own
        rest = column % own
        side = jnp.where((zone == 2) == (me % 2 == 0), 1, 2)
        block = jnp.where(zone == 1, 0, side)
        turned = (rest // owned + count - aux) % count
        return block * own + turned * owned + rest % owned

    for q in range(m_ref.shape[0]):
        picked, blocks = [], []
        for cols, mat in ((mine_cols, m_ref), (peer_cols, pm_ref)):
            for m in range(mat.shape[1]):
                picked.append(window[place(cols[q, m])])
                blocks.append(mat[q, m])
        out_ref[q] = lax.dot_general(
            jnp.concatenate(picked, axis=1),
            jnp.concatenate(blocks, axis=1),
            NT,
            preferred_element_type=F32,
        ).astype(BF16)


def metric(mine_cols, peer_cols, near, even, odd, m, pm, count):
    owned, listed, width, _ = m.shape
    half = near.shape[1]
    return pl.pallas_call(
        functools.partial(metric_kernel, owned, count),
        in_specs=[SMEM] * 2 + [VMEM] * 5,
        out_specs=VMEM,
        out_shape=jax.ShapeDtypeStruct((owned, half, width), BF16),
        scratch_shapes=[pltpu.VMEM((3 * owned * count, half, width), BF16)],
        compiler_params=pltpu.CompilerParams(vmem_limit_bytes=VMEM_LIMIT),
        cost_estimate=pl.CostEstimate(
            flops=4 * owned * listed * width * width * half,
            bytes_accessed=4 * m.size + 6 * near.size,
            transcendentals=0,
        ),
        name="metric",
    )(mine_cols, peer_cols, near, even, odd, m, pm)


def build_kernel(parts, slot_ref, t_ref, *rest):
    piece_refs, (out_ref, table) = rest[:-2], rest[-2:]
    aux = lax.axis_index("aux")
    blocks, listed, width, _ = t_ref.shape
    owned = piece_refs[0].shape[0]
    rows = width // parts
    for k, piece in enumerate(piece_refs):
        table[k * owned : (k + 1) * owned] = piece[...]
    for p in range(blocks):
        left = [t_ref[p, k] for k in range(listed)]
        right = [table[slot_ref[p, k]] for k in range(listed)]
        total = lax.dot_general(
            jnp.concatenate(left, axis=1), jnp.concatenate(right, axis=1), NT, preferred_element_type=F32
        ).astype(BF16)
        for part in range(parts):
            out_ref[lax.rem(part + parts - aux, parts), p] = total[part * rows : (part + 1) * rows]


def build(slots, three_centre, pieces, parts, name):
    blocks, listed, width, _ = three_centre.shape
    owned, half, _ = pieces[0].shape
    return pl.pallas_call(
        functools.partial(build_kernel, parts),
        in_specs=[SMEM] + [VMEM] * (1 + len(pieces)),
        out_specs=VMEM,
        out_shape=jax.ShapeDtypeStruct((parts, blocks, width // parts, half), BF16),
        scratch_shapes=[pltpu.VMEM((len(pieces) * owned, half, width), BF16)],
        compiler_params=pltpu.CompilerParams(vmem_limit_bytes=VMEM_LIMIT),
        cost_estimate=pl.CostEstimate(
            flops=2 * blocks * listed * width * width * half,
            bytes_accessed=2 * (three_centre.size + blocks * width * half),
            transcendentals=0,
        ),
        name=name,
    )(slots, three_centre, *pieces)


def exchange(array, axis, distance):
    return lax.ppermute(array, axis, [(i, i ^ distance) for i in range(lax.axis_size(axis))])


def ahead_by(array, axis, distance):
    count = lax.axis_size(axis)
    return lax.ppermute(array, axis, [(i, (i + distance) % count) for i in range(count)])


def pairs_from(array, axis, first):
    swaps = []
    for low in range(first, lax.axis_size(axis) - 1, 2):
        swaps += [(low, low + 1), (low + 1, low)]
    return lax.ppermute(array, axis, swaps)


def shards(
    densities, three_centre, block_tile, owner_domain, owner_tile, metric_inverse, metric_columns
):
    domains = lax.axis_size("space")
    aux_count = lax.axis_size("aux")
    touched = owner_tile.shape[-1]
    owned, _, width, _ = metric_inverse.shape
    half = densities.shape[2] // 2
    domain = owner_domain.reshape(touched)
    number = owner_tile.reshape(touched)

    keep, send, slots = fit(block_tile, domain, number, densities, three_centre, domains, owned)
    got = exchange(send, "sub", 1)
    chip = (keep.astype(F32) + got.astype(F32)).astype(BF16).reshape(domains, owned, half, width)
    chip, own_metric, own_columns = lax.optimization_barrier((chip, metric_inverse, metric_columns))
    arrived = [exchange(chip[k], "space", k) for k in range(1, domains)]
    peer_metric = exchange(own_metric, "sub", 1)
    peer_columns = exchange(own_columns, "sub", 1)
    arrived, peer_metric, peer_columns = lax.optimization_barrier((arrived, peer_metric, peer_columns))
    total = chip[0].astype(F32)
    for piece in arrived:
        total = total + piece.astype(F32)
    fitted = total.astype(BF16)

    near = jnp.concatenate(
        [fitted] + [ahead_by(fitted, "aux", aux_count - k) for k in range(1, aux_count)]
    )
    even = pairs_from(near, "space", 0)
    odd = pairs_from(near, "space", 1)
    coefficients = metric(
        metric_columns, peer_columns, near, even, odd, metric_inverse, peer_metric, aux_count
    )

    pieces = [coefficients] + [exchange(coefficients, "space", k) for k in range(1, domains)]
    other = [exchange(piece, "sub", 1) for piece in pieces]

    sums = []
    for name, tiles in (("build_own", pieces), ("build_other", other)):
        parts = build(slots, three_centre, tiles, aux_count, name)
        terms = [parts[0]] + [ahead_by(parts[k], "aux", k) for k in range(1, aux_count)]
        sums.append(sum(term.astype(F32) for term in terms).astype(BF16))
    first = lax.axis_index("sub") == 0
    low, high = jnp.where(first, sums[0], sums[1]), jnp.where(first, sums[1], sums[0])
    return jnp.concatenate([low, high], axis=2)


def solution(mesh):
    placed = (
        P(("frag", "space", "sub"), None, None),
        P(("frag", "space", "sub"), "aux", None, None),
        P(("frag", "space", "sub"), "aux"),
        P(("frag", "space", "sub"), "aux", None, None),
        P(("frag", "space", "sub"), "aux", None),
        P(("frag", "space", "aux"), "sub", None, None),
        P(("frag", "space", "aux"), "sub"),
    )
    return jax.shard_map(
        shards,
        mesh=mesh,
        in_specs=placed,
        out_specs=P(("frag", "space", "sub"), "aux", None),
        check_vma=False,
    )
```

time: 64.1 us -> 57.9 us (0.903)
  local copies, waits for them, and re-layouts: 4.97 us -> 0.06 us
  Pallas kernels: 14.3 us -> 10.1 us
  waiting for transfers between devices: 24.6 us -> 25.8 us
  other arithmetic: 0.95 us -> 2 us
  starting transfers between devices: 18.9 us -> 19.6 us
    unnamed x22 -> x8, local copies, waits for them, and re-layouts: 4.95 us -> 0.02 us
    pallas_call x3, Pallas kernels: 13.1 us -> 8.9 us  [the longest x1 5.69 us: fit(): pl.pallas_call(functools.partial(fit_kernel, owned, half), in_specs=[pl.B...]
    ppermute x2 -> x3, waiting for transfers between devices: 5.69 us -> 7.76 us  [ahead_by(): lax.ppermute(array, axis, [(i, (i + distance) % count) for i in range(cou...]
    ppermute x13, waiting for transfers between devices: 16.9 us -> 14.9 us  [exchange(): lax.ppermute(array, axis, [(i, i ^ distance) for i in range(lax.axis_size...]
    ppermute x2, waiting for transfers between devices: 2.04 us -> 3.16 us  [pairs_from(): return lax.ppermute(array, axis, swaps)]
    convert_element_type x1, other arithmetic: 0.11 us -> 1.1 us  [shards(): (keep.astype(F32) + got.astype(F32)).astype(BF16)]
    convert_element_type x1 -> x0, other arithmetic: 0.77 us -> none  [shards(): return result.astype(BF16)]
    concatenate x0 -> x1, other arithmetic: none -> 0.74 us  [shards(): return jnp.concatenate([low, high], axis=2)]
  transfers between devices with their start and end apart: 17 -> 18, of which waited for: 11 -> 9; matrix products, arithmetic and copies ran while one was open for 0% -> 0% of each run, Pallas kernels for 7% -> 6%
where the time goes in v2:
time: 57.9 us; the launch traced here: 57.8 us
  waiting for transfers between devices  25.8 us (45%)
  starting transfers between devices  19.6 us (34%)
  Pallas kernels  10.1 us (17%)
  other arithmetic  2 us (3%)
    ppermute x13, waiting for transfers between devices, exchange(): lax.ppermute(array, axis, [(i, i ^ distance) for i in range(lax.axis_size...  14.9 us
    ppermute x13, starting transfers between devices, exchange(): lax.ppermute(array, axis, [(i, i ^ distance) for i in range(lax.axis_size...  13.4 us
    ppermute x3, waiting for transfers between devices, ahead_by(): lax.ppermute(array, axis, [(i, (i + distance) % count) for i in range(cou...  7.76 us
    pallas_call x1, Pallas kernels, fit(): pl.pallas_call(functools.partial(fit_kernel, owned, half), in_specs=[pl.B...  5.69 us
    ppermute x3, starting transfers between devices, ahead_by(): lax.ppermute(array, axis, [(i, (i + distance) % count) for i in range(cou...  3.68 us
    pallas_call x2, Pallas kernels, build(): pl.pallas_call(functools.partial(build_kernel, parts), in_specs=[SMEM] +...  3.21 us
    ppermute x2, waiting for transfers between devices, pairs_from(): return lax.ppermute(array, axis, swaps)  3.16 us
    ppermute x2, starting transfers between devices, pairs_from(): return lax.ppermute(array, axis, swaps)  2.57 us
  transfers between devices with their start and end apart: 18, of which 9 were waited for; matrix products, arithmetic and copies ran while one was open for 0% of the time, Pallas kernels for 6%

profile of v2, /device:TPU:0, one launch (start us, length us, event | category | flops | bytes accessed | tf_op | source)
XLA Modules:
  0.0 57.8 jit_solution(14173791389534359842)
XLA Ops:
  0.0 5.7 %fit.1 = (bf16[12,128,128]{2,1,0:T(8,128)(2,1)}, bf16[12,128,128]{2,1,0:T(8,128)(2,1)}, s32[8,12]{1,0:T(8,128)}) custom-call(s32[8,12]{1,0:T(8,128)} %tile_hbm.1, s32[32]{0:T(128)} %bitcast.36, s32[32]{0:T(128)} %bitcast.37, bf16[8,128,256]{2,1,0:T(8,128)(2,1)} %d_hbm.1, bf16[8,12,128,128]{3,2,1,0:T(8,128)(2,1)} %t_ref.3), custom_call_target="tpu_custom_call" | custom-call | flops 805306368 | bytes 3670016 | tf_op jit(solution)/shard_map/fit/pallas_call | solution.py:60
  6.2 1.6 %collective-permute-done = bf16[12,128,128]{2,1,0:T(8,128)(2,1)S(1)} collective-permute-done((bf16[12,128,128]{2,1,0:T(8,128)(2,1)}, bf16[12,128,128]{2,1,0:T(8,128)(2,1)S(1)}, u32[]{:S(2)}, u32[]{:S(2)}) %collective-permute-start) | collective-permute-done | bytes 393248 | tf_op jit(solution)/shard_map/ppermute | solution.py:173
  7.8 1.1 %add_convert_fusion = bf16[12,128,128]{2,1,0:T(8,128)(2,1)S(1)} fusion(bf16[12,128,128]{2,1,0:T(8,128)(2,1)S(1)} %collective-permute-done, bf16[12,128,128]{2,1,0:T(8,128)(2,1)} %get-tuple-element.17), kind=kLoop, calls=%fused_computation | loop fusion | flops 786432 | bytes 1179648 | tf_op jit(solution)/shard_map/convert_element_type | solution.py:201
  9.4 2.8 %collective-permute-start.1 = (bf16[3,128,128]{2,1,0:T(8,128)(2,1)S(1)}, bf16[3,128,128]{2,1,0:T(8,128)(2,1)S(1)}, u32[]{:S(2)}, u32[]{:S(2)}) collective-permute-start(bf16[3,128,128]{2,1,0:T(8,128)(2,1)S(1)} %get-tuple-element.31), channel_id=1, source_target_pairs={{0,4},{4,0},{8,12},{12,8},{1,5},{5,1},{9,13},{13,9},{2,6},{6,2},{1... | collective-permute-start | bytes 294920 | tf_op jit(solution)/shard_map/ppermute | solution.py:173
  12.2 2.6 %collective-permute-start.2 = (bf16[3,128,128]{2,1,0:T(8,128)(2,1)S(1)}, bf16[3,128,128]{2,1,0:T(8,128)(2,1)S(1)}, u32[]{:S(2)}, u32[]{:S(2)}) collective-permute-start(bf16[3,128,128]{2,1,0:T(8,128)(2,1)S(1)} %get-tuple-element.30), channel_id=1, source_target_pairs={{0,8},{4,12},{8,0},{12,4},{1,9},{5,13},{9,1},{13,5},{2,10},{6,14},... | collective-permute-start | bytes 294920 | tf_op jit(solution)/shard_map/ppermute | solution.py:173
  14.8 1.2 %collective-permute-done.5.peer_cols = s32[3,4]{1,0:T(4,128)S(1)} collective-permute-done((s32[3,4]{1,0:T(4,128)S(1)}, s32[3,4]{1,0:T(4,128)S(1)}, u32[]{:S(2)}, u32[]{:S(2)}) %collective-permute-start.5) | collective-permute-done | bytes 80 | tf_op jit(solution)/shard_map/ppermute | solution.py:173
  15.9 7.0 %collective-permute-done.2 = bf16[3,128,128]{2,1,0:T(8,128)(2,1)S(1)} collective-permute-done((bf16[3,128,128]{2,1,0:T(8,128)(2,1)S(1)}, bf16[3,128,128]{2,1,0:T(8,128)(2,1)S(1)}, u32[]{:S(2)}, u32[]{:S(2)}) %collective-permute-start.2) | collective-permute-done | bytes 98336 | tf_op jit(solution)/shard_map/ppermute | solution.py:173
  23.0 1.5 %collective-permute-start.6 = (bf16[3,128,128]{2,1,0:T(8,128)(2,1)S(1)}, bf16[3,128,128]{2,1,0:T(8,128)(2,1)S(1)}, u32[]{:S(2)}, u32[]{:S(2)}) collective-permute-start(bf16[3,128,128]{2,1,0:T(8,128)(2,1)S(1)} %fusion.4), channel_id=1, source_target_pairs={{0,2},{2,0},{1,3},{3,1},{4,6},{6,4},{5,7},{7,5},{8,10},{10,8},{9,1... | collective-permute-start | bytes 294920 | tf_op jit(solution)/shard_map/ppermute | solution.py:178
  24.5 3.2 %collective-permute-done.6 = bf16[3,128,128]{2,1,0:T(8,128)(2,1)S(1)} collective-permute-done((bf16[3,128,128]{2,1,0:T(8,128)(2,1)S(1)}, bf16[3,128,128]{2,1,0:T(8,128)(2,1)S(1)}, u32[]{:S(2)}, u32[]{:S(2)}) %collective-permute-start.6) | collective-permute-done | bytes 98336 | tf_op jit(solution)/shard_map/ppermute | solution.py:178
  27.7 1.9 %collective-permute-start.7 = (bf16[6,128,128]{2,1,0:T(8,128)(2,1)S(1)}, bf16[6,128,128]{2,1,0:T(8,128)(2,1)S(1)}, u32[]{:S(2)}, u32[]{:S(2)}) collective-permute-start(bf16[6,128,128]{2,1,0:T(8,128)(2,1)S(1)} %pad_maximum_fusion.1.near_ref), channel_id=1, source_target_pairs={{0,4},{4,0},{8,12},{12,8},{1,5},{5,1},{9,13},{13,9},{2,6},{6,2},{1... | collective-permute-start | bytes 589832 | tf_op jit(solution)/shard_map/ppermute | solution.py:185
  29.6 0.7 %collective-permute-start.8 = (bf16[6,128,128]{2,1,0:T(8,128)(2,1)S(1)}, bf16[6,128,128]{2,1,0:T(8,128)(2,1)S(1)}, u32[]{:S(2)}, u32[]{:S(2)}) collective-permute-start(bf16[6,128,128]{2,1,0:T(8,128)(2,1)S(1)} %pad_maximum_fusion.1.near_ref), channel_id=1, source_target_pairs={{4,8},{8,4},{5,9},{9,5},{6,10},{10,6},{7,11},{11,7},{20,24},{24,20... | collective-permute-start | bytes 589832 | tf_op jit(solution)/shard_map/ppermute | solution.py:185
  30.3 3.2 %collective-permute-done.7.even_ref = bf16[6,128,128]{2,1,0:T(8,128)(2,1)S(1)} collective-permute-done((bf16[6,128,128]{2,1,0:T(8,128)(2,1)S(1)}, bf16[6,128,128]{2,1,0:T(8,128)(2,1)S(1)}, u32[]{:S(2)}, u32[]{:S(2)}) %collective-permute-start.7) | collective-permute-done | bytes 196640 | tf_op jit(solution)/shard_map/ppermute | solution.py:185
  33.4 1.2 %metric.1.rest_0_ = bf16[3,128,128]{2,1,0:T(8,128)(2,1)S(1)} custom-call(s32[3,4]{1,0:T(4,128)S(1)} %copy-done.3, s32[3,4]{1,0:T(4,128)S(1)} %collective-permute-done.5.peer_cols, bf16[6,128,128]{2,1,0:T(8,128)(2,1)S(1)} %pad_maximum_fusion.1.near_ref, bf16[6,128,128]{2,1,0:T(8,128)(2,1)S(1)} %collective-permute-done.7.even_ref, ...), custom_call_target="tpu_custom_call" | custom-call | flops 100663296 | bytes 1376256 | tf_op jit(solution)/shard_map/metric/pallas_call | solution.py:119
  34.6 4.0 %collective-permute-start.9 = (bf16[3,128,128]{2,1,0:T(8,128)(2,1)S(1)}, bf16[3,128,128]{2,1,0:T(8,128)(2,1)S(1)}, u32[]{:S(2)}, u32[]{:S(2)}) collective-permute-start(bf16[3,128,128]{2,1,0:T(8,128)(2,1)S(1)} %metric.1.rest_0_), channel_id=1, source_target_pairs={{0,4},{4,0},{8,12},{12,8},{1,5},{5,1},{9,13},{13,9},{2,6},{6,2},{1... | collective-permute-start | bytes 294920 | tf_op jit(solution)/shard_map/ppermute | solution.py:173
  38.6 1.2 %collective-permute-start.10 = (bf16[3,128,128]{2,1,0:T(8,128)(2,1)S(1)}, bf16[3,128,128]{2,1,0:T(8,128)(2,1)S(1)}, u32[]{:S(2)}, u32[]{:S(2)}) collective-permute-start(bf16[3,128,128]{2,1,0:T(8,128)(2,1)S(1)} %metric.1.rest_0_), channel_id=1, source_target_pairs={{0,8},{4,12},{8,0},{12,4},{1,9},{5,13},{9,1},{13,5},{2,10},{6,14},... | collective-permute-start | bytes 294920 | tf_op jit(solution)/shard_map/ppermute | solution.py:173
  39.8 1.4 %collective-permute-start.11 = (bf16[3,128,128]{2,1,0:T(8,128)(2,1)S(1)}, bf16[3,128,128]{2,1,0:T(8,128)(2,1)S(1)}, u32[]{:S(2)}, u32[]{:S(2)}) collective-permute-start(bf16[3,128,128]{2,1,0:T(8,128)(2,1)S(1)} %metric.1.rest_0_), channel_id=1, source_target_pairs={{0,12},{4,8},{8,4},{12,0},{1,13},{5,9},{9,5},{13,1},{2,14},{6,10},... | collective-permute-start | bytes 294920 | tf_op jit(solution)/shard_map/ppermute | solution.py:173
  41.2 1.2 %collective-permute-done.9.rest_1_ = bf16[3,128,128]{2,1,0:T(8,128)(2,1)S(1)} collective-permute-done((bf16[3,128,128]{2,1,0:T(8,128)(2,1)S(1)}, bf16[3,128,128]{2,1,0:T(8,128)(2,1)S(1)}, u32[]{:S(2)}, u32[]{:S(2)}) %collective-permute-start.9) | collective-permute-done | bytes 98336 | tf_op jit(solution)/shard_map/ppermute | solution.py:173
  42.4 4.0 %collective-permute-done.10.rest_2_ = bf16[3,128,128]{2,1,0:T(8,128)(2,1)S(1)} collective-permute-done((bf16[3,128,128]{2,1,0:T(8,128)(2,1)S(1)}, bf16[3,128,128]{2,1,0:T(8,128)(2,1)S(1)}, u32[]{:S(2)}, u32[]{:S(2)}) %collective-permute-start.10) | collective-permute-done | bytes 98336 | tf_op jit(solution)/shard_map/ppermute | solution.py:173
  46.9 1.6 %build_own.1 = bf16[2,8,64,128]{3,2,1,0:T(8,128)(2,1)S(1)} custom-call(s32[8,12]{1,0:T(8,128)S(1)} %copy-done.2, bf16[8,12,128,128]{3,2,1,0:T(8,128)(2,1)S(1)} %copy-done, bf16[3,128,128]{2,1,0:T(8,128)(2,1)S(1)} %metric.1.rest_0_, bf16[3,128,128]{2,1,0:T(8,128)(2,1)S(1)} %collective-permute-done.9.rest_1_, ...), custom_call_target="tpu_custom_call" | custom-call | flops 402653184 | bytes 3407872 | tf_op jit(solution)/shard_map/build_own/pallas_call | solution.py:156
  48.5 1.6 %collective-permute-start.12 = (bf16[8,64,128]{2,1,0:T(8,128)(2,1)S(1)}, bf16[8,64,128]{2,1,0:T(8,128)(2,1)S(1)}, u32[]{:S(2)}, u32[]{:S(2)}) collective-permute-start(bf16[8,64,128]{2,1,0:T(8,128)(2,1)S(1)} %slice_bitcast_fusion.2), channel_id=1, source_target_pairs={{0,2},{2,0},{1,3},{3,1},{4,6},{6,4},{5,7},{7,5},{8,10},{10,8},{9,1... | collective-permute-start | bytes 393224 | tf_op jit(solution)/shard_map/ppermute | solution.py:178
  50.1 1.6 %build_other.1 = bf16[2,8,64,128]{3,2,1,0:T(8,128)(2,1)S(1)} custom-call(s32[8,12]{1,0:T(8,128)S(1)} %copy-done.2, bf16[8,12,128,128]{3,2,1,0:T(8,128)(2,1)S(1)} %copy-done, bf16[3,128,128]{2,1,0:T(8,128)(2,1)S(1)} %collective-permute-done.13.rest_0_, bf16[3,128,128]{2,1,0:T(8,128)(2,1)S(1)} %collective-permute-done.14.rest_1_, ...), custom_call_target="tpu_custom_call" | custom-call | flops 402653184 | bytes 3407872 | tf_op jit(solution)/shard_map/build_other/pallas_call | solution.py:156
  52.3 1.7 %collective-permute-done.12 = bf16[8,64,128]{2,1,0:T(8,128)(2,1)S(1)} collective-permute-done((bf16[8,64,128]{2,1,0:T(8,128)(2,1)S(1)}, bf16[8,64,128]{2,1,0:T(8,128)(2,1)S(1)}, u32[]{:S(2)}, u32[]{:S(2)}) %collective-permute-start.12) | collective-permute-done | bytes 131104 | tf_op jit(solution)/shard_map/ppermute | solution.py:178
  54.0 2.9 %collective-permute-done.17 = bf16[8,64,128]{2,1,0:T(8,128)(2,1)S(1)} collective-permute-done((bf16[8,64,128]{2,1,0:T(8,128)(2,1)S(1)}, bf16[8,64,128]{2,1,0:T(8,128)(2,1)S(1)}, u32[]{:S(2)}, u32[]{:S(2)}) %collective-permute-start.17) | collective-permute-done | bytes 131104 | tf_op jit(solution)/shard_map/ppermute | solution.py:178
  57.0 0.7 %pad_maximum_fusion = bf16[8,64,256]{2,1,0:T(8,128)(2,1)} fusion(bf16[8,64,128]{2,1,0:T(8,128)(2,1)S(1)} %get-tuple-element.28, bf16[8,64,128]{2,1,0:T(8,128)(2,1)S(1)} %get-tuple-element.27), kind=kLoop, calls=%fused_computation.1 | loop fusion | flops 524288 | bytes 524288 | tf_op jit(solution)/shard_map/concatenate | solution.py:231
  (32 shorter events, 2.3 us)
Async XLA Ops:
  0.0 8.9 %copy-start.1 = (bf16[3,4,128,128]{3,2,1,0:T(8,128)(2,1)S(1)}, bf16[3,4,128,128]{3,2,1,0:T(8,128)(2,1)}, u32[]{:S(2)}) copy-start(bf16[3,4,128,128]{3,2,1,0:T(8,128)(2,1)} %m_ref.1) | copy-start | bytes 1179652
  0.0 14.8 %copy-start.3 = (s32[3,4]{1,0:T(4,128)S(1)}, s32[3,4]{1,0:T(4,128)}, u32[]{:S(2)}) copy-start(s32[3,4]{1,0:T(4,128)} %mine_cols.1) | copy-start | bytes 148
  0.0 46.9 %copy-start = (bf16[8,12,128,128]{3,2,1,0:T(8,128)(2,1)S(1)}, bf16[8,12,128,128]{3,2,1,0:T(8,128)(2,1)}, u32[]{:S(2)}) copy-start(bf16[8,12,128,128]{3,2,1,0:T(8,128)(2,1)} %t_ref.3) | copy-start | bytes 9437188
  5.7 41.2 %copy-start.2 = (s32[8,12]{1,0:T(8,128)S(1)}, s32[8,12]{1,0:T(8,128)}, u32[]{:S(2)}) copy-start(s32[8,12]{1,0:T(8,128)} %get-tuple-element.16.slot_ref) | copy-start | bytes 1156
  5.7 2.1 %collective-permute-start = (bf16[12,128,128]{2,1,0:T(8,128)(2,1)}, bf16[12,128,128]{2,1,0:T(8,128)(2,1)S(1)}, u32[]{:S(2)}, u32[]{:S(2)}) collective-permute-start(bf16[12,128,128]{2,1,0:T(8,128)(2,1)} %get-tuple-element.18), channel_id=1, source_target_pairs={{0,1},{1,0},{2,3},{3,2},{4,5},{5,4},{6,7},{7,6},{8,9},{9,8},{10,11... | collective-permute-start | bytes 1179656 | tf_op jit(solution)/shard_map/ppermute | solution.py:173
  8.9 14.0 %collective-permute-start.4 = (bf16[3,4,128,128]{3,2,1,0:T(8,128)(2,1)S(1)}, bf16[3,4,128,128]{3,2,1,0:T(8,128)(2,1)S(1)}, u32[]{:S(2)}, u32[]{:S(2)}) collective-permute-start(bf16[3,4,128,128]{3,2,1,0:T(8,128)(2,1)S(1)} %copy-done.1), channel_id=1, source_target_pairs={{0,1},{1,0},{2,3},{3,2},{4,5},{5,4},{6,7},{7,6},{8,9},{9,8},{10,11... | collective-permute-start | bytes 1179656 | tf_op jit(solution)/shard_map/ppermute | solution.py:173
  9.4 6.5 %collective-permute-start.1 = (bf16[3,128,128]{2,1,0:T(8,128)(2,1)S(1)}, bf16[3,128,128]{2,1,0:T(8,128)(2,1)S(1)}, u32[]{:S(2)}, u32[]{:S(2)}) collective-permute-start(bf16[3,128,128]{2,1,0:T(8,128)(2,1)S(1)} %get-tuple-element.31), channel_id=1, source_target_pairs={{0,4},{4,0},{8,12},{12,8},{1,5},{5,1},{9,13},{13,9},{2,6},{6,2},{1... | collective-permute-start | bytes 294920 | tf_op jit(solution)/shard_map/ppermute | solution.py:173
  12.2 10.7 %collective-permute-start.2 = (bf16[3,128,128]{2,1,0:T(8,128)(2,1)S(1)}, bf16[3,128,128]{2,1,0:T(8,128)(2,1)S(1)}, u32[]{:S(2)}, u32[]{:S(2)}) collective-permute-start(bf16[3,128,128]{2,1,0:T(8,128)(2,1)S(1)} %get-tuple-element.30), channel_id=1, source_target_pairs={{0,8},{4,12},{8,0},{12,4},{1,9},{5,13},{9,1},{13,5},{2,10},{6,14},... | collective-permute-start | bytes 294920 | tf_op jit(solution)/shard_map/ppermute | solution.py:173
  14.8 8.1 %collective-permute-start.3 = (bf16[3,128,128]{2,1,0:T(8,128)(2,1)S(1)}, bf16[3,128,128]{2,1,0:T(8,128)(2,1)S(1)}, u32[]{:S(2)}, u32[]{:S(2)}) collective-permute-start(bf16[3,128,128]{2,1,0:T(8,128)(2,1)S(1)} %get-tuple-element.29), channel_id=1, source_target_pairs={{0,12},{4,8},{8,4},{12,0},{1,13},{5,9},{9,5},{13,1},{2,14},{6,10},... | collective-permute-start | bytes 294920 | tf_op jit(solution)/shard_map/ppermute | solution.py:173
  14.8 1.2 %collective-permute-start.5 = (s32[3,4]{1,0:T(4,128)S(1)}, s32[3,4]{1,0:T(4,128)S(1)}, u32[]{:S(2)}, u32[]{:S(2)}) collective-permute-start(s32[3,4]{1,0:T(4,128)S(1)} %copy-done.3), channel_id=1, source_target_pairs={{0,1},{1,0},{2,3},{3,2},{4,5},{5,4},{6,7},{7,6},{8,9},{9,8},{10,11... | collective-permute-start | bytes 152 | tf_op jit(solution)/shard_map/ppermute | solution.py:173
  23.0 4.7 %collective-permute-start.6 = (bf16[3,128,128]{2,1,0:T(8,128)(2,1)S(1)}, bf16[3,128,128]{2,1,0:T(8,128)(2,1)S(1)}, u32[]{:S(2)}, u32[]{:S(2)}) collective-permute-start(bf16[3,128,128]{2,1,0:T(8,128)(2,1)S(1)} %fusion.4), channel_id=1, source_target_pairs={{0,2},{2,0},{1,3},{3,1},{4,6},{6,4},{5,7},{7,5},{8,10},{10,8},{9,1... | collective-permute-start | bytes 294920 | tf_op jit(solution)/shard_map/ppermute | solution.py:178
  27.7 5.7 %collective-permute-start.7 = (bf16[6,128,128]{2,1,0:T(8,128)(2,1)S(1)}, bf16[6,128,128]{2,1,0:T(8,128)(2,1)S(1)}, u32[]{:S(2)}, u32[]{:S(2)}) collective-permute-start(bf16[6,128,128]{2,1,0:T(8,128)(2,1)S(1)} %pad_maximum_fusion.1.near_ref), channel_id=1, source_target_pairs={{0,4},{4,0},{8,12},{12,8},{1,5},{5,1},{9,13},{13,9},{2,6},{6,2},{1... | collective-permute-start | bytes 589832 | tf_op jit(solution)/shard_map/ppermute | solution.py:185
  29.6 3.8 %collective-permute-start.8 = (bf16[6,128,128]{2,1,0:T(8,128)(2,1)S(1)}, bf16[6,128,128]{2,1,0:T(8,128)(2,1)S(1)}, u32[]{:S(2)}, u32[]{:S(2)}) collective-permute-start(bf16[6,128,128]{2,1,0:T(8,128)(2,1)S(1)} %pad_maximum_fusion.1.near_ref), channel_id=1, source_target_pairs={{4,8},{8,4},{5,9},{9,5},{6,10},{10,6},{7,11},{11,7},{20,24},{24,20... | collective-permute-start | bytes 589832 | tf_op jit(solution)/shard_map/ppermute | solution.py:185
  34.6 7.7 %collective-permute-start.9 = (bf16[3,128,128]{2,1,0:T(8,128)(2,1)S(1)}, bf16[3,128,128]{2,1,0:T(8,128)(2,1)S(1)}, u32[]{:S(2)}, u32[]{:S(2)}) collective-permute-start(bf16[3,128,128]{2,1,0:T(8,128)(2,1)S(1)} %metric.1.rest_0_), channel_id=1, source_target_pairs={{0,4},{4,0},{8,12},{12,8},{1,5},{5,1},{9,13},{13,9},{2,6},{6,2},{1... | collective-permute-start | bytes 294920 | tf_op jit(solution)/shard_map/ppermute | solution.py:173
  38.6 7.8 %collective-permute-start.10 = (bf16[3,128,128]{2,1,0:T(8,128)(2,1)S(1)}, bf16[3,128,128]{2,1,0:T(8,128)(2,1)S(1)}, u32[]{:S(2)}, u32[]{:S(2)}) collective-permute-start(bf16[3,128,128]{2,1,0:T(8,128)(2,1)S(1)} %metric.1.rest_0_), channel_id=1, source_target_pairs={{0,8},{4,12},{8,0},{12,4},{1,9},{5,13},{9,1},{13,5},{2,10},{6,14},... | collective-permute-start | bytes 294920 | tf_op jit(solution)/shard_map/ppermute | solution.py:173
  39.8 6.6 %collective-permute-start.11 = (bf16[3,128,128]{2,1,0:T(8,128)(2,1)S(1)}, bf16[3,128,128]{2,1,0:T(8,128)(2,1)S(1)}, u32[]{:S(2)}, u32[]{:S(2)}) collective-permute-start(bf16[3,128,128]{2,1,0:T(8,128)(2,1)S(1)} %metric.1.rest_0_), channel_id=1, source_target_pairs={{0,12},{4,8},{8,4},{12,0},{1,13},{5,9},{9,5},{13,1},{2,14},{6,10},... | collective-permute-start | bytes 294920 | tf_op jit(solution)/shard_map/ppermute | solution.py:173
  41.2 8.9 %collective-permute-start.13 = (bf16[3,128,128]{2,1,0:T(8,128)(2,1)S(1)}, bf16[3,128,128]{2,1,0:T(8,128)(2,1)S(1)}, u32[]{:S(2)}, u32[]{:S(2)}) collective-permute-start(bf16[3,128,128]{2,1,0:T(8,128)(2,1)S(1)} %metric.1.rest_0_), channel_id=1, source_target_pairs={{0,1},{1,0},{2,3},{3,2},{4,5},{5,4},{6,7},{7,6},{8,9},{9,8},{10,11... | collective-permute-start | bytes 294920 | tf_op jit(solution)/shard_map/ppermute | solution.py:173
  42.3 7.7 %collective-permute-start.14 = (bf16[3,128,128]{2,1,0:T(8,128)(2,1)S(1)}, bf16[3,128,128]{2,1,0:T(8,128)(2,1)S(1)}, u32[]{:S(2)}, u32[]{:S(2)}) collective-permute-start(bf16[3,128,128]{2,1,0:T(8,128)(2,1)S(1)} %collective-permute-done.9.rest_1_), channel_id=1, source_target_pairs={{0,1},{1,0},{2,3},{3,2},{4,5},{5,4},{6,7},{7,6},{8,9},{9,8},{10,11... | collective-permute-start | bytes 294920 | tf_op jit(solution)/shard_map/ppermute | solution.py:173
  46.4 3.7 %collective-permute-start.15 = (bf16[3,128,128]{2,1,0:T(8,128)(2,1)S(1)}, bf16[3,128,128]{2,1,0:T(8,128)(2,1)S(1)}, u32[]{:S(2)}, u32[]{:S(2)}) collective-permute-start(bf16[3,128,128]{2,1,0:T(8,128)(2,1)S(1)} %collective-permute-done.10.rest_2_), channel_id=1, source_target_pairs={{0,1},{1,0},{2,3},{3,2},{4,5},{5,4},{6,7},{7,6},{8,9},{9,8},{10,11... | collective-permute-start | bytes 294920 | tf_op jit(solution)/shard_map/ppermute | solution.py:173
  46.4 3.7 %collective-permute-start.16 = (bf16[3,128,128]{2,1,0:T(8,128)(2,1)S(1)}, bf16[3,128,128]{2,1,0:T(8,128)(2,1)S(1)}, u32[]{:S(2)}, u32[]{:S(2)}) collective-permute-start(bf16[3,128,128]{2,1,0:T(8,128)(2,1)S(1)} %collective-permute-done.11.rest_3_), channel_id=1, source_target_pairs={{0,1},{1,0},{2,3},{3,2},{4,5},{5,4},{6,7},{7,6},{8,9},{9,8},{10,11... | collective-permute-start | bytes 294920 | tf_op jit(solution)/shard_map/ppermute | solution.py:173
  48.5 5.5 %collective-permute-start.12 = (bf16[8,64,128]{2,1,0:T(8,128)(2,1)S(1)}, bf16[8,64,128]{2,1,0:T(8,128)(2,1)S(1)}, u32[]{:S(2)}, u32[]{:S(2)}) collective-permute-start(bf16[8,64,128]{2,1,0:T(8,128)(2,1)S(1)} %slice_bitcast_fusion.2), channel_id=1, source_target_pairs={{0,2},{2,0},{1,3},{3,1},{4,6},{6,4},{5,7},{7,5},{8,10},{10,8},{9,1... | collective-permute-start | bytes 393224 | tf_op jit(solution)/shard_map/ppermute | solution.py:178
  51.7 5.2 %collective-permute-start.17 = (bf16[8,64,128]{2,1,0:T(8,128)(2,1)S(1)}, bf16[8,64,128]{2,1,0:T(8,128)(2,1)S(1)}, u32[]{:S(2)}, u32[]{:S(2)}) collective-permute-start(bf16[8,64,128]{2,1,0:T(8,128)(2,1)S(1)} %slice_bitcast_fusion), channel_id=1, source_target_pairs={{0,2},{2,0},{1,3},{3,1},{4,6},{6,4},{5,7},{7,5},{8,10},{10,8},{9,1... | collective-permute-start | bytes 393224 | tf_op jit(solution)/shard_map/ppermute | solution.py:178

commit v3 on v2

--- a/solution.py
+++ b/solution.py
@@ -11,68 +11,66 @@
 F32 = jnp.float32
 NT = (((1,), (1,)), ((), ()))
 VMEM_LIMIT = 32 * 1024 * 1024
-FIT_VMEM_LIMIT = 56 * 1024 * 1024
+FIT_VMEM_LIMIT = 53 * 1024 * 1024
 VMEM = pl.BlockSpec(memory_space=pltpu.VMEM)
 SMEM = pl.BlockSpec(memory_space=pltpu.SMEM)
 
 
 def fit_kernel(
-    owned, half, tile_hbm, domain_hbm, number_hbm, d_hbm, t_hbm, keep_ref, send_ref, slot_ref,
-    acc, tile_ref, domain_ref, number_ref, d_ref, t_ref, small_sem, d_sem, t_sem,
+    owned, half, groups, table_ref, d_hbm, t_hbm, keep_ref, send_ref, slot_ref, acc, d_ref, t_ref, d_sem, t_sem
 ):
     me = lax.axis_index("space")
     mine = lax.axis_index("sub")
     blocks, listed = t_ref.shape[:2]
-    small = [
-        pltpu.make_async_copy(tile_hbm, tile_ref, small_sem.at[0]),
-        pltpu.make_async_copy(domain_hbm, domain_ref, small_sem.at[1]),
-        pltpu.make_async_copy(number_hbm, number_ref, small_sem.at[2]),
-    ]
-    d_copies = [pltpu.make_async_copy(d_hbm.at[p], d_ref.at[p], d_sem.at[p]) for p in range(blocks)]
-    t_copies = [pltpu.make_async_copy(t_hbm.at[p], t_ref.at[p], t_sem.at[p]) for p in range(blocks)]
-    for copy in small:
-        copy.start()
-    for p in range(blocks):
-        d_copies[p].start()
-        t_copies[p].start()
+    copies, begin = [], 0
+    for i, size in enumerate(groups):
+        part = pl.ds(begin, size)
+        copies.append(
+            (
+                pltpu.make_async_copy(d_hbm.at[part], d_ref.at[part], d_sem.at[i]),
+                pltpu.make_async_copy(t_hbm.at[part], t_ref.at[part], t_sem.at[i]),
+            )
+        )
+        begin += size
+    for pair in copies:
+        for copy in pair:
+            copy.start()
     acc[...] = jnp.zeros_like(acc)
-    for copy in small:
-        copy.wait()
-    for p in range(blocks):
-        d_copies[p].wait()
-        rows = jnp.transpose(d_ref[p])
-        t_copies[p].wait()
-        for k in range(listed):
-            touched = tile_ref[p, k]
-            slot = jnp.bitwise_xor(domain_ref[touched], me) * owned + number_ref[touched]
-            slot_ref[p, k] = slot
-            acc[slot] += jnp.dot(rows, t_ref[p, k], preferred_element_type=F32)
+    begin = 0
+    for size, pair in zip(groups, copies):
+        for copy in pair:
+            copy.wait()
+        for p in range(begin, begin + size):
+            rows = jnp.transpose(d_ref[p])
+            for k in range(listed):
+                touched = table_ref[p, k]
+                slot = jnp.bitwise_xor(table_ref[blocks, touched], me) * owned + table_ref[blocks + 1, touched]
+                slot_ref[p, k] = slot
+                acc[slot] += jnp.dot(rows, t_ref[p, k], preferred_element_type=F32)
+        begin += size
     keep_ref[...] = acc[:, pl.ds(pl.multiple_of(mine * half, half), half), :].astype(BF16)
     send_ref[...] = acc[:, pl.ds(pl.multiple_of((1 - mine) * half, half), half), :].astype(BF16)
 
 
-def fit(block_tile, domain, number, densities, three_centre, domains, owned):
+def fit(tables, densities, three_centre, domains, owned):
     blocks, listed, width, _ = three_centre.shape
     columns = densities.shape[2]
     half = columns // 2
-    slots = domains * owned
-    out = jax.ShapeDtypeStruct((slots, half, width), BF16)
+    count = domains * owned
+    groups = (blocks // 4, blocks // 4, blocks - 2 * (blocks // 4))
+    out = jax.ShapeDtypeStruct((count, half, width), BF16)
     return pl.pallas_call(
-        functools.partial(fit_kernel, owned, half),
-        in_specs=[pl.BlockSpec(memory_space=pltpu.HBM)] * 5,
+        functools.partial(fit_kernel, owned, half, groups),
+        in_specs=[SMEM] + [pl.BlockSpec(memory_space=pltpu.HBM)] * 2,
         out_specs=[VMEM, VMEM, SMEM],
         scratch_shapes=[
-            pltpu.VMEM((slots, columns, width), F32),
-            pltpu.SMEM(block_tile.shape, jnp.int32),
-            pltpu.SMEM(domain.shape, jnp.int32),
-            pltpu.SMEM(number.shape, jnp.int32),
+            pltpu.VMEM((count, columns, width), F32),
             pltpu.VMEM(densities.shape, BF16),
             pltpu.VMEM(three_centre.shape, BF16),
-            pltpu.SemaphoreType.DMA((3,)),
-            pltpu.SemaphoreType.DMA((blocks,)),
-            pltpu.SemaphoreType.DMA((blocks,)),
+            pltpu.SemaphoreType.DMA((len(groups),)),
+            pltpu.SemaphoreType.DMA((len(groups),)),
         ],
-        out_shape=[out, out, jax.ShapeDtypeStruct(block_tile.shape, jnp.int32)],
+        out_shape=[out, out, jax.ShapeDtypeStruct((blocks, listed), jnp.int32)],
         compiler_params=pltpu.CompilerParams(vmem_limit_bytes=FIT_VMEM_LIMIT),
         cost_estimate=pl.CostEstimate(
             flops=2 * blocks * listed * width * width * columns,
@@ -80,10 +78,10 @@
             transcendentals=0,
         ),
         name="fit",
-    )(block_tile, domain, number, densities, three_centre)
-
-
-def metric_kernel(owned, count, mine_cols, peer_cols, near_ref, even_ref, odd_ref, m_ref, pm_ref, out_ref, window):
+    )(tables, densities, three_centre)
+
+
+def metric_kernel(owned, count, mine_cols, peer_cols, near_ref, odd_ref, even_ref, m_ref, pm_ref, out_ref, window):
     me = lax.axis_index("space")
     aux = lax.axis_index("aux")
     own = owned * count
@@ -113,7 +111,7 @@
         ).astype(BF16)
 
 
-def metric(mine_cols, peer_cols, near, even, odd, m, pm, count):
+def metric(mine_cols, peer_cols, near, odd, even, m, pm, count):
     owned, listed, width, _ = m.shape
     half = near.shape[1]
     return pl.pallas_call(
@@ -129,7 +127,7 @@
             transcendentals=0,
         ),
         name="metric",
-    )(mine_cols, peer_cols, near, even, odd, m, pm)
+    )(mine_cols, peer_cols, near, odd, even, m, pm)
 
 
 def build_kernel(parts, slot_ref, t_ref, *rest):
@@ -196,7 +194,11 @@
     domain = owner_domain.reshape(touched)
     number = owner_tile.reshape(touched)
 
-    keep, send, slots = fit(block_tile, domain, number, densities, three_centre, domains, owned)
+    wide = max(touched, block_tile.shape[1])
+    tables = jnp.concatenate(
+        [jnp.pad(row, ((0, 0), (0, wide - row.shape[1]))) for row in (block_tile, domain[None], number[None])]
+    )
+    keep, send, slots = fit(tables, densities, three_centre, domains, owned)
     got = exchange(send, "sub", 1)
     chip = (keep.astype(F32) + got.astype(F32)).astype(BF16).reshape(domains, owned, half, width)
     chip, own_metric, own_columns = lax.optimization_barrier((chip, metric_inverse, metric_columns))
@@ -212,10 +214,10 @@
     near = jnp.concatenate(
         [fitted] + [ahead_by(fitted, "aux", aux_count - k) for k in range(1, aux_count)]
     )
+    odd = pairs_from(near, "space", 1)
     even = pairs_from(near, "space", 0)
-    odd = pairs_from(near, "space", 1)
     coefficients = metric(
-        metric_columns, peer_columns, near, even, odd, metric_inverse, peer_metric, aux_count
+        metric_columns, peer_columns, near, odd, even, metric_inverse, peer_metric, aux_count
     )
 
     pieces = [coefficients] + [exchange(coefficients, "space", k) for k in range(1, domains)]

time: 57.9 us -> 57.9 us (level)
  starting transfers between devices: 19.6 us -> 20.5 us
  Pallas kernels: 10.1 us -> 9.5 us
    ppermute x2, starting transfers between devices: 2.57 us -> 5.43 us  [pairs_from(): return lax.ppermute(array, axis, swaps)]
    ppermute x13, starting transfers between devices: 13.4 us -> 11.4 us  [exchange(): lax.ppermute(array, axis, [(i, i ^ distance) for i in range(lax.axis_size...]
    convert_element_type x1, other arithmetic: 1.1 us -> 0.11 us  [shards(): (keep.astype(F32) + got.astype(F32)).astype(BF16)]
    concatenate x0 -> x1, other arithmetic: none -> 0.76 us  [shards(): jnp.concatenate([jnp.pad(row, ((0, 0), (0, wide - row.shape[1]))) for row...]
    pallas_call x1, Pallas kernels: 5.69 us -> 5 us  [fit(): pl.pallas_call(functools.partial(fit_kernel, owned, half, groups), in_spe...]
where the time goes in v3:
time: 57.9 us; the launch traced here: 57.7 us
  waiting for transfers between devices  25.8 us (45%)
  starting transfers between devices  20.5 us (35%)
  Pallas kernels  9.5 us (16%)
  other arithmetic  1.77 us (3%)
    ppermute x13, waiting for transfers between devices, exchange(): lax.ppermute(array, axis, [(i, i ^ distance) for i in range(lax.axis_size...  14.4 us
    ppermute x13, starting transfers between devices, exchange(): lax.ppermute(array, axis, [(i, i ^ distance) for i in range(lax.axis_size...  11.4 us
    ppermute x3, waiting for transfers between devices, ahead_by(): lax.ppermute(array, axis, [(i, (i + distance) % count) for i in range(cou...  7.76 us
    ppermute x2, starting transfers between devices, pairs_from(): return lax.ppermute(array, axis, swaps)  5.43 us
    pallas_call x1, Pallas kernels, fit(): pl.pallas_call(functools.partial(fit_kernel, owned, half, groups), in_spe...  5 us
    ppermute x3, starting transfers between devices, ahead_by(): lax.ppermute(array, axis, [(i, (i + distance) % count) for i in range(cou...  3.68 us
    ppermute x2, waiting for transfers between devices, pairs_from(): return lax.ppermute(array, axis, swaps)  3.65 us
    pallas_call x2, Pallas kernels, build(): pl.pallas_call(functools.partial(build_kernel, parts), in_specs=[SMEM] +...  3.28 us
  transfers between devices with their start and end apart: 18, of which 9 were waited for; matrix products, arithmetic and copies ran while one was open for 0% of the time, Pallas kernels for 6%

profile of v3, /device:TPU:0, one launch (start us, length us, event | category | flops | bytes accessed | tf_op | source)
XLA Modules:
  0.0 57.7 jit_solution(6788953622559543439)
XLA Ops:
  0.0 0.8 %fusion.5.table_ref = s32[10,32]{1,0:T(8,128)S(1)} fusion(s32[8,12]{1,0:T(8,128)} %param.9, s32[1,32]{1,0:T(1,128)} %bitcast.36, s32[1,32]{1,0:T(1,128)} %bitcast.37), kind=kLoop, calls=%fused_computation.21 | loop fusion | flops 640 | bytes 1920 | tf_op jit(solution)/shard_map/concatenate | solution.py:198
  0.8 5.0 %fit.1 = (bf16[12,128,128]{2,1,0:T(8,128)(2,1)S(1)}, bf16[12,128,128]{2,1,0:T(8,128)(2,1)S(1)}, s32[8,12]{1,0:T(8,128)S(1)}) custom-call(s32[10,32]{1,0:T(8,128)S(1)} %fusion.5.table_ref, bf16[8,128,256]{2,1,0:T(8,128)(2,1)} %d_hbm.1, bf16[8,12,128,128]{3,2,1,0:T(8,128)(2,1)} %t_ref.3), custom_call_target="tpu_custom_call" | custom-call | flops 805306368 | bytes 3670016 | tf_op jit(solution)/shard_map/fit/pallas_call | solution.py:62
  6.3 1.3 %collective-permute-done = bf16[12,128,128]{2,1,0:T(8,128)(2,1)S(1)} collective-permute-done((bf16[12,128,128]{2,1,0:T(8,128)(2,1)S(1)}, bf16[12,128,128]{2,1,0:T(8,128)(2,1)S(1)}, u32[]{:S(2)}, u32[]{:S(2)}) %collective-permute-start) | collective-permute-done | bytes 393248 | tf_op jit(solution)/shard_map/ppermute | solution.py:171
  8.2 2.8 %collective-permute-start.1 = (bf16[3,128,128]{2,1,0:T(8,128)(2,1)S(1)}, bf16[3,128,128]{2,1,0:T(8,128)(2,1)S(1)}, u32[]{:S(2)}, u32[]{:S(2)}) collective-permute-start(bf16[3,128,128]{2,1,0:T(8,128)(2,1)S(1)} %get-tuple-element.31), channel_id=1, source_target_pairs={{0,4},{4,0},{8,12},{12,8},{1,5},{5,1},{9,13},{13,9},{2,6},{6,2},{1... | collective-permute-start | bytes 294920 | tf_op jit(solution)/shard_map/ppermute | solution.py:171
  11.0 2.6 %collective-permute-start.2 = (bf16[3,128,128]{2,1,0:T(8,128)(2,1)S(1)}, bf16[3,128,128]{2,1,0:T(8,128)(2,1)S(1)}, u32[]{:S(2)}, u32[]{:S(2)}) collective-permute-start(bf16[3,128,128]{2,1,0:T(8,128)(2,1)S(1)} %get-tuple-element.30), channel_id=1, source_target_pairs={{0,8},{4,12},{8,0},{12,4},{1,9},{5,13},{9,1},{13,5},{2,10},{6,14},... | collective-permute-start | bytes 294920 | tf_op jit(solution)/shard_map/ppermute | solution.py:171
  13.6 1.2 %collective-permute-done.5.peer_cols = s32[3,4]{1,0:T(4,128)S(1)} collective-permute-done((s32[3,4]{1,0:T(4,128)S(1)}, s32[3,4]{1,0:T(4,128)S(1)}, u32[]{:S(2)}, u32[]{:S(2)}) %collective-permute-start.5) | collective-permute-done | bytes 80 | tf_op jit(solution)/shard_map/ppermute | solution.py:171
  14.8 7.0 %collective-permute-done.2 = bf16[3,128,128]{2,1,0:T(8,128)(2,1)S(1)} collective-permute-done((bf16[3,128,128]{2,1,0:T(8,128)(2,1)S(1)}, bf16[3,128,128]{2,1,0:T(8,128)(2,1)S(1)}, u32[]{:S(2)}, u32[]{:S(2)}) %collective-permute-start.2) | collective-permute-done | bytes 98336 | tf_op jit(solution)/shard_map/ppermute | solution.py:171
  21.8 1.5 %collective-permute-start.6 = (bf16[3,128,128]{2,1,0:T(8,128)(2,1)S(1)}, bf16[3,128,128]{2,1,0:T(8,128)(2,1)S(1)}, u32[]{:S(2)}, u32[]{:S(2)}) collective-permute-start(bf16[3,128,128]{2,1,0:T(8,128)(2,1)S(1)} %fusion.4), channel_id=1, source_target_pairs={{0,2},{2,0},{1,3},{3,1},{4,6},{6,4},{5,7},{7,5},{8,10},{10,8},{9,1... | collective-permute-start | bytes 294920 | tf_op jit(solution)/shard_map/ppermute | solution.py:176
  23.3 3.2 %collective-permute-done.6 = bf16[3,128,128]{2,1,0:T(8,128)(2,1)S(1)} collective-permute-done((bf16[3,128,128]{2,1,0:T(8,128)(2,1)S(1)}, bf16[3,128,128]{2,1,0:T(8,128)(2,1)S(1)}, u32[]{:S(2)}, u32[]{:S(2)}) %collective-permute-start.6) | collective-permute-done | bytes 98336 | tf_op jit(solution)/shard_map/ppermute | solution.py:176
  26.5 0.7 %collective-permute-start.7 = (bf16[6,128,128]{2,1,0:T(8,128)(2,1)S(1)}, bf16[6,128,128]{2,1,0:T(8,128)(2,1)S(1)}, u32[]{:S(2)}, u32[]{:S(2)}) collective-permute-start(bf16[6,128,128]{2,1,0:T(8,128)(2,1)S(1)} %pad_maximum_fusion.1.near_ref), channel_id=1, source_target_pairs={{4,8},{8,4},{5,9},{9,5},{6,10},{10,6},{7,11},{11,7},{20,24},{24,20... | collective-permute-start | bytes 589832 | tf_op jit(solution)/shard_map/ppermute | solution.py:183
  27.2 4.8 %collective-permute-start.8 = (bf16[6,128,128]{2,1,0:T(8,128)(2,1)S(1)}, bf16[6,128,128]{2,1,0:T(8,128)(2,1)S(1)}, u32[]{:S(2)}, u32[]{:S(2)}) collective-permute-start(bf16[6,128,128]{2,1,0:T(8,128)(2,1)S(1)} %pad_maximum_fusion.1.near_ref), channel_id=1, source_target_pairs={{0,4},{4,0},{8,12},{12,8},{1,5},{5,1},{9,13},{13,9},{2,6},{6,2},{1... | collective-permute-start | bytes 589832 | tf_op jit(solution)/shard_map/ppermute | solution.py:183
  32.0 3.6 %collective-permute-done.8.even_ref = bf16[6,128,128]{2,1,0:T(8,128)(2,1)S(1)} collective-permute-done((bf16[6,128,128]{2,1,0:T(8,128)(2,1)S(1)}, bf16[6,128,128]{2,1,0:T(8,128)(2,1)S(1)}, u32[]{:S(2)}, u32[]{:S(2)}) %collective-permute-start.8) | collective-permute-done | bytes 196640 | tf_op jit(solution)/shard_map/ppermute | solution.py:183
  35.6 1.2 %metric.1.rest_0_ = bf16[3,128,128]{2,1,0:T(8,128)(2,1)S(1)} custom-call(s32[3,4]{1,0:T(4,128)S(1)} %copy-done.2, s32[3,4]{1,0:T(4,128)S(1)} %collective-permute-done.5.peer_cols, bf16[6,128,128]{2,1,0:T(8,128)(2,1)S(1)} %pad_maximum_fusion.1.near_ref, bf16[6,128,128]{2,1,0:T(8,128)(2,1)S(1)} %collective-permute-done.7.odd_ref, ...), custom_call_target="tpu_custom_call" | custom-call | flops 100663296 | bytes 1376256 | tf_op jit(solution)/shard_map/metric/pallas_call | solution.py:117
  36.8 2.1 %collective-permute-start.9 = (bf16[3,128,128]{2,1,0:T(8,128)(2,1)S(1)}, bf16[3,128,128]{2,1,0:T(8,128)(2,1)S(1)}, u32[]{:S(2)}, u32[]{:S(2)}) collective-permute-start(bf16[3,128,128]{2,1,0:T(8,128)(2,1)S(1)} %metric.1.rest_0_), channel_id=1, source_target_pairs={{0,4},{4,0},{8,12},{12,8},{1,5},{5,1},{9,13},{13,9},{2,6},{6,2},{1... | collective-permute-start | bytes 294920 | tf_op jit(solution)/shard_map/ppermute | solution.py:171
  38.9 2.4 %collective-permute-start.11 = (bf16[3,128,128]{2,1,0:T(8,128)(2,1)S(1)}, bf16[3,128,128]{2,1,0:T(8,128)(2,1)S(1)}, u32[]{:S(2)}, u32[]{:S(2)}) collective-permute-start(bf16[3,128,128]{2,1,0:T(8,128)(2,1)S(1)} %metric.1.rest_0_), channel_id=1, source_target_pairs={{0,12},{4,8},{8,4},{12,0},{1,13},{5,9},{9,5},{13,1},{2,14},{6,10},... | collective-permute-start | bytes 294920 | tf_op jit(solution)/shard_map/ppermute | solution.py:171
  41.4 1.7 %collective-permute-done.9.rest_1_ = bf16[3,128,128]{2,1,0:T(8,128)(2,1)S(1)} collective-permute-done((bf16[3,128,128]{2,1,0:T(8,128)(2,1)S(1)}, bf16[3,128,128]{2,1,0:T(8,128)(2,1)S(1)}, u32[]{:S(2)}, u32[]{:S(2)}) %collective-permute-start.9) | collective-permute-done | bytes 98336 | tf_op jit(solution)/shard_map/ppermute | solution.py:171
  43.1 3.2 %collective-permute-done.10.rest_2_ = bf16[3,128,128]{2,1,0:T(8,128)(2,1)S(1)} collective-permute-done((bf16[3,128,128]{2,1,0:T(8,128)(2,1)S(1)}, bf16[3,128,128]{2,1,0:T(8,128)(2,1)S(1)}, u32[]{:S(2)}, u32[]{:S(2)}) %collective-permute-start.10) | collective-permute-done | bytes 98336 | tf_op jit(solution)/shard_map/ppermute | solution.py:171
  46.8 1.6 %build_own.1 = bf16[2,8,64,128]{3,2,1,0:T(8,128)(2,1)S(1)} custom-call(s32[8,12]{1,0:T(8,128)S(1)} %get-tuple-element.16.slot_ref, bf16[8,12,128,128]{3,2,1,0:T(8,128)(2,1)S(1)} %copy-done, bf16[3,128,128]{2,1,0:T(8,128)(2,1)S(1)} %metric.1.rest_0_, bf16[3,128,128]{2,1,0:T(8,128)(2,1)S(1)} %collective-permute-done.9.rest_1_, ...), custom_call_target="tpu_custom_call" | custom-call | flops 402653184 | bytes 3407872 | tf_op jit(solution)/shard_map/build_own/pallas_call | solution.py:154
  48.4 1.6 %collective-permute-start.12 = (bf16[8,64,128]{2,1,0:T(8,128)(2,1)S(1)}, bf16[8,64,128]{2,1,0:T(8,128)(2,1)S(1)}, u32[]{:S(2)}, u32[]{:S(2)}) collective-permute-start(bf16[8,64,128]{2,1,0:T(8,128)(2,1)S(1)} %slice_bitcast_fusion.2), channel_id=1, source_target_pairs={{0,2},{2,0},{1,3},{3,1},{4,6},{6,4},{5,7},{7,5},{8,10},{10,8},{9,1... | collective-permute-start | bytes 393224 | tf_op jit(solution)/shard_map/ppermute | solution.py:176
  50.0 1.6 %build_other.1 = bf16[2,8,64,128]{3,2,1,0:T(8,128)(2,1)S(1)} custom-call(s32[8,12]{1,0:T(8,128)S(1)} %get-tuple-element.16.slot_ref, bf16[8,12,128,128]{3,2,1,0:T(8,128)(2,1)S(1)} %copy-done, bf16[3,128,128]{2,1,0:T(8,128)(2,1)S(1)} %collective-permute-done.13.rest_0_, bf16[3,128,128]{2,1,0:T(8,128)(2,1)S(1)} %collective-permute-done.14.rest_1_, ...), custom_call_target="tpu_custom_call" | custom-call | flops 402653184 | bytes 3407872 | tf_op jit(solution)/shard_map/build_other/pallas_call | solution.py:154
  51.7 0.6 %collective-permute-start.17 = (bf16[8,64,128]{2,1,0:T(8,128)(2,1)S(1)}, bf16[8,64,128]{2,1,0:T(8,128)(2,1)S(1)}, u32[]{:S(2)}, u32[]{:S(2)}) collective-permute-start(bf16[8,64,128]{2,1,0:T(8,128)(2,1)S(1)} %slice_bitcast_fusion), channel_id=1, source_target_pairs={{0,2},{2,0},{1,3},{3,1},{4,6},{6,4},{5,7},{7,5},{8,10},{10,8},{9,1... | collective-permute-start | bytes 393224 | tf_op jit(solution)/shard_map/ppermute | solution.py:176
  52.3 1.6 %collective-permute-done.12 = bf16[8,64,128]{2,1,0:T(8,128)(2,1)S(1)} collective-permute-done((bf16[8,64,128]{2,1,0:T(8,128)(2,1)S(1)}, bf16[8,64,128]{2,1,0:T(8,128)(2,1)S(1)}, u32[]{:S(2)}, u32[]{:S(2)}) %collective-permute-start.12) | collective-permute-done | bytes 131104 | tf_op jit(solution)/shard_map/ppermute | solution.py:176
  53.9 3.0 %collective-permute-done.17 = bf16[8,64,128]{2,1,0:T(8,128)(2,1)S(1)} collective-permute-done((bf16[8,64,128]{2,1,0:T(8,128)(2,1)S(1)}, bf16[8,64,128]{2,1,0:T(8,128)(2,1)S(1)}, u32[]{:S(2)}, u32[]{:S(2)}) %collective-permute-start.17) | collective-permute-done | bytes 131104 | tf_op jit(solution)/shard_map/ppermute | solution.py:176
  57.0 0.7 %pad_maximum_fusion = bf16[8,64,256]{2,1,0:T(8,128)(2,1)} fusion(bf16[8,64,128]{2,1,0:T(8,128)(2,1)S(1)} %get-tuple-element.28, bf16[8,64,128]{2,1,0:T(8,128)(2,1)S(1)} %get-tuple-element.27), kind=kLoop, calls=%fused_computation.1 | loop fusion | flops 524288 | bytes 524288 | tf_op jit(solution)/shard_map/concatenate | solution.py:233
  (31 shorter events, 1.8 us)
Async XLA Ops:
  0.0 7.8 %copy-start.1 = (bf16[3,4,128,128]{3,2,1,0:T(8,128)(2,1)S(1)}, bf16[3,4,128,128]{3,2,1,0:T(8,128)(2,1)}, u32[]{:S(2)}) copy-start(bf16[3,4,128,128]{3,2,1,0:T(8,128)(2,1)} %m_ref.1) | copy-start | bytes 1179652
  0.0 13.6 %copy-start.2 = (s32[3,4]{1,0:T(4,128)S(1)}, s32[3,4]{1,0:T(4,128)}, u32[]{:S(2)}) copy-start(s32[3,4]{1,0:T(4,128)} %mine_cols.1) | copy-start | bytes 148
  0.8 46.0 %copy-start = (bf16[8,12,128,128]{3,2,1,0:T(8,128)(2,1)S(1)}, bf16[8,12,128,128]{3,2,1,0:T(8,128)(2,1)}, u32[]{:S(2)}) copy-start(bf16[8,12,128,128]{3,2,1,0:T(8,128)(2,1)} %t_ref.3) | copy-start | bytes 9437188
  5.8 1.9 %collective-permute-start = (bf16[12,128,128]{2,1,0:T(8,128)(2,1)S(1)}, bf16[12,128,128]{2,1,0:T(8,128)(2,1)S(1)}, u32[]{:S(2)}, u32[]{:S(2)}) collective-permute-start(bf16[12,128,128]{2,1,0:T(8,128)(2,1)S(1)} %get-tuple-element.18), channel_id=1, source_target_pairs={{0,1},{1,0},{2,3},{3,2},{4,5},{5,4},{6,7},{7,6},{8,9},{9,8},{10,11... | collective-permute-start | bytes 1179656 | tf_op jit(solution)/shard_map/ppermute | solution.py:171
  7.8 14.0 %collective-permute-start.4 = (bf16[3,4,128,128]{3,2,1,0:T(8,128)(2,1)S(1)}, bf16[3,4,128,128]{3,2,1,0:T(8,128)(2,1)S(1)}, u32[]{:S(2)}, u32[]{:S(2)}) collective-permute-start(bf16[3,4,128,128]{3,2,1,0:T(8,128)(2,1)S(1)} %copy-done.1), channel_id=1, source_target_pairs={{0,1},{1,0},{2,3},{3,2},{4,5},{5,4},{6,7},{7,6},{8,9},{9,8},{10,11... | collective-permute-start | bytes 1179656 | tf_op jit(solution)/shard_map/ppermute | solution.py:171
  8.2 6.5 %collective-permute-start.1 = (bf16[3,128,128]{2,1,0:T(8,128)(2,1)S(1)}, bf16[3,128,128]{2,1,0:T(8,128)(2,1)S(1)}, u32[]{:S(2)}, u32[]{:S(2)}) collective-permute-start(bf16[3,128,128]{2,1,0:T(8,128)(2,1)S(1)} %get-tuple-element.31), channel_id=1, source_target_pairs={{0,4},{4,0},{8,12},{12,8},{1,5},{5,1},{9,13},{13,9},{2,6},{6,2},{1... | collective-permute-start | bytes 294920 | tf_op jit(solution)/shard_map/ppermute | solution.py:171
  11.0 10.7 %collective-permute-start.2 = (bf16[3,128,128]{2,1,0:T(8,128)(2,1)S(1)}, bf16[3,128,128]{2,1,0:T(8,128)(2,1)S(1)}, u32[]{:S(2)}, u32[]{:S(2)}) collective-permute-start(bf16[3,128,128]{2,1,0:T(8,128)(2,1)S(1)} %get-tuple-element.30), channel_id=1, source_target_pairs={{0,8},{4,12},{8,0},{12,4},{1,9},{5,13},{9,1},{13,5},{2,10},{6,14},... | collective-permute-start | bytes 294920 | tf_op jit(solution)/shard_map/ppermute | solution.py:171
  13.6 8.1 %collective-permute-start.3 = (bf16[3,128,128]{2,1,0:T(8,128)(2,1)S(1)}, bf16[3,128,128]{2,1,0:T(8,128)(2,1)S(1)}, u32[]{:S(2)}, u32[]{:S(2)}) collective-permute-start(bf16[3,128,128]{2,1,0:T(8,128)(2,1)S(1)} %get-tuple-element.29), channel_id=1, source_target_pairs={{0,12},{4,8},{8,4},{12,0},{1,13},{5,9},{9,5},{13,1},{2,14},{6,10},... | collective-permute-start | bytes 294920 | tf_op jit(solution)/shard_map/ppermute | solution.py:171
  13.6 1.2 %collective-permute-start.5 = (s32[3,4]{1,0:T(4,128)S(1)}, s32[3,4]{1,0:T(4,128)S(1)}, u32[]{:S(2)}, u32[]{:S(2)}) collective-permute-start(s32[3,4]{1,0:T(4,128)S(1)} %copy-done.2), channel_id=1, source_target_pairs={{0,1},{1,0},{2,3},{3,2},{4,5},{5,4},{6,7},{7,6},{8,9},{9,8},{10,11... | collective-permute-start | bytes 152 | tf_op jit(solution)/shard_map/ppermute | solution.py:171
  21.8 4.7 %collective-permute-start.6 = (bf16[3,128,128]{2,1,0:T(8,128)(2,1)S(1)}, bf16[3,128,128]{2,1,0:T(8,128)(2,1)S(1)}, u32[]{:S(2)}, u32[]{:S(2)}) collective-permute-start(bf16[3,128,128]{2,1,0:T(8,128)(2,1)S(1)} %fusion.4), channel_id=1, source_target_pairs={{0,2},{2,0},{1,3},{3,1},{4,6},{6,4},{5,7},{7,5},{8,10},{10,8},{9,1... | collective-permute-start | bytes 294920 | tf_op jit(solution)/shard_map/ppermute | solution.py:176
  26.5 5.4 %collective-permute-start.7 = (bf16[6,128,128]{2,1,0:T(8,128)(2,1)S(1)}, bf16[6,128,128]{2,1,0:T(8,128)(2,1)S(1)}, u32[]{:S(2)}, u32[]{:S(2)}) collective-permute-start(bf16[6,128,128]{2,1,0:T(8,128)(2,1)S(1)} %pad_maximum_fusion.1.near_ref), channel_id=1, source_target_pairs={{4,8},{8,4},{5,9},{9,5},{6,10},{10,6},{7,11},{11,7},{20,24},{24,20... | collective-permute-start | bytes 589832 | tf_op jit(solution)/shard_map/ppermute | solution.py:183
  27.2 8.4 %collective-permute-start.8 = (bf16[6,128,128]{2,1,0:T(8,128)(2,1)S(1)}, bf16[6,128,128]{2,1,0:T(8,128)(2,1)S(1)}, u32[]{:S(2)}, u32[]{:S(2)}) collective-permute-start(bf16[6,128,128]{2,1,0:T(8,128)(2,1)S(1)} %pad_maximum_fusion.1.near_ref), channel_id=1, source_target_pairs={{0,4},{4,0},{8,12},{12,8},{1,5},{5,1},{9,13},{13,9},{2,6},{6,2},{1... | collective-permute-start | bytes 589832 | tf_op jit(solution)/shard_map/ppermute | solution.py:183
  36.8 6.3 %collective-permute-start.9 = (bf16[3,128,128]{2,1,0:T(8,128)(2,1)S(1)}, bf16[3,128,128]{2,1,0:T(8,128)(2,1)S(1)}, u32[]{:S(2)}, u32[]{:S(2)}) collective-permute-start(bf16[3,128,128]{2,1,0:T(8,128)(2,1)S(1)} %metric.1.rest_0_), channel_id=1, source_target_pairs={{0,4},{4,0},{8,12},{12,8},{1,5},{5,1},{9,13},{13,9},{2,6},{6,2},{1... | collective-permute-start | bytes 294920 | tf_op jit(solution)/shard_map/ppermute | solution.py:171
  38.9 7.3 %collective-permute-start.10 = (bf16[3,128,128]{2,1,0:T(8,128)(2,1)S(1)}, bf16[3,128,128]{2,1,0:T(8,128)(2,1)S(1)}, u32[]{:S(2)}, u32[]{:S(2)}) collective-permute-start(bf16[3,128,128]{2,1,0:T(8,128)(2,1)S(1)} %metric.1.rest_0_), channel_id=1, source_target_pairs={{0,8},{4,12},{8,0},{12,4},{1,9},{5,13},{9,1},{13,5},{2,10},{6,14},... | collective-permute-start | bytes 294920 | tf_op jit(solution)/shard_map/ppermute | solution.py:171
  38.9 7.3 %collective-permute-start.11 = (bf16[3,128,128]{2,1,0:T(8,128)(2,1)S(1)}, bf16[3,128,128]{2,1,0:T(8,128)(2,1)S(1)}, u32[]{:S(2)}, u32[]{:S(2)}) collective-permute-start(bf16[3,128,128]{2,1,0:T(8,128)(2,1)S(1)} %metric.1.rest_0_), channel_id=1, source_target_pairs={{0,12},{4,8},{8,4},{12,0},{1,13},{5,9},{9,5},{13,1},{2,14},{6,10},... | collective-permute-start | bytes 294920 | tf_op jit(solution)/shard_map/ppermute | solution.py:171
  41.4 8.7 %collective-permute-start.13 = (bf16[3,128,128]{2,1,0:T(8,128)(2,1)S(1)}, bf16[3,128,128]{2,1,0:T(8,128)(2,1)S(1)}, u32[]{:S(2)}, u32[]{:S(2)}) collective-permute-start(bf16[3,128,128]{2,1,0:T(8,128)(2,1)S(1)} %metric.1.rest_0_), channel_id=1, source_target_pairs={{0,1},{1,0},{2,3},{3,2},{4,5},{5,4},{6,7},{7,6},{8,9},{9,8},{10,11... | collective-permute-start | bytes 294920 | tf_op jit(solution)/shard_map/ppermute | solution.py:171
  43.1 6.9 %collective-permute-start.14 = (bf16[3,128,128]{2,1,0:T(8,128)(2,1)S(1)}, bf16[3,128,128]{2,1,0:T(8,128)(2,1)S(1)}, u32[]{:S(2)}, u32[]{:S(2)}) collective-permute-start(bf16[3,128,128]{2,1,0:T(8,128)(2,1)S(1)} %collective-permute-done.9.rest_1_), channel_id=1, source_target_pairs={{0,1},{1,0},{2,3},{3,2},{4,5},{5,4},{6,7},{7,6},{8,9},{9,8},{10,11... | collective-permute-start | bytes 294920 | tf_op jit(solution)/shard_map/ppermute | solution.py:171
  46.3 3.8 %collective-permute-start.15 = (bf16[3,128,128]{2,1,0:T(8,128)(2,1)S(1)}, bf16[3,128,128]{2,1,0:T(8,128)(2,1)S(1)}, u32[]{:S(2)}, u32[]{:S(2)}) collective-permute-start(bf16[3,128,128]{2,1,0:T(8,128)(2,1)S(1)} %collective-permute-done.10.rest_2_), channel_id=1, source_target_pairs={{0,1},{1,0},{2,3},{3,2},{4,5},{5,4},{6,7},{7,6},{8,9},{9,8},{10,11... | collective-permute-start | bytes 294920 | tf_op jit(solution)/shard_map/ppermute | solution.py:171
  46.3 3.8 %collective-permute-start.16 = (bf16[3,128,128]{2,1,0:T(8,128)(2,1)S(1)}, bf16[3,128,128]{2,1,0:T(8,128)(2,1)S(1)}, u32[]{:S(2)}, u32[]{:S(2)}) collective-permute-start(bf16[3,128,128]{2,1,0:T(8,128)(2,1)S(1)} %collective-permute-done.11.rest_3_), channel_id=1, source_target_pairs={{0,1},{1,0},{2,3},{3,2},{4,5},{5,4},{6,7},{7,6},{8,9},{9,8},{10,11... | collective-permute-start | bytes 294920 | tf_op jit(solution)/shard_map/ppermute | solution.py:171
  48.4 5.5 %collective-permute-start.12 = (bf16[8,64,128]{2,1,0:T(8,128)(2,1)S(1)}, bf16[8,64,128]{2,1,0:T(8,128)(2,1)S(1)}, u32[]{:S(2)}, u32[]{:S(2)}) collective-permute-start(bf16[8,64,128]{2,1,0:T(8,128)(2,1)S(1)} %slice_bitcast_fusion.2), channel_id=1, source_target_pairs={{0,2},{2,0},{1,3},{3,1},{4,6},{6,4},{5,7},{7,5},{8,10},{10,8},{9,1... | collective-permute-start | bytes 393224 | tf_op jit(solution)/shard_map/ppermute | solution.py:176
  51.7 5.2 %collective-permute-start.17 = (bf16[8,64,128]{2,1,0:T(8,128)(2,1)S(1)}, bf16[8,64,128]{2,1,0:T(8,128)(2,1)S(1)}, u32[]{:S(2)}, u32[]{:S(2)}) collective-permute-start(bf16[8,64,128]{2,1,0:T(8,128)(2,1)S(1)} %slice_bitcast_fusion), channel_id=1, source_target_pairs={{0,2},{2,0},{1,3},{3,1},{4,6},{6,4},{5,7},{7,5},{8,10},{10,8},{9,1... | collective-permute-start | bytes 393224 | tf_op jit(solution)/shard_map/ppermute | solution.py:176

commit v4 on v3

--- a/solution.py
+++ b/solution.py
@@ -81,7 +81,7 @@
     )(tables, densities, three_centre)
 
 
-def metric_kernel(owned, count, mine_cols, peer_cols, near_ref, odd_ref, even_ref, m_ref, pm_ref, out_ref, window):
+def metric_kernel(owned, count, mine_cols, peer_cols, near_ref, even_ref, odd_ref, m_ref, pm_ref, out_ref, window):
     me = lax.axis_index("space")
     aux = lax.axis_index("aux")
     own = owned * count
@@ -111,7 +111,7 @@
         ).astype(BF16)
 
 
-def metric(mine_cols, peer_cols, near, odd, even, m, pm, count):
+def metric(mine_cols, peer_cols, near, even, odd, m, pm, count):
     owned, listed, width, _ = m.shape
     half = near.shape[1]
     return pl.pallas_call(
@@ -127,16 +127,16 @@
             transcendentals=0,
         ),
         name="metric",
-    )(mine_cols, peer_cols, near, odd, even, m, pm)
-
-
-def build_kernel(parts, slot_ref, t_ref, *rest):
+    )(mine_cols, peer_cols, near, even, odd, m, pm)
+
+
+def build_kernel(parts, order, slot_ref, t_ref, *rest):
     piece_refs, (out_ref, table) = rest[:-2], rest[-2:]
     aux = lax.axis_index("aux")
     blocks, listed, width, _ = t_ref.shape
     owned = piece_refs[0].shape[0]
     rows = width // parts
-    for k, piece in enumerate(piece_refs):
+    for k, piece in zip(order, piece_refs):
         table[k * owned : (k + 1) * owned] = piece[...]
     for p in range(blocks):
         left = [t_ref[p, k] for k in range(listed)]
@@ -148,11 +148,11 @@
             out_ref[lax.rem(part + parts - aux, parts), p] = total[part * rows : (part + 1) * rows]
 
 
-def build(slots, three_centre, pieces, parts, name):
+def build(slots, three_centre, pieces, order, parts, name):
     blocks, listed, width, _ = three_centre.shape
     owned, half, _ = pieces[0].shape
     return pl.pallas_call(
-        functools.partial(build_kernel, parts),
+        functools.partial(build_kernel, parts, order),
         in_specs=[SMEM] + [VMEM] * (1 + len(pieces)),
         out_specs=VMEM,
         out_shape=jax.ShapeDtypeStruct((parts, blocks, width // parts, half), BF16),
@@ -214,18 +214,19 @@
     near = jnp.concatenate(
         [fitted] + [ahead_by(fitted, "aux", aux_count - k) for k in range(1, aux_count)]
     )
+    even = pairs_from(near, "space", 0)
     odd = pairs_from(near, "space", 1)
-    even = pairs_from(near, "space", 0)
     coefficients = metric(
-        metric_columns, peer_columns, near, odd, even, metric_inverse, peer_metric, aux_count
-    )
-
-    pieces = [coefficients] + [exchange(coefficients, "space", k) for k in range(1, domains)]
+        metric_columns, peer_columns, near, even, odd, metric_inverse, peer_metric, aux_count
+    )
+
+    order = [0] + list(range(domains - 1, 0, -1))
+    pieces = [coefficients] + [exchange(coefficients, "space", k) for k in order[1:]]
     other = [exchange(piece, "sub", 1) for piece in pieces]
 
     sums = []
     for name, tiles in (("build_own", pieces), ("build_other", other)):
-        parts = build(slots, three_centre, tiles, aux_count, name)
+        parts = build(slots, three_centre, tiles, order, aux_count, name)
         terms = [parts[0]] + [ahead_by(parts[k], "aux", k) for k in range(1, aux_count)]
         sums.append(sum(term.astype(F32) for term in terms).astype(BF16))
     first = lax.axis_index("sub") == 0

time: 57.9 us -> 56.2 us (0.971)
  starting transfers between devices: 20.5 us -> 19.4 us
  waiting for transfers between devices: 25.8 us -> 25.2 us
    ppermute x2, starting transfers between devices: 5.43 us -> 2.58 us  [pairs_from(): return lax.ppermute(array, axis, swaps)]
    ppermute x13, starting transfers between devices: 11.4 us -> 13.1 us  [exchange(): lax.ppermute(array, axis, [(i, i ^ distance) for i in range(lax.axis_size...]
  transfers between devices with their start and end apart: 18 -> 18, of which waited for: 9 -> 10; matrix products, arithmetic and copies ran while one was open for 0% -> 0% of each run, Pallas kernels for 6% -> 6%
where the time goes in v4:
time: 56.2 us; the launch traced here: 56.1 us
  waiting for transfers between devices  25.2 us (45%)
  starting transfers between devices  19.4 us (35%)
  Pallas kernels  9.5 us (17%)
  other arithmetic  1.77 us (3%)
    ppermute x13, waiting for transfers between devices, exchange(): lax.ppermute(array, axis, [(i, i ^ distance) for i in range(lax.axis_size...  13.9 us
    ppermute x13, starting transfers between devices, exchange(): lax.ppermute(array, axis, [(i, i ^ distance) for i in range(lax.axis_size...  13.1 us
    ppermute x3, waiting for transfers between devices, ahead_by(): lax.ppermute(array, axis, [(i, (i + distance) % count) for i in range(cou...  8.22 us
    pallas_call x1, Pallas kernels, fit(): pl.pallas_call(functools.partial(fit_kernel, owned, half, groups), in_spe...  5 us
    ppermute x3, starting transfers between devices, ahead_by(): lax.ppermute(array, axis, [(i, (i + distance) % count) for i in range(cou...  3.68 us
    pallas_call x2, Pallas kernels, build(): pl.pallas_call(functools.partial(build_kernel, parts, order), in_specs=[S...  3.28 us
    ppermute x2, waiting for transfers between devices, pairs_from(): return lax.ppermute(array, axis, swaps)  3.15 us
    ppermute x2, starting transfers between devices, pairs_from(): return lax.ppermute(array, axis, swaps)  2.58 us
  transfers between devices with their start and end apart: 18, of which 10 were waited for; matrix products, arithmetic and copies ran while one was open for 0% of the time, Pallas kernels for 6%

profile of v4, /device:TPU:0, one launch (start us, length us, event | category | flops | bytes accessed | tf_op | source)
XLA Modules:
  0.0 56.1 jit_solution(12577937257683083338)
XLA Ops:
  0.0 0.8 %fusion.5.table_ref = s32[10,32]{1,0:T(8,128)S(1)} fusion(s32[8,12]{1,0:T(8,128)} %param.9, s32[1,32]{1,0:T(1,128)} %bitcast.36, s32[1,32]{1,0:T(1,128)} %bitcast.37), kind=kLoop, calls=%fused_computation.21 | loop fusion | flops 640 | bytes 1920 | tf_op jit(solution)/shard_map/concatenate | solution.py:198
  0.8 5.0 %fit.1 = (bf16[12,128,128]{2,1,0:T(8,128)(2,1)S(1)}, bf16[12,128,128]{2,1,0:T(8,128)(2,1)S(1)}, s32[8,12]{1,0:T(8,128)S(1)}) custom-call(s32[10,32]{1,0:T(8,128)S(1)} %fusion.5.table_ref, bf16[8,128,256]{2,1,0:T(8,128)(2,1)} %d_hbm.1, bf16[8,12,128,128]{3,2,1,0:T(8,128)(2,1)} %t_ref.3), custom_call_target="tpu_custom_call" | custom-call | flops 805306368 | bytes 3670016 | tf_op jit(solution)/shard_map/fit/pallas_call | solution.py:62
  6.3 1.3 %collective-permute-done = bf16[12,128,128]{2,1,0:T(8,128)(2,1)S(1)} collective-permute-done((bf16[12,128,128]{2,1,0:T(8,128)(2,1)S(1)}, bf16[12,128,128]{2,1,0:T(8,128)(2,1)S(1)}, u32[]{:S(2)}, u32[]{:S(2)}) %collective-permute-start) | collective-permute-done | bytes 393248 | tf_op jit(solution)/shard_map/ppermute | solution.py:171
  8.2 2.8 %collective-permute-start.1 = (bf16[3,128,128]{2,1,0:T(8,128)(2,1)S(1)}, bf16[3,128,128]{2,1,0:T(8,128)(2,1)S(1)}, u32[]{:S(2)}, u32[]{:S(2)}) collective-permute-start(bf16[3,128,128]{2,1,0:T(8,128)(2,1)S(1)} %get-tuple-element.31), channel_id=1, source_target_pairs={{0,4},{4,0},{8,12},{12,8},{1,5},{5,1},{9,13},{13,9},{2,6},{6,2},{1... | collective-permute-start | bytes 294920 | tf_op jit(solution)/shard_map/ppermute | solution.py:171
  11.0 2.6 %collective-permute-start.2 = (bf16[3,128,128]{2,1,0:T(8,128)(2,1)S(1)}, bf16[3,128,128]{2,1,0:T(8,128)(2,1)S(1)}, u32[]{:S(2)}, u32[]{:S(2)}) collective-permute-start(bf16[3,128,128]{2,1,0:T(8,128)(2,1)S(1)} %get-tuple-element.30), channel_id=1, source_target_pairs={{0,8},{4,12},{8,0},{12,4},{1,9},{5,13},{9,1},{13,5},{2,10},{6,14},... | collective-permute-start | bytes 294920 | tf_op jit(solution)/shard_map/ppermute | solution.py:171
  13.6 1.2 %collective-permute-done.5.peer_cols = s32[3,4]{1,0:T(4,128)S(1)} collective-permute-done((s32[3,4]{1,0:T(4,128)S(1)}, s32[3,4]{1,0:T(4,128)S(1)}, u32[]{:S(2)}, u32[]{:S(2)}) %collective-permute-start.5) | collective-permute-done | bytes 80 | tf_op jit(solution)/shard_map/ppermute | solution.py:171
  14.8 7.0 %collective-permute-done.2 = bf16[3,128,128]{2,1,0:T(8,128)(2,1)S(1)} collective-permute-done((bf16[3,128,128]{2,1,0:T(8,128)(2,1)S(1)}, bf16[3,128,128]{2,1,0:T(8,128)(2,1)S(1)}, u32[]{:S(2)}, u32[]{:S(2)}) %collective-permute-start.2) | collective-permute-done | bytes 98336 | tf_op jit(solution)/shard_map/ppermute | solution.py:171
  21.8 1.5 %collective-permute-start.6 = (bf16[3,128,128]{2,1,0:T(8,128)(2,1)S(1)}, bf16[3,128,128]{2,1,0:T(8,128)(2,1)S(1)}, u32[]{:S(2)}, u32[]{:S(2)}) collective-permute-start(bf16[3,128,128]{2,1,0:T(8,128)(2,1)S(1)} %fusion.4), channel_id=1, source_target_pairs={{0,2},{2,0},{1,3},{3,1},{4,6},{6,4},{5,7},{7,5},{8,10},{10,8},{9,1... | collective-permute-start | bytes 294920 | tf_op jit(solution)/shard_map/ppermute | solution.py:176
  23.3 3.2 %collective-permute-done.6 = bf16[3,128,128]{2,1,0:T(8,128)(2,1)S(1)} collective-permute-done((bf16[3,128,128]{2,1,0:T(8,128)(2,1)S(1)}, bf16[3,128,128]{2,1,0:T(8,128)(2,1)S(1)}, u32[]{:S(2)}, u32[]{:S(2)}) %collective-permute-start.6) | collective-permute-done | bytes 98336 | tf_op jit(solution)/shard_map/ppermute | solution.py:176
  26.5 1.9 %collective-permute-start.7 = (bf16[6,128,128]{2,1,0:T(8,128)(2,1)S(1)}, bf16[6,128,128]{2,1,0:T(8,128)(2,1)S(1)}, u32[]{:S(2)}, u32[]{:S(2)}) collective-permute-start(bf16[6,128,128]{2,1,0:T(8,128)(2,1)S(1)} %pad_maximum_fusion.1.near_ref), channel_id=1, source_target_pairs={{0,4},{4,0},{8,12},{12,8},{1,5},{5,1},{9,13},{13,9},{2,6},{6,2},{1... | collective-permute-start | bytes 589832 | tf_op jit(solution)/shard_map/ppermute | solution.py:183
  28.4 0.7 %collective-permute-start.8 = (bf16[6,128,128]{2,1,0:T(8,128)(2,1)S(1)}, bf16[6,128,128]{2,1,0:T(8,128)(2,1)S(1)}, u32[]{:S(2)}, u32[]{:S(2)}) collective-permute-start(bf16[6,128,128]{2,1,0:T(8,128)(2,1)S(1)} %pad_maximum_fusion.1.near_ref), channel_id=1, source_target_pairs={{4,8},{8,4},{5,9},{9,5},{6,10},{10,6},{7,11},{11,7},{20,24},{24,20... | collective-permute-start | bytes 589832 | tf_op jit(solution)/shard_map/ppermute | solution.py:183
  29.1 3.2 %collective-permute-done.7.even_ref = bf16[6,128,128]{2,1,0:T(8,128)(2,1)S(1)} collective-permute-done((bf16[6,128,128]{2,1,0:T(8,128)(2,1)S(1)}, bf16[6,128,128]{2,1,0:T(8,128)(2,1)S(1)}, u32[]{:S(2)}, u32[]{:S(2)}) %collective-permute-start.7) | collective-permute-done | bytes 196640 | tf_op jit(solution)/shard_map/ppermute | solution.py:183
  32.3 1.2 %metric.1.rest_0_ = bf16[3,128,128]{2,1,0:T(8,128)(2,1)S(1)} custom-call(s32[3,4]{1,0:T(4,128)S(1)} %copy-done.2, s32[3,4]{1,0:T(4,128)S(1)} %collective-permute-done.5.peer_cols, bf16[6,128,128]{2,1,0:T(8,128)(2,1)S(1)} %pad_maximum_fusion.1.near_ref, bf16[6,128,128]{2,1,0:T(8,128)(2,1)S(1)} %collective-permute-done.7.even_ref, ...), custom_call_target="tpu_custom_call" | custom-call | flops 100663296 | bytes 1376256 | tf_op jit(solution)/shard_map/metric/pallas_call | solution.py:117
  33.5 2.6 %collective-permute-start.9 = (bf16[3,128,128]{2,1,0:T(8,128)(2,1)S(1)}, bf16[3,128,128]{2,1,0:T(8,128)(2,1)S(1)}, u32[]{:S(2)}, u32[]{:S(2)}) collective-permute-start(bf16[3,128,128]{2,1,0:T(8,128)(2,1)S(1)} %metric.1.rest_0_), channel_id=1, source_target_pairs={{0,12},{4,8},{8,4},{12,0},{1,13},{5,9},{9,5},{13,1},{2,14},{6,10},... | collective-permute-start | bytes 294920 | tf_op jit(solution)/shard_map/ppermute | solution.py:171
  36.1 3.9 %collective-permute-start.10 = (bf16[3,128,128]{2,1,0:T(8,128)(2,1)S(1)}, bf16[3,128,128]{2,1,0:T(8,128)(2,1)S(1)}, u32[]{:S(2)}, u32[]{:S(2)}) collective-permute-start(bf16[3,128,128]{2,1,0:T(8,128)(2,1)S(1)} %metric.1.rest_0_), channel_id=1, source_target_pairs={{0,8},{4,12},{8,0},{12,4},{1,9},{5,13},{9,1},{13,5},{2,10},{6,14},... | collective-permute-start | bytes 294920 | tf_op jit(solution)/shard_map/ppermute | solution.py:171
  40.3 0.7 %collective-permute-done.9.rest_1_ = bf16[3,128,128]{2,1,0:T(8,128)(2,1)S(1)} collective-permute-done((bf16[3,128,128]{2,1,0:T(8,128)(2,1)S(1)}, bf16[3,128,128]{2,1,0:T(8,128)(2,1)S(1)}, u32[]{:S(2)}, u32[]{:S(2)}) %collective-permute-start.9) | collective-permute-done | bytes 98336 | tf_op jit(solution)/shard_map/ppermute | solution.py:171
  41.0 2.6 %collective-permute-done.10.rest_2_ = bf16[3,128,128]{2,1,0:T(8,128)(2,1)S(1)} collective-permute-done((bf16[3,128,128]{2,1,0:T(8,128)(2,1)S(1)}, bf16[3,128,128]{2,1,0:T(8,128)(2,1)S(1)}, u32[]{:S(2)}, u32[]{:S(2)}) %collective-permute-start.10) | collective-permute-done | bytes 98336 | tf_op jit(solution)/shard_map/ppermute | solution.py:171
  43.6 1.0 %collective-permute-done.11.rest_3_ = bf16[3,128,128]{2,1,0:T(8,128)(2,1)S(1)} collective-permute-done((bf16[3,128,128]{2,1,0:T(8,128)(2,1)S(1)}, bf16[3,128,128]{2,1,0:T(8,128)(2,1)S(1)}, u32[]{:S(2)}, u32[]{:S(2)}) %collective-permute-start.11) | collective-permute-done | bytes 98336 | tf_op jit(solution)/shard_map/ppermute | solution.py:171
  44.7 1.6 %build_own.1 = bf16[2,8,64,128]{3,2,1,0:T(8,128)(2,1)S(1)} custom-call(s32[8,12]{1,0:T(8,128)S(1)} %get-tuple-element.16.slot_ref, bf16[8,12,128,128]{3,2,1,0:T(8,128)(2,1)S(1)} %copy-done, bf16[3,128,128]{2,1,0:T(8,128)(2,1)S(1)} %metric.1.rest_0_, bf16[3,128,128]{2,1,0:T(8,128)(2,1)S(1)} %collective-permute-done.9.rest_1_, ...), custom_call_target="tpu_custom_call" | custom-call | flops 402653184 | bytes 3407872 | tf_op jit(solution)/shard_map/build_own/pallas_call | solution.py:154
  46.3 1.5 %collective-permute-start.12 = (bf16[8,64,128]{2,1,0:T(8,128)(2,1)S(1)}, bf16[8,64,128]{2,1,0:T(8,128)(2,1)S(1)}, u32[]{:S(2)}, u32[]{:S(2)}) collective-permute-start(bf16[8,64,128]{2,1,0:T(8,128)(2,1)S(1)} %slice_bitcast_fusion.2), channel_id=1, source_target_pairs={{0,2},{2,0},{1,3},{3,1},{4,6},{6,4},{5,7},{7,5},{8,10},{10,8},{9,1... | collective-permute-start | bytes 393224 | tf_op jit(solution)/shard_map/ppermute | solution.py:176
  47.9 1.6 %build_other.1 = bf16[2,8,64,128]{3,2,1,0:T(8,128)(2,1)S(1)} custom-call(s32[8,12]{1,0:T(8,128)S(1)} %get-tuple-element.16.slot_ref, bf16[8,12,128,128]{3,2,1,0:T(8,128)(2,1)S(1)} %copy-done, bf16[3,128,128]{2,1,0:T(8,128)(2,1)S(1)} %collective-permute-done.13.rest_0_, bf16[3,128,128]{2,1,0:T(8,128)(2,1)S(1)} %collective-permute-done.14.rest_1_, ...), custom_call_target="tpu_custom_call" | custom-call | flops 402653184 | bytes 3407872 | tf_op jit(solution)/shard_map/build_other/pallas_call | solution.py:154
  50.2 2.1 %collective-permute-done.12 = bf16[8,64,128]{2,1,0:T(8,128)(2,1)S(1)} collective-permute-done((bf16[8,64,128]{2,1,0:T(8,128)(2,1)S(1)}, bf16[8,64,128]{2,1,0:T(8,128)(2,1)S(1)}, u32[]{:S(2)}, u32[]{:S(2)}) %collective-permute-start.12) | collective-permute-done | bytes 131104 | tf_op jit(solution)/shard_map/ppermute | solution.py:176
  52.3 2.9 %collective-permute-done.17 = bf16[8,64,128]{2,1,0:T(8,128)(2,1)S(1)} collective-permute-done((bf16[8,64,128]{2,1,0:T(8,128)(2,1)S(1)}, bf16[8,64,128]{2,1,0:T(8,128)(2,1)S(1)}, u32[]{:S(2)}, u32[]{:S(2)}) %collective-permute-start.17) | collective-permute-done | bytes 131104 | tf_op jit(solution)/shard_map/ppermute | solution.py:176
  55.3 0.7 %pad_maximum_fusion = bf16[8,64,256]{2,1,0:T(8,128)(2,1)} fusion(bf16[8,64,128]{2,1,0:T(8,128)(2,1)S(1)} %get-tuple-element.28, bf16[8,64,128]{2,1,0:T(8,128)(2,1)S(1)} %get-tuple-element.27), kind=kLoop, calls=%fused_computation.1 | loop fusion | flops 524288 | bytes 524288 | tf_op jit(solution)/shard_map/concatenate | solution.py:234
  (31 shorter events, 2.2 us)
Async XLA Ops:
  0.0 7.8 %copy-start.1 = (bf16[3,4,128,128]{3,2,1,0:T(8,128)(2,1)S(1)}, bf16[3,4,128,128]{3,2,1,0:T(8,128)(2,1)}, u32[]{:S(2)}) copy-start(bf16[3,4,128,128]{3,2,1,0:T(8,128)(2,1)} %m_ref.1) | copy-start | bytes 1179652
  0.0 13.6 %copy-start.2 = (s32[3,4]{1,0:T(4,128)S(1)}, s32[3,4]{1,0:T(4,128)}, u32[]{:S(2)}) copy-start(s32[3,4]{1,0:T(4,128)} %mine_cols.1) | copy-start | bytes 148
  0.8 43.9 %copy-start = (bf16[8,12,128,128]{3,2,1,0:T(8,128)(2,1)S(1)}, bf16[8,12,128,128]{3,2,1,0:T(8,128)(2,1)}, u32[]{:S(2)}) copy-start(bf16[8,12,128,128]{3,2,1,0:T(8,128)(2,1)} %t_ref.3) | copy-start | bytes 9437188
  5.8 1.9 %collective-permute-start = (bf16[12,128,128]{2,1,0:T(8,128)(2,1)S(1)}, bf16[12,128,128]{2,1,0:T(8,128)(2,1)S(1)}, u32[]{:S(2)}, u32[]{:S(2)}) collective-permute-start(bf16[12,128,128]{2,1,0:T(8,128)(2,1)S(1)} %get-tuple-element.18), channel_id=1, source_target_pairs={{0,1},{1,0},{2,3},{3,2},{4,5},{5,4},{6,7},{7,6},{8,9},{9,8},{10,11... | collective-permute-start | bytes 1179656 | tf_op jit(solution)/shard_map/ppermute | solution.py:171
  7.8 14.0 %collective-permute-start.4 = (bf16[3,4,128,128]{3,2,1,0:T(8,128)(2,1)S(1)}, bf16[3,4,128,128]{3,2,1,0:T(8,128)(2,1)S(1)}, u32[]{:S(2)}, u32[]{:S(2)}) collective-permute-start(bf16[3,4,128,128]{3,2,1,0:T(8,128)(2,1)S(1)} %copy-done.1), channel_id=1, source_target_pairs={{0,1},{1,0},{2,3},{3,2},{4,5},{5,4},{6,7},{7,6},{8,9},{9,8},{10,11... | collective-permute-start | bytes 1179656 | tf_op jit(solution)/shard_map/ppermute | solution.py:171
  8.2 6.5 %collective-permute-start.1 = (bf16[3,128,128]{2,1,0:T(8,128)(2,1)S(1)}, bf16[3,128,128]{2,1,0:T(8,128)(2,1)S(1)}, u32[]{:S(2)}, u32[]{:S(2)}) collective-permute-start(bf16[3,128,128]{2,1,0:T(8,128)(2,1)S(1)} %get-tuple-element.31), channel_id=1, source_target_pairs={{0,4},{4,0},{8,12},{12,8},{1,5},{5,1},{9,13},{13,9},{2,6},{6,2},{1... | collective-permute-start | bytes 294920 | tf_op jit(solution)/shard_map/ppermute | solution.py:171
  11.0 10.7 %collective-permute-start.2 = (bf16[3,128,128]{2,1,0:T(8,128)(2,1)S(1)}, bf16[3,128,128]{2,1,0:T(8,128)(2,1)S(1)}, u32[]{:S(2)}, u32[]{:S(2)}) collective-permute-start(bf16[3,128,128]{2,1,0:T(8,128)(2,1)S(1)} %get-tuple-element.30), channel_id=1, source_target_pairs={{0,8},{4,12},{8,0},{12,4},{1,9},{5,13},{9,1},{13,5},{2,10},{6,14},... | collective-permute-start | bytes 294920 | tf_op jit(solution)/shard_map/ppermute | solution.py:171
  13.6 8.1 %collective-permute-start.3 = (bf16[3,128,128]{2,1,0:T(8,128)(2,1)S(1)}, bf16[3,128,128]{2,1,0:T(8,128)(2,1)S(1)}, u32[]{:S(2)}, u32[]{:S(2)}) collective-permute-start(bf16[3,128,128]{2,1,0:T(8,128)(2,1)S(1)} %get-tuple-element.29), channel_id=1, source_target_pairs={{0,12},{4,8},{8,4},{12,0},{1,13},{5,9},{9,5},{13,1},{2,14},{6,10},... | collective-permute-start | bytes 294920 | tf_op jit(solution)/shard_map/ppermute | solution.py:171
  13.6 1.2 %collective-permute-start.5 = (s32[3,4]{1,0:T(4,128)S(1)}, s32[3,4]{1,0:T(4,128)S(1)}, u32[]{:S(2)}, u32[]{:S(2)}) collective-permute-start(s32[3,4]{1,0:T(4,128)S(1)} %copy-done.2), channel_id=1, source_target_pairs={{0,1},{1,0},{2,3},{3,2},{4,5},{5,4},{6,7},{7,6},{8,9},{9,8},{10,11... | collective-permute-start | bytes 152 | tf_op jit(solution)/shard_map/ppermute | solution.py:171
  21.8 4.7 %collective-permute-start.6 = (bf16[3,128,128]{2,1,0:T(8,128)(2,1)S(1)}, bf16[3,128,128]{2,1,0:T(8,128)(2,1)S(1)}, u32[]{:S(2)}, u32[]{:S(2)}) collective-permute-start(bf16[3,128,128]{2,1,0:T(8,128)(2,1)S(1)} %fusion.4), channel_id=1, source_target_pairs={{0,2},{2,0},{1,3},{3,1},{4,6},{6,4},{5,7},{7,5},{8,10},{10,8},{9,1... | collective-permute-start | bytes 294920 | tf_op jit(solution)/shard_map/ppermute | solution.py:176
  26.5 5.7 %collective-permute-start.7 = (bf16[6,128,128]{2,1,0:T(8,128)(2,1)S(1)}, bf16[6,128,128]{2,1,0:T(8,128)(2,1)S(1)}, u32[]{:S(2)}, u32[]{:S(2)}) collective-permute-start(bf16[6,128,128]{2,1,0:T(8,128)(2,1)S(1)} %pad_maximum_fusion.1.near_ref), channel_id=1, source_target_pairs={{0,4},{4,0},{8,12},{12,8},{1,5},{5,1},{9,13},{13,9},{2,6},{6,2},{1... | collective-permute-start | bytes 589832 | tf_op jit(solution)/shard_map/ppermute | solution.py:183
  28.4 3.8 %collective-permute-start.8 = (bf16[6,128,128]{2,1,0:T(8,128)(2,1)S(1)}, bf16[6,128,128]{2,1,0:T(8,128)(2,1)S(1)}, u32[]{:S(2)}, u32[]{:S(2)}) collective-permute-start(bf16[6,128,128]{2,1,0:T(8,128)(2,1)S(1)} %pad_maximum_fusion.1.near_ref), channel_id=1, source_target_pairs={{4,8},{8,4},{5,9},{9,5},{6,10},{10,6},{7,11},{11,7},{20,24},{24,20... | collective-permute-start | bytes 589832 | tf_op jit(solution)/shard_map/ppermute | solution.py:183
  33.5 7.5 %collective-permute-start.9 = (bf16[3,128,128]{2,1,0:T(8,128)(2,1)S(1)}, bf16[3,128,128]{2,1,0:T(8,128)(2,1)S(1)}, u32[]{:S(2)}, u32[]{:S(2)}) collective-permute-start(bf16[3,128,128]{2,1,0:T(8,128)(2,1)S(1)} %metric.1.rest_0_), channel_id=1, source_target_pairs={{0,12},{4,8},{8,4},{12,0},{1,13},{5,9},{9,5},{13,1},{2,14},{6,10},... | collective-permute-start | bytes 294920 | tf_op jit(solution)/shard_map/ppermute | solution.py:171
  36.1 7.5 %collective-permute-start.10 = (bf16[3,128,128]{2,1,0:T(8,128)(2,1)S(1)}, bf16[3,128,128]{2,1,0:T(8,128)(2,1)S(1)}, u32[]{:S(2)}, u32[]{:S(2)}) collective-permute-start(bf16[3,128,128]{2,1,0:T(8,128)(2,1)S(1)} %metric.1.rest_0_), channel_id=1, source_target_pairs={{0,8},{4,12},{8,0},{12,4},{1,9},{5,13},{9,1},{13,5},{2,10},{6,14},... | collective-permute-start | bytes 294920 | tf_op jit(solution)/shard_map/ppermute | solution.py:171
  40.0 4.7 %collective-permute-start.11 = (bf16[3,128,128]{2,1,0:T(8,128)(2,1)S(1)}, bf16[3,128,128]{2,1,0:T(8,128)(2,1)S(1)}, u32[]{:S(2)}, u32[]{:S(2)}) collective-permute-start(bf16[3,128,128]{2,1,0:T(8,128)(2,1)S(1)} %metric.1.rest_0_), channel_id=1, source_target_pairs={{0,4},{4,0},{8,12},{12,8},{1,5},{5,1},{9,13},{13,9},{2,6},{6,2},{1... | collective-permute-start | bytes 294920 | tf_op jit(solution)/shard_map/ppermute | solution.py:171
  40.3 7.6 %collective-permute-start.13 = (bf16[3,128,128]{2,1,0:T(8,128)(2,1)S(1)}, bf16[3,128,128]{2,1,0:T(8,128)(2,1)S(1)}, u32[]{:S(2)}, u32[]{:S(2)}) collective-permute-start(bf16[3,128,128]{2,1,0:T(8,128)(2,1)S(1)} %metric.1.rest_0_), channel_id=1, source_target_pairs={{0,1},{1,0},{2,3},{3,2},{4,5},{5,4},{6,7},{7,6},{8,9},{9,8},{10,11... | collective-permute-start | bytes 294920 | tf_op jit(solution)/shard_map/ppermute | solution.py:171
  41.0 6.9 %collective-permute-start.14 = (bf16[3,128,128]{2,1,0:T(8,128)(2,1)S(1)}, bf16[3,128,128]{2,1,0:T(8,128)(2,1)S(1)}, u32[]{:S(2)}, u32[]{:S(2)}) collective-permute-start(bf16[3,128,128]{2,1,0:T(8,128)(2,1)S(1)} %collective-permute-done.9.rest_1_), channel_id=1, source_target_pairs={{0,1},{1,0},{2,3},{3,2},{4,5},{5,4},{6,7},{7,6},{8,9},{9,8},{10,11... | collective-permute-start | bytes 294920 | tf_op jit(solution)/shard_map/ppermute | solution.py:171
  43.6 4.3 %collective-permute-start.15 = (bf16[3,128,128]{2,1,0:T(8,128)(2,1)S(1)}, bf16[3,128,128]{2,1,0:T(8,128)(2,1)S(1)}, u32[]{:S(2)}, u32[]{:S(2)}) collective-permute-start(bf16[3,128,128]{2,1,0:T(8,128)(2,1)S(1)} %collective-permute-done.10.rest_2_), channel_id=1, source_target_pairs={{0,1},{1,0},{2,3},{3,2},{4,5},{5,4},{6,7},{7,6},{8,9},{9,8},{10,11... | collective-permute-start | bytes 294920 | tf_op jit(solution)/shard_map/ppermute | solution.py:171
  44.7 3.2 %collective-permute-start.16 = (bf16[3,128,128]{2,1,0:T(8,128)(2,1)S(1)}, bf16[3,128,128]{2,1,0:T(8,128)(2,1)S(1)}, u32[]{:S(2)}, u32[]{:S(2)}) collective-permute-start(bf16[3,128,128]{2,1,0:T(8,128)(2,1)S(1)} %collective-permute-done.11.rest_3_), channel_id=1, source_target_pairs={{0,1},{1,0},{2,3},{3,2},{4,5},{5,4},{6,7},{7,6},{8,9},{9,8},{10,11... | collective-permute-start | bytes 294920 | tf_op jit(solution)/shard_map/ppermute | solution.py:171
  46.3 6.0 %collective-permute-start.12 = (bf16[8,64,128]{2,1,0:T(8,128)(2,1)S(1)}, bf16[8,64,128]{2,1,0:T(8,128)(2,1)S(1)}, u32[]{:S(2)}, u32[]{:S(2)}) collective-permute-start(bf16[8,64,128]{2,1,0:T(8,128)(2,1)S(1)} %slice_bitcast_fusion.2), channel_id=1, source_target_pairs={{0,2},{2,0},{1,3},{3,1},{4,6},{6,4},{5,7},{7,5},{8,10},{10,8},{9,1... | collective-permute-start | bytes 393224 | tf_op jit(solution)/shard_map/ppermute | solution.py:176
  49.5 5.7 %collective-permute-start.17 = (bf16[8,64,128]{2,1,0:T(8,128)(2,1)S(1)}, bf16[8,64,128]{2,1,0:T(8,128)(2,1)S(1)}, u32[]{:S(2)}, u32[]{:S(2)}) collective-permute-start(bf16[8,64,128]{2,1,0:T(8,128)(2,1)S(1)} %slice_bitcast_fusion), channel_id=1, source_target_pairs={{0,2},{2,0},{1,3},{3,1},{4,6},{6,4},{5,7},{7,5},{8,10},{10,8},{9,1... | collective-permute-start | bytes 393224 | tf_op jit(solution)/shard_map/ppermute | solution.py:176

commit v5 on v4

--- a/solution.py
+++ b/solution.py
@@ -11,17 +11,25 @@
 F32 = jnp.float32
 NT = (((1,), (1,)), ((), ()))
 VMEM_LIMIT = 32 * 1024 * 1024
-FIT_VMEM_LIMIT = 53 * 1024 * 1024
 VMEM = pl.BlockSpec(memory_space=pltpu.VMEM)
 SMEM = pl.BlockSpec(memory_space=pltpu.SMEM)
+ANY = pl.BlockSpec(memory_space=pl.ANY)
 
 
 def fit_kernel(
-    owned, half, groups, table_ref, d_hbm, t_hbm, keep_ref, send_ref, slot_ref, acc, d_ref, t_ref, d_sem, t_sem
+    owned, half, groups, tile_hbm, domain_hbm, number_hbm, d_hbm, t_hbm, keep_ref, send_ref, slot_any,
+    acc, tile_ref, domain_ref, number_ref, slot_ref, d_ref, t_ref, small_sem, d_sem, t_sem,
 ):
     me = lax.axis_index("space")
     mine = lax.axis_index("sub")
     blocks, listed = t_ref.shape[:2]
+    small = [
+        pltpu.make_async_copy(tile_hbm, tile_ref, small_sem.at[0]),
+        pltpu.make_async_copy(domain_hbm, domain_ref, small_sem.at[1]),
+        pltpu.make_async_copy(number_hbm, number_ref, small_sem.at[2]),
+    ]
+    for copy in small:
+        copy.start()
     copies, begin = [], 0
     for i, size in enumerate(groups):
         part = pl.ds(begin, size)
@@ -36,6 +44,8 @@
         for copy in pair:
             copy.start()
     acc[...] = jnp.zeros_like(acc)
+    for copy in small:
+        copy.wait()
     begin = 0
     for size, pair in zip(groups, copies):
         for copy in pair:
@@ -43,42 +53,52 @@
         for p in range(begin, begin + size):
             rows = jnp.transpose(d_ref[p])
             for k in range(listed):
-                touched = table_ref[p, k]
-                slot = jnp.bitwise_xor(table_ref[blocks, touched], me) * owned + table_ref[blocks + 1, touched]
+                touched = tile_ref[p, k]
+                slot = jnp.bitwise_xor(domain_ref[touched], me) * owned + number_ref[touched]
                 slot_ref[p, k] = slot
                 acc[slot] += jnp.dot(rows, t_ref[p, k], preferred_element_type=F32)
         begin += size
+    slot_copy = pltpu.make_async_copy(slot_ref, slot_any, small_sem.at[3])
+    slot_copy.start()
     keep_ref[...] = acc[:, pl.ds(pl.multiple_of(mine * half, half), half), :].astype(BF16)
     send_ref[...] = acc[:, pl.ds(pl.multiple_of((1 - mine) * half, half), half), :].astype(BF16)
-
-
-def fit(tables, densities, three_centre, domains, owned):
+    slot_copy.wait()
+
+
+def fit(block_tile, domain, number, densities, three_centre, domains, owned):
     blocks, listed, width, _ = three_centre.shape
     columns = densities.shape[2]
     half = columns // 2
     count = domains * owned
-    groups = (blocks // 4, blocks // 4, blocks - 2 * (blocks // 4))
+    groups = (blocks // 4, 3 * blocks // 8, blocks - blocks // 4 - 3 * blocks // 8)
     out = jax.ShapeDtypeStruct((count, half, width), BF16)
+    operands = (block_tile, domain, number, densities, three_centre)
+    operands = [pltpu.with_memory_space_constraint(operand, pltpu.HBM) for operand in operands]
     return pl.pallas_call(
         functools.partial(fit_kernel, owned, half, groups),
-        in_specs=[SMEM] + [pl.BlockSpec(memory_space=pltpu.HBM)] * 2,
-        out_specs=[VMEM, VMEM, SMEM],
+        in_specs=[pl.BlockSpec(memory_space=pltpu.HBM)] * 5,
+        out_specs=[VMEM, VMEM, ANY],
         scratch_shapes=[
             pltpu.VMEM((count, columns, width), F32),
+            pltpu.SMEM(block_tile.shape, jnp.int32),
+            pltpu.SMEM(domain.shape, jnp.int32),
+            pltpu.SMEM(number.shape, jnp.int32),
+            pltpu.SMEM(block_tile.shape, jnp.int32),
             pltpu.VMEM(densities.shape, BF16),
             pltpu.VMEM(three_centre.shape, BF16),
+            pltpu.SemaphoreType.DMA((4,)),
             pltpu.SemaphoreType.DMA((len(groups),)),
             pltpu.SemaphoreType.DMA((len(groups),)),
         ],
-        out_shape=[out, out, jax.ShapeDtypeStruct((blocks, listed), jnp.int32)],
-        compiler_params=pltpu.CompilerParams(vmem_limit_bytes=FIT_VMEM_LIMIT),
+        out_shape=[out, out, jax.ShapeDtypeStruct(block_tile.shape, jnp.int32)],
+        compiler_params=pltpu.CompilerParams(vmem_limit_bytes=VMEM_LIMIT),
         cost_estimate=pl.CostEstimate(
             flops=2 * blocks * listed * width * width * columns,
             bytes_accessed=2 * (three_centre.size + densities.size),
             transcendentals=0,
         ),
         name="fit",
-    )(tables, densities, three_centre)
+    )(*operands)
 
 
 def metric_kernel(owned, count, mine_cols, peer_cols, near_ref, even_ref, odd_ref, m_ref, pm_ref, out_ref, window):
@@ -194,11 +214,7 @@
     domain = owner_domain.reshape(touched)
     number = owner_tile.reshape(touched)
 
-    wide = max(touched, block_tile.shape[1])
-    tables = jnp.concatenate(
-        [jnp.pad(row, ((0, 0), (0, wide - row.shape[1]))) for row in (block_tile, domain[None], number[None])]
-    )
-    keep, send, slots = fit(tables, densities, three_centre, domains, owned)
+    keep, send, slots = fit(block_tile, domain, number, densities, three_centre, domains, owned)
     got = exchange(send, "sub", 1)
     chip = (keep.astype(F32) + got.astype(F32)).astype(BF16).reshape(domains, owned, half, width)
     chip, own_metric, own_columns = lax.optimization_barrier((chip, metric_inverse, metric_columns))

time: 56.2 us -> 54.6 us (0.972)
  Pallas kernels: 9.5 us -> 8.65 us
  other arithmetic: 1.77 us -> 1.01 us
    pallas_call x1, Pallas kernels: 5 us -> 4.21 us  [fit(): pl.pallas_call(functools.partial(fit_kernel, owned, half, groups), in_spe...]
    concatenate x1 -> x0, other arithmetic: 0.76 us -> none  [shards(): jnp.concatenate([jnp.pad(row, ((0, 0), (0, wide - row.shape[1]))) for row...]
where the time goes in v5:
time: 54.6 us; the launch traced here: 54.5 us
  waiting for transfers between devices  25.2 us (46%)
  starting transfers between devices  19.4 us (36%)
  Pallas kernels  8.65 us (16%)
  other arithmetic  1.01 us (2%)
    ppermute x13, waiting for transfers between devices, exchange(): lax.ppermute(array, axis, [(i, i ^ distance) for i in range(lax.axis_size...  13.8 us
    ppermute x13, starting transfers between devices, exchange(): lax.ppermute(array, axis, [(i, i ^ distance) for i in range(lax.axis_size...  13.2 us
    ppermute x3, waiting for transfers between devices, ahead_by(): lax.ppermute(array, axis, [(i, (i + distance) % count) for i in range(cou...  8.21 us
    pallas_call x1, Pallas kernels, fit(): pl.pallas_call(functools.partial(fit_kernel, owned, half, groups), in_spe...  4.21 us
    ppermute x3, starting transfers between devices, ahead_by(): lax.ppermute(array, axis, [(i, (i + distance) % count) for i in range(cou...  3.7 us
    pallas_call x2, Pallas kernels, build(): pl.pallas_call(functools.partial(build_kernel, parts, order), in_specs=[S...  3.22 us
    ppermute x2, waiting for transfers between devices, pairs_from(): return lax.ppermute(array, axis, swaps)  3.14 us
    ppermute x2, starting transfers between devices, pairs_from(): return lax.ppermute(array, axis, swaps)  2.59 us
  transfers between devices with their start and end apart: 18, of which 10 were waited for; matrix products, arithmetic and copies ran while one was open for 0% of the time, Pallas kernels for 6%

profile of v5, /device:TPU:0, one launch (start us, length us, event | category | flops | bytes accessed | tf_op | source)
XLA Modules:
  0.0 54.5 jit_solution(15767764461670261447)
XLA Ops:
  0.0 4.2 %fit.1 = (bf16[12,128,128]{2,1,0:T(8,128)(2,1)S(1)}, bf16[12,128,128]{2,1,0:T(8,128)(2,1)S(1)}, s32[8,12]{1,0:T(8,128)S(1)}) custom-call(s32[8,12]{1,0:T(8,128)} %tile_hbm.1, s32[32]{0:T(128)} %bitcast.36, s32[32]{0:T(128)} %bitcast.37, bf16[8,128,256]{2,1,0:T(8,128)(2,1)} %d_hbm.1, bf16[8,12,128,128]{3,2,1,0:T(8,128)(2,1)} %t_ref.3), custom_call_target="tpu_custom_call" | custom-call | flops 805306368 | bytes 3670016 | tf_op jit(solution)/shard_map/fit/pallas_call | solution.py:77
  4.7 1.3 %collective-permute-done = bf16[12,128,128]{2,1,0:T(8,128)(2,1)S(1)} collective-permute-done((bf16[12,128,128]{2,1,0:T(8,128)(2,1)S(1)}, bf16[12,128,128]{2,1,0:T(8,128)(2,1)S(1)}, u32[]{:S(2)}, u32[]{:S(2)}) %collective-permute-start) | collective-permute-done | bytes 393248 | tf_op jit(solution)/shard_map/ppermute | solution.py:191
  6.7 2.8 %collective-permute-start.1 = (bf16[3,128,128]{2,1,0:T(8,128)(2,1)S(1)}, bf16[3,128,128]{2,1,0:T(8,128)(2,1)S(1)}, u32[]{:S(2)}, u32[]{:S(2)}) collective-permute-start(bf16[3,128,128]{2,1,0:T(8,128)(2,1)S(1)} %get-tuple-element.31), channel_id=1, source_target_pairs={{0,4},{4,0},{8,12},{12,8},{1,5},{5,1},{9,13},{13,9},{2,6},{6,2},{1... | collective-permute-start | bytes 294920 | tf_op jit(solution)/shard_map/ppermute | solution.py:191
  9.5 2.6 %collective-permute-start.2 = (bf16[3,128,128]{2,1,0:T(8,128)(2,1)S(1)}, bf16[3,128,128]{2,1,0:T(8,128)(2,1)S(1)}, u32[]{:S(2)}, u32[]{:S(2)}) collective-permute-start(bf16[3,128,128]{2,1,0:T(8,128)(2,1)S(1)} %get-tuple-element.30), channel_id=1, source_target_pairs={{0,8},{4,12},{8,0},{12,4},{1,9},{5,13},{9,1},{13,5},{2,10},{6,14},... | collective-permute-start | bytes 294920 | tf_op jit(solution)/shard_map/ppermute | solution.py:191
  12.1 1.2 %collective-permute-done.5.peer_cols = s32[3,4]{1,0:T(4,128)S(1)} collective-permute-done((s32[3,4]{1,0:T(4,128)S(1)}, s32[3,4]{1,0:T(4,128)S(1)}, u32[]{:S(2)}, u32[]{:S(2)}) %collective-permute-start.5) | collective-permute-done | bytes 80 | tf_op jit(solution)/shard_map/ppermute | solution.py:191
  13.2 6.9 %collective-permute-done.2 = bf16[3,128,128]{2,1,0:T(8,128)(2,1)S(1)} collective-permute-done((bf16[3,128,128]{2,1,0:T(8,128)(2,1)S(1)}, bf16[3,128,128]{2,1,0:T(8,128)(2,1)S(1)}, u32[]{:S(2)}, u32[]{:S(2)}) %collective-permute-start.2) | collective-permute-done | bytes 98336 | tf_op jit(solution)/shard_map/ppermute | solution.py:191
  20.2 1.5 %collective-permute-start.6 = (bf16[3,128,128]{2,1,0:T(8,128)(2,1)S(1)}, bf16[3,128,128]{2,1,0:T(8,128)(2,1)S(1)}, u32[]{:S(2)}, u32[]{:S(2)}) collective-permute-start(bf16[3,128,128]{2,1,0:T(8,128)(2,1)S(1)} %fusion.4), channel_id=1, source_target_pairs={{0,2},{2,0},{1,3},{3,1},{4,6},{6,4},{5,7},{7,5},{8,10},{10,8},{9,1... | collective-permute-start | bytes 294920 | tf_op jit(solution)/shard_map/ppermute | solution.py:196
  21.8 3.1 %collective-permute-done.6 = bf16[3,128,128]{2,1,0:T(8,128)(2,1)S(1)} collective-permute-done((bf16[3,128,128]{2,1,0:T(8,128)(2,1)S(1)}, bf16[3,128,128]{2,1,0:T(8,128)(2,1)S(1)}, u32[]{:S(2)}, u32[]{:S(2)}) %collective-permute-start.6) | collective-permute-done | bytes 98336 | tf_op jit(solution)/shard_map/ppermute | solution.py:196
  24.9 1.9 %collective-permute-start.7 = (bf16[6,128,128]{2,1,0:T(8,128)(2,1)S(1)}, bf16[6,128,128]{2,1,0:T(8,128)(2,1)S(1)}, u32[]{:S(2)}, u32[]{:S(2)}) collective-permute-start(bf16[6,128,128]{2,1,0:T(8,128)(2,1)S(1)} %pad_maximum_fusion.1.near_ref), channel_id=1, source_target_pairs={{0,4},{4,0},{8,12},{12,8},{1,5},{5,1},{9,13},{13,9},{2,6},{6,2},{1... | collective-permute-start | bytes 589832 | tf_op jit(solution)/shard_map/ppermute | solution.py:203
  26.9 0.7 %collective-permute-start.8 = (bf16[6,128,128]{2,1,0:T(8,128)(2,1)S(1)}, bf16[6,128,128]{2,1,0:T(8,128)(2,1)S(1)}, u32[]{:S(2)}, u32[]{:S(2)}) collective-permute-start(bf16[6,128,128]{2,1,0:T(8,128)(2,1)S(1)} %pad_maximum_fusion.1.near_ref), channel_id=1, source_target_pairs={{4,8},{8,4},{5,9},{9,5},{6,10},{10,6},{7,11},{11,7},{20,24},{24,20... | collective-permute-start | bytes 589832 | tf_op jit(solution)/shard_map/ppermute | solution.py:203
  27.5 3.1 %collective-permute-done.7.even_ref = bf16[6,128,128]{2,1,0:T(8,128)(2,1)S(1)} collective-permute-done((bf16[6,128,128]{2,1,0:T(8,128)(2,1)S(1)}, bf16[6,128,128]{2,1,0:T(8,128)(2,1)S(1)}, u32[]{:S(2)}, u32[]{:S(2)}) %collective-permute-start.7) | collective-permute-done | bytes 196640 | tf_op jit(solution)/shard_map/ppermute | solution.py:203
  30.7 1.2 %metric.1.rest_0_ = bf16[3,128,128]{2,1,0:T(8,128)(2,1)S(1)} custom-call(s32[3,4]{1,0:T(4,128)S(1)} %copy-done.2, s32[3,4]{1,0:T(4,128)S(1)} %collective-permute-done.5.peer_cols, bf16[6,128,128]{2,1,0:T(8,128)(2,1)S(1)} %pad_maximum_fusion.1.near_ref, bf16[6,128,128]{2,1,0:T(8,128)(2,1)S(1)} %collective-permute-done.7.even_ref, ...), custom_call_target="tpu_custom_call" | custom-call | flops 100663296 | bytes 1376256 | tf_op jit(solution)/shard_map/metric/pallas_call | solution.py:137
  31.9 2.7 %collective-permute-start.9 = (bf16[3,128,128]{2,1,0:T(8,128)(2,1)S(1)}, bf16[3,128,128]{2,1,0:T(8,128)(2,1)S(1)}, u32[]{:S(2)}, u32[]{:S(2)}) collective-permute-start(bf16[3,128,128]{2,1,0:T(8,128)(2,1)S(1)} %metric.1.rest_0_), channel_id=1, source_target_pairs={{0,12},{4,8},{8,4},{12,0},{1,13},{5,9},{9,5},{13,1},{2,14},{6,10},... | collective-permute-start | bytes 294920 | tf_op jit(solution)/shard_map/ppermute | solution.py:191
  34.6 3.8 %collective-permute-start.10 = (bf16[3,128,128]{2,1,0:T(8,128)(2,1)S(1)}, bf16[3,128,128]{2,1,0:T(8,128)(2,1)S(1)}, u32[]{:S(2)}, u32[]{:S(2)}) collective-permute-start(bf16[3,128,128]{2,1,0:T(8,128)(2,1)S(1)} %metric.1.rest_0_), channel_id=1, source_target_pairs={{0,8},{4,12},{8,0},{12,4},{1,9},{5,13},{9,1},{13,5},{2,10},{6,14},... | collective-permute-start | bytes 294920 | tf_op jit(solution)/shard_map/ppermute | solution.py:191
  38.7 0.7 %collective-permute-done.9.rest_1_ = bf16[3,128,128]{2,1,0:T(8,128)(2,1)S(1)} collective-permute-done((bf16[3,128,128]{2,1,0:T(8,128)(2,1)S(1)}, bf16[3,128,128]{2,1,0:T(8,128)(2,1)S(1)}, u32[]{:S(2)}, u32[]{:S(2)}) %collective-permute-start.9) | collective-permute-done | bytes 98336 | tf_op jit(solution)/shard_map/ppermute | solution.py:191
  39.4 2.6 %collective-permute-done.10.rest_2_ = bf16[3,128,128]{2,1,0:T(8,128)(2,1)S(1)} collective-permute-done((bf16[3,128,128]{2,1,0:T(8,128)(2,1)S(1)}, bf16[3,128,128]{2,1,0:T(8,128)(2,1)S(1)}, u32[]{:S(2)}, u32[]{:S(2)}) %collective-permute-start.10) | collective-permute-done | bytes 98336 | tf_op jit(solution)/shard_map/ppermute | solution.py:191
  42.0 1.0 %collective-permute-done.11.rest_3_ = bf16[3,128,128]{2,1,0:T(8,128)(2,1)S(1)} collective-permute-done((bf16[3,128,128]{2,1,0:T(8,128)(2,1)S(1)}, bf16[3,128,128]{2,1,0:T(8,128)(2,1)S(1)}, u32[]{:S(2)}, u32[]{:S(2)}) %collective-permute-start.11) | collective-permute-done | bytes 98336 | tf_op jit(solution)/shard_map/ppermute | solution.py:191
  43.1 1.6 %build_own.1 = bf16[2,8,64,128]{3,2,1,0:T(8,128)(2,1)S(1)} custom-call(s32[8,12]{1,0:T(8,128)S(1)} %get-tuple-element.16.slot_ref, bf16[8,12,128,128]{3,2,1,0:T(8,128)(2,1)S(1)} %copy-done, bf16[3,128,128]{2,1,0:T(8,128)(2,1)S(1)} %metric.1.rest_0_, bf16[3,128,128]{2,1,0:T(8,128)(2,1)S(1)} %collective-permute-done.9.rest_1_, ...), custom_call_target="tpu_custom_call" | custom-call | flops 402653184 | bytes 3407872 | tf_op jit(solution)/shard_map/build_own/pallas_call | solution.py:174
  44.7 1.5 %collective-permute-start.12 = (bf16[8,64,128]{2,1,0:T(8,128)(2,1)S(1)}, bf16[8,64,128]{2,1,0:T(8,128)(2,1)S(1)}, u32[]{:S(2)}, u32[]{:S(2)}) collective-permute-start(bf16[8,64,128]{2,1,0:T(8,128)(2,1)S(1)} %slice_bitcast_fusion.2), channel_id=1, source_target_pairs={{0,2},{2,0},{1,3},{3,1},{4,6},{6,4},{5,7},{7,5},{8,10},{10,8},{9,1... | collective-permute-start | bytes 393224 | tf_op jit(solution)/shard_map/ppermute | solution.py:196
  46.3 1.6 %build_other.1 = bf16[2,8,64,128]{3,2,1,0:T(8,128)(2,1)S(1)} custom-call(s32[8,12]{1,0:T(8,128)S(1)} %get-tuple-element.16.slot_ref, bf16[8,12,128,128]{3,2,1,0:T(8,128)(2,1)S(1)} %copy-done, bf16[3,128,128]{2,1,0:T(8,128)(2,1)S(1)} %collective-permute-done.13.rest_0_, bf16[3,128,128]{2,1,0:T(8,128)(2,1)S(1)} %collective-permute-done.14.rest_1_, ...), custom_call_target="tpu_custom_call" | custom-call | flops 402653184 | bytes 3407872 | tf_op jit(solution)/shard_map/build_other/pallas_call | solution.py:174
  47.9 0.6 %collective-permute-start.17 = (bf16[8,64,128]{2,1,0:T(8,128)(2,1)S(1)}, bf16[8,64,128]{2,1,0:T(8,128)(2,1)S(1)}, u32[]{:S(2)}, u32[]{:S(2)}) collective-permute-start(bf16[8,64,128]{2,1,0:T(8,128)(2,1)S(1)} %slice_bitcast_fusion), channel_id=1, source_target_pairs={{0,2},{2,0},{1,3},{3,1},{4,6},{6,4},{5,7},{7,5},{8,10},{10,8},{9,1... | collective-permute-start | bytes 393224 | tf_op jit(solution)/shard_map/ppermute | solution.py:196
  48.5 2.2 %collective-permute-done.12 = bf16[8,64,128]{2,1,0:T(8,128)(2,1)S(1)} collective-permute-done((bf16[8,64,128]{2,1,0:T(8,128)(2,1)S(1)}, bf16[8,64,128]{2,1,0:T(8,128)(2,1)S(1)}, u32[]{:S(2)}, u32[]{:S(2)}) %collective-permute-start.12) | collective-permute-done | bytes 131104 | tf_op jit(solution)/shard_map/ppermute | solution.py:196
  50.7 2.9 %collective-permute-done.17 = bf16[8,64,128]{2,1,0:T(8,128)(2,1)S(1)} collective-permute-done((bf16[8,64,128]{2,1,0:T(8,128)(2,1)S(1)}, bf16[8,64,128]{2,1,0:T(8,128)(2,1)S(1)}, u32[]{:S(2)}, u32[]{:S(2)}) %collective-permute-start.17) | collective-permute-done | bytes 131104 | tf_op jit(solution)/shard_map/ppermute | solution.py:196
  53.7 0.7 %pad_maximum_fusion = bf16[8,64,256]{2,1,0:T(8,128)(2,1)} fusion(bf16[8,64,128]{2,1,0:T(8,128)(2,1)S(1)} %get-tuple-element.28, bf16[8,64,128]{2,1,0:T(8,128)(2,1)S(1)} %get-tuple-element.27), kind=kLoop, calls=%fused_computation.1 | loop fusion | flops 524288 | bytes 524288 | tf_op jit(solution)/shard_map/concatenate | solution.py:250
  (30 shorter events, 1.6 us)
Async XLA Ops:
  0.0 6.2 %copy-start.1 = (bf16[3,4,128,128]{3,2,1,0:T(8,128)(2,1)S(1)}, bf16[3,4,128,128]{3,2,1,0:T(8,128)(2,1)}, u32[]{:S(2)}) copy-start(bf16[3,4,128,128]{3,2,1,0:T(8,128)(2,1)} %m_ref.1) | copy-start | bytes 1179652
  0.0 12.1 %copy-start.2 = (s32[3,4]{1,0:T(4,128)S(1)}, s32[3,4]{1,0:T(4,128)}, u32[]{:S(2)}) copy-start(s32[3,4]{1,0:T(4,128)} %mine_cols.1) | copy-start | bytes 148
  0.0 43.1 %copy-start = (bf16[8,12,128,128]{3,2,1,0:T(8,128)(2,1)S(1)}, bf16[8,12,128,128]{3,2,1,0:T(8,128)(2,1)}, u32[]{:S(2)}) copy-start(bf16[8,12,128,128]{3,2,1,0:T(8,128)(2,1)} %t_ref.3) | copy-start | bytes 9437188
  4.2 1.9 %collective-permute-start = (bf16[12,128,128]{2,1,0:T(8,128)(2,1)S(1)}, bf16[12,128,128]{2,1,0:T(8,128)(2,1)S(1)}, u32[]{:S(2)}, u32[]{:S(2)}) collective-permute-start(bf16[12,128,128]{2,1,0:T(8,128)(2,1)S(1)} %get-tuple-element.18), channel_id=1, source_target_pairs={{0,1},{1,0},{2,3},{3,2},{4,5},{5,4},{6,7},{7,6},{8,9},{9,8},{10,11... | collective-permute-start | bytes 1179656 | tf_op jit(solution)/shard_map/ppermute | solution.py:191
  6.2 14.0 %collective-permute-start.4 = (bf16[3,4,128,128]{3,2,1,0:T(8,128)(2,1)S(1)}, bf16[3,4,128,128]{3,2,1,0:T(8,128)(2,1)S(1)}, u32[]{:S(2)}, u32[]{:S(2)}) collective-permute-start(bf16[3,4,128,128]{3,2,1,0:T(8,128)(2,1)S(1)} %copy-done.1), channel_id=1, source_target_pairs={{0,1},{1,0},{2,3},{3,2},{4,5},{5,4},{6,7},{7,6},{8,9},{9,8},{10,11... | collective-permute-start | bytes 1179656 | tf_op jit(solution)/shard_map/ppermute | solution.py:191
  6.7 6.5 %collective-permute-start.1 = (bf16[3,128,128]{2,1,0:T(8,128)(2,1)S(1)}, bf16[3,128,128]{2,1,0:T(8,128)(2,1)S(1)}, u32[]{:S(2)}, u32[]{:S(2)}) collective-permute-start(bf16[3,128,128]{2,1,0:T(8,128)(2,1)S(1)} %get-tuple-element.31), channel_id=1, source_target_pairs={{0,4},{4,0},{8,12},{12,8},{1,5},{5,1},{9,13},{13,9},{2,6},{6,2},{1... | collective-permute-start | bytes 294920 | tf_op jit(solution)/shard_map/ppermute | solution.py:191
  9.5 10.7 %collective-permute-start.2 = (bf16[3,128,128]{2,1,0:T(8,128)(2,1)S(1)}, bf16[3,128,128]{2,1,0:T(8,128)(2,1)S(1)}, u32[]{:S(2)}, u32[]{:S(2)}) collective-permute-start(bf16[3,128,128]{2,1,0:T(8,128)(2,1)S(1)} %get-tuple-element.30), channel_id=1, source_target_pairs={{0,8},{4,12},{8,0},{12,4},{1,9},{5,13},{9,1},{13,5},{2,10},{6,14},... | collective-permute-start | bytes 294920 | tf_op jit(solution)/shard_map/ppermute | solution.py:191
  12.1 8.1 %collective-permute-start.3 = (bf16[3,128,128]{2,1,0:T(8,128)(2,1)S(1)}, bf16[3,128,128]{2,1,0:T(8,128)(2,1)S(1)}, u32[]{:S(2)}, u32[]{:S(2)}) collective-permute-start(bf16[3,128,128]{2,1,0:T(8,128)(2,1)S(1)} %get-tuple-element.29), channel_id=1, source_target_pairs={{0,12},{4,8},{8,4},{12,0},{1,13},{5,9},{9,5},{13,1},{2,14},{6,10},... | collective-permute-start | bytes 294920 | tf_op jit(solution)/shard_map/ppermute | solution.py:191
  12.1 1.2 %collective-permute-start.5 = (s32[3,4]{1,0:T(4,128)S(1)}, s32[3,4]{1,0:T(4,128)S(1)}, u32[]{:S(2)}, u32[]{:S(2)}) collective-permute-start(s32[3,4]{1,0:T(4,128)S(1)} %copy-done.2), channel_id=1, source_target_pairs={{0,1},{1,0},{2,3},{3,2},{4,5},{5,4},{6,7},{7,6},{8,9},{9,8},{10,11... | collective-permute-start | bytes 152 | tf_op jit(solution)/shard_map/ppermute | solution.py:191
  20.2 4.7 %collective-permute-start.6 = (bf16[3,128,128]{2,1,0:T(8,128)(2,1)S(1)}, bf16[3,128,128]{2,1,0:T(8,128)(2,1)S(1)}, u32[]{:S(2)}, u32[]{:S(2)}) collective-permute-start(bf16[3,128,128]{2,1,0:T(8,128)(2,1)S(1)} %fusion.4), channel_id=1, source_target_pairs={{0,2},{2,0},{1,3},{3,1},{4,6},{6,4},{5,7},{7,5},{8,10},{10,8},{9,1... | collective-permute-start | bytes 294920 | tf_op jit(solution)/shard_map/ppermute | solution.py:196
  24.9 5.7 %collective-permute-start.7 = (bf16[6,128,128]{2,1,0:T(8,128)(2,1)S(1)}, bf16[6,128,128]{2,1,0:T(8,128)(2,1)S(1)}, u32[]{:S(2)}, u32[]{:S(2)}) collective-permute-start(bf16[6,128,128]{2,1,0:T(8,128)(2,1)S(1)} %pad_maximum_fusion.1.near_ref), channel_id=1, source_target_pairs={{0,4},{4,0},{8,12},{12,8},{1,5},{5,1},{9,13},{13,9},{2,6},{6,2},{1... | collective-permute-start | bytes 589832 | tf_op jit(solution)/shard_map/ppermute | solution.py:203
  26.9 3.8 %collective-permute-start.8 = (bf16[6,128,128]{2,1,0:T(8,128)(2,1)S(1)}, bf16[6,128,128]{2,1,0:T(8,128)(2,1)S(1)}, u32[]{:S(2)}, u32[]{:S(2)}) collective-permute-start(bf16[6,128,128]{2,1,0:T(8,128)(2,1)S(1)} %pad_maximum_fusion.1.near_ref), channel_id=1, source_target_pairs={{4,8},{8,4},{5,9},{9,5},{6,10},{10,6},{7,11},{11,7},{20,24},{24,20... | collective-permute-start | bytes 589832 | tf_op jit(solution)/shard_map/ppermute | solution.py:203
  31.9 7.5 %collective-permute-start.9 = (bf16[3,128,128]{2,1,0:T(8,128)(2,1)S(1)}, bf16[3,128,128]{2,1,0:T(8,128)(2,1)S(1)}, u32[]{:S(2)}, u32[]{:S(2)}) collective-permute-start(bf16[3,128,128]{2,1,0:T(8,128)(2,1)S(1)} %metric.1.rest_0_), channel_id=1, source_target_pairs={{0,12},{4,8},{8,4},{12,0},{1,13},{5,9},{9,5},{13,1},{2,14},{6,10},... | collective-permute-start | bytes 294920 | tf_op jit(solution)/shard_map/ppermute | solution.py:191
  34.6 7.5 %collective-permute-start.10 = (bf16[3,128,128]{2,1,0:T(8,128)(2,1)S(1)}, bf16[3,128,128]{2,1,0:T(8,128)(2,1)S(1)}, u32[]{:S(2)}, u32[]{:S(2)}) collective-permute-start(bf16[3,128,128]{2,1,0:T(8,128)(2,1)S(1)} %metric.1.rest_0_), channel_id=1, source_target_pairs={{0,8},{4,12},{8,0},{12,4},{1,9},{5,13},{9,1},{13,5},{2,10},{6,14},... | collective-permute-start | bytes 294920 | tf_op jit(solution)/shard_map/ppermute | solution.py:191
  38.4 4.7 %collective-permute-start.11 = (bf16[3,128,128]{2,1,0:T(8,128)(2,1)S(1)}, bf16[3,128,128]{2,1,0:T(8,128)(2,1)S(1)}, u32[]{:S(2)}, u32[]{:S(2)}) collective-permute-start(bf16[3,128,128]{2,1,0:T(8,128)(2,1)S(1)} %metric.1.rest_0_), channel_id=1, source_target_pairs={{0,4},{4,0},{8,12},{12,8},{1,5},{5,1},{9,13},{13,9},{2,6},{6,2},{1... | collective-permute-start | bytes 294920 | tf_op jit(solution)/shard_map/ppermute | solution.py:191
  38.7 7.6 %collective-permute-start.13 = (bf16[3,128,128]{2,1,0:T(8,128)(2,1)S(1)}, bf16[3,128,128]{2,1,0:T(8,128)(2,1)S(1)}, u32[]{:S(2)}, u32[]{:S(2)}) collective-permute-start(bf16[3,128,128]{2,1,0:T(8,128)(2,1)S(1)} %metric.1.rest_0_), channel_id=1, source_target_pairs={{0,1},{1,0},{2,3},{3,2},{4,5},{5,4},{6,7},{7,6},{8,9},{9,8},{10,11... | collective-permute-start | bytes 294920 | tf_op jit(solution)/shard_map/ppermute | solution.py:191
  39.4 6.8 %collective-permute-start.14 = (bf16[3,128,128]{2,1,0:T(8,128)(2,1)S(1)}, bf16[3,128,128]{2,1,0:T(8,128)(2,1)S(1)}, u32[]{:S(2)}, u32[]{:S(2)}) collective-permute-start(bf16[3,128,128]{2,1,0:T(8,128)(2,1)S(1)} %collective-permute-done.9.rest_1_), channel_id=1, source_target_pairs={{0,1},{1,0},{2,3},{3,2},{4,5},{5,4},{6,7},{7,6},{8,9},{9,8},{10,11... | collective-permute-start | bytes 294920 | tf_op jit(solution)/shard_map/ppermute | solution.py:191
  42.0 4.2 %collective-permute-start.15 = (bf16[3,128,128]{2,1,0:T(8,128)(2,1)S(1)}, bf16[3,128,128]{2,1,0:T(8,128)(2,1)S(1)}, u32[]{:S(2)}, u32[]{:S(2)}) collective-permute-start(bf16[3,128,128]{2,1,0:T(8,128)(2,1)S(1)} %collective-permute-done.10.rest_2_), channel_id=1, source_target_pairs={{0,1},{1,0},{2,3},{3,2},{4,5},{5,4},{6,7},{7,6},{8,9},{9,8},{10,11... | collective-permute-start | bytes 294920 | tf_op jit(solution)/shard_map/ppermute | solution.py:191
  43.1 3.2 %collective-permute-start.16 = (bf16[3,128,128]{2,1,0:T(8,128)(2,1)S(1)}, bf16[3,128,128]{2,1,0:T(8,128)(2,1)S(1)}, u32[]{:S(2)}, u32[]{:S(2)}) collective-permute-start(bf16[3,128,128]{2,1,0:T(8,128)(2,1)S(1)} %collective-permute-done.11.rest_3_), channel_id=1, source_target_pairs={{0,1},{1,0},{2,3},{3,2},{4,5},{5,4},{6,7},{7,6},{8,9},{9,8},{10,11... | collective-permute-start | bytes 294920 | tf_op jit(solution)/shard_map/ppermute | solution.py:191
  44.7 6.0 %collective-permute-start.12 = (bf16[8,64,128]{2,1,0:T(8,128)(2,1)S(1)}, bf16[8,64,128]{2,1,0:T(8,128)(2,1)S(1)}, u32[]{:S(2)}, u32[]{:S(2)}) collective-permute-start(bf16[8,64,128]{2,1,0:T(8,128)(2,1)S(1)} %slice_bitcast_fusion.2), channel_id=1, source_target_pairs={{0,2},{2,0},{1,3},{3,1},{4,6},{6,4},{5,7},{7,5},{8,10},{10,8},{9,1... | collective-permute-start | bytes 393224 | tf_op jit(solution)/shard_map/ppermute | solution.py:196
  47.9 5.7 %collective-permute-start.17 = (bf16[8,64,128]{2,1,0:T(8,128)(2,1)S(1)}, bf16[8,64,128]{2,1,0:T(8,128)(2,1)S(1)}, u32[]{:S(2)}, u32[]{:S(2)}) collective-permute-start(bf16[8,64,128]{2,1,0:T(8,128)(2,1)S(1)} %slice_bitcast_fusion), channel_id=1, source_target_pairs={{0,2},{2,0},{1,3},{3,1},{4,6},{6,4},{5,7},{7,5},{8,10},{10,8},{9,1... | collective-permute-start | bytes 393224 | tf_op jit(solution)/shard_map/ppermute | solution.py:196

commit v6 on v5

--- a/solution.py
+++ b/solution.py
@@ -16,9 +16,9 @@
 ANY = pl.BlockSpec(memory_space=pl.ANY)
 
 
-def fit_kernel(
-    owned, half, groups, tile_hbm, domain_hbm, number_hbm, d_hbm, t_hbm, keep_ref, send_ref, slot_any,
-    acc, tile_ref, domain_ref, number_ref, slot_ref, d_ref, t_ref, small_sem, d_sem, t_sem,
+def fit_other_kernel(
+    owned, half, groups, tile_hbm, domain_hbm, number_hbm, d_hbm, t_hbm, send_ref, slot_any, own_ref, t_ref,
+    acc, tile_ref, domain_ref, number_ref, slot_ref, d_ref, small_sem, d_sem, t_sem,
 ):
     me = lax.axis_index("space")
     mine = lax.axis_index("sub")
@@ -46,12 +46,15 @@
     acc[...] = jnp.zeros_like(acc)
     for copy in small:
         copy.wait()
+    other = pl.multiple_of((1 - mine) * half, half)
+    own = pl.multiple_of(mine * half, half)
     begin = 0
     for size, pair in zip(groups, copies):
         for copy in pair:
             copy.wait()
         for p in range(begin, begin + size):
-            rows = jnp.transpose(d_ref[p])
+            rows = jnp.transpose(d_ref[p, :, pl.ds(other, half)])
+            own_ref[p] = jnp.transpose(d_ref[p, :, pl.ds(own, half)])
             for k in range(listed):
                 touched = tile_ref[p, k]
                 slot = jnp.bitwise_xor(domain_ref[touched], me) * owned + number_ref[touched]
@@ -60,48 +63,84 @@
         begin += size
     slot_copy = pltpu.make_async_copy(slot_ref, slot_any, small_sem.at[3])
     slot_copy.start()
-    keep_ref[...] = acc[:, pl.ds(pl.multiple_of(mine * half, half), half), :].astype(BF16)
-    send_ref[...] = acc[:, pl.ds(pl.multiple_of((1 - mine) * half, half), half), :].astype(BF16)
+    send_ref[...] = acc[...].astype(BF16)
     slot_copy.wait()
 
 
-def fit(block_tile, domain, number, densities, three_centre, domains, owned):
+def fit_other(block_tile, domain, number, densities, three_centre, domains, owned):
     blocks, listed, width, _ = three_centre.shape
-    columns = densities.shape[2]
-    half = columns // 2
+    half = densities.shape[2] // 2
     count = domains * owned
     groups = (blocks // 4, 3 * blocks // 8, blocks - blocks // 4 - 3 * blocks // 8)
-    out = jax.ShapeDtypeStruct((count, half, width), BF16)
     operands = (block_tile, domain, number, densities, three_centre)
     operands = [pltpu.with_memory_space_constraint(operand, pltpu.HBM) for operand in operands]
     return pl.pallas_call(
-        functools.partial(fit_kernel, owned, half, groups),
+        functools.partial(fit_other_kernel, owned, half, groups),
         in_specs=[pl.BlockSpec(memory_space=pltpu.HBM)] * 5,
-        out_specs=[VMEM, VMEM, ANY],
+        out_specs=[VMEM, ANY, VMEM, VMEM],
         scratch_shapes=[
-            pltpu.VMEM((count, columns, width), F32),
+            pltpu.VMEM((count, half, width), F32),
             pltpu.SMEM(block_tile.shape, jnp.int32),
             pltpu.SMEM(domain.shape, jnp.int32),
             pltpu.SMEM(number.shape, jnp.int32),
             pltpu.SMEM(block_tile.shape, jnp.int32),
             pltpu.VMEM(densities.shape, BF16),
-            pltpu.VMEM(three_centre.shape, BF16),
             pltpu.SemaphoreType.DMA((4,)),
             pltpu.SemaphoreType.DMA((len(groups),)),
             pltpu.SemaphoreType.DMA((len(groups),)),
         ],
-        out_shape=[out, out, jax.ShapeDtypeStruct(block_tile.shape, jnp.int32)],
+        out_shape=[
+            jax.ShapeDtypeStruct((count, half, width), BF16),
+            jax.ShapeDtypeStruct(block_tile.shape, jnp.int32),
+            jax.ShapeDtypeStruct((blocks, half, width), BF16),
+            jax.ShapeDtypeStruct(three_centre.shape, BF16),
+        ],
         compiler_params=pltpu.CompilerParams(vmem_limit_bytes=VMEM_LIMIT),
         cost_estimate=pl.CostEstimate(
-            flops=2 * blocks * listed * width * width * columns,
+            flops=2 * blocks * listed * width * width * half,
             bytes_accessed=2 * (three_centre.size + densities.size),
             transcendentals=0,
         ),
-        name="fit",
+        name="fit_other",
     )(*operands)
 
 
-def metric_kernel(owned, count, mine_cols, peer_cols, near_ref, even_ref, odd_ref, m_ref, pm_ref, out_ref, window):
+def fit_own_kernel(slot_any, own_ref, t_ref, keep_ref, acc, slot_ref, sem):
+    slot_copy = pltpu.make_async_copy(slot_any, slot_ref, sem)
+    slot_copy.start()
+    acc[...] = jnp.zeros_like(acc)
+    slot_copy.wait()
+    for p in range(t_ref.shape[0]):
+        rows = own_ref[p]
+        for k in range(t_ref.shape[1]):
+            acc[slot_ref[p, k]] += jnp.dot(rows, t_ref[p, k], preferred_element_type=F32)
+    keep_ref[...] = acc[...].astype(BF16)
+
+
+def fit_own(slots, own_rows, three_centre, count):
+    blocks, listed, width, _ = three_centre.shape
+    half = own_rows.shape[1]
+    return pl.pallas_call(
+        fit_own_kernel,
+        in_specs=[ANY, VMEM, VMEM],
+        out_specs=VMEM,
+        scratch_shapes=[
+            pltpu.VMEM((count, half, width), F32),
+            pltpu.SMEM(slots.shape, jnp.int32),
+            pltpu.SemaphoreType.DMA,
+        ],
+        out_shape=jax.ShapeDtypeStruct((count, half, width), BF16),
+        compiler_params=pltpu.CompilerParams(vmem_limit_bytes=VMEM_LIMIT),
+        cost_estimate=pl.CostEstimate(
+            flops=2 * blocks * listed * width * width * half,
+            bytes_accessed=2 * (three_centre.size + own_rows.size),
+            transcendentals=0,
+        ),
+        name="fit_own",
+    )(slots, own_rows, three_centre)
+
+
+def metric_kernel(owned, count, mine_cols, peer_cols, near_ref, odd_ref, even_ref, m_ref, pm_ref, out_ref, window):
     me = lax.axis_index("space")
     aux = lax.axis_index("aux")
     own = owned * count
@@ -131,7 +170,7 @@
         ).astype(BF16)
 
 
-def metric(mine_cols, peer_cols, near, even, odd, m, pm, count):
+def metric(mine_cols, peer_cols, near, odd, even, m, pm, count):
     owned, listed, width, _ = m.shape
     half = near.shape[1]
     return pl.pallas_call(
@@ -147,7 +186,7 @@
             transcendentals=0,
         ),
         name="metric",
-    )(mine_cols, peer_cols, near, even, odd, m, pm)
+    )(mine_cols, peer_cols, near, odd, even, m, pm)
 
 
 def build_kernel(parts, order, slot_ref, t_ref, *rest):
@@ -214,26 +253,30 @@
     domain = owner_domain.reshape(touched)
     number = owner_tile.reshape(touched)
 
-    keep, send, slots = fit(block_tile, domain, number, densities, three_centre, domains, owned)
+    send, slots, own_rows, three_centre = fit_other(
+        block_tile, domain, number, densities, three_centre, domains, owned
+    )
     got = exchange(send, "sub", 1)
+    keep = fit_own(slots, own_rows, three_centre, domains * owned)
     chip = (keep.astype(F32) + got.astype(F32)).astype(BF16).reshape(domains, owned, half, width)
     chip, own_metric, own_columns = lax.optimization_barrier((chip, metric_inverse, metric_columns))
     arrived = [exchange(chip[k], "space", k) for k in range(1, domains)]
     peer_metric = exchange(own_metric, "sub", 1)
     peer_columns = exchange(own_columns, "sub", 1)
-    arrived, peer_metric, peer_columns = lax.optimization_barrier((arrived, peer_metric, peer_columns))
+    arrived, peer_metric, peer_columns = lax.optimization_barrier((arrived[::-1], peer_metric, peer_columns))
+    arrived = arrived[::-1]
     total = chip[0].astype(F32)
-    for piece in arrived:
+    for piece in arrived[::-1]:
         total = total + piece.astype(F32)
     fitted = total.astype(BF16)
 
     near = jnp.concatenate(
         [fitted] + [ahead_by(fitted, "aux", aux_count - k) for k in range(1, aux_count)]
     )
+    odd = pairs_from(near, "space", 1)
     even = pairs_from(near, "space", 0)
-    odd = pairs_from(near, "space", 1)
     coefficients = metric(
-        metric_columns, peer_columns, near, even, odd, metric_inverse, peer_metric, aux_count
+        metric_columns, peer_columns, near, odd, even, metric_inverse, peer_metric, aux_count
     )
 
     order = [0] + list(range(domains - 1, 0, -1))

time: 54.6 us -> 53 us (0.971)
  waiting for transfers between devices: 25.2 us -> 23.7 us
  starting transfers between devices: 19.4 us -> 18.4 us
  Pallas kernels: 8.65 us -> 9.51 us
    ppermute x13, starting transfers between devices: 13.2 us -> 11.4 us  [exchange(): lax.ppermute(array, axis, [(i, i ^ distance) for i in range(lax.axis_size...]
    ppermute x13, waiting for transfers between devices: 13.8 us -> 12.7 us  [exchange(): lax.ppermute(array, axis, [(i, i ^ distance) for i in range(lax.axis_size...]
    pallas_call x1 -> x2, Pallas kernels: 4.21 us -> 5.07 us  [the longest x1 3.39 us: fit_other(): pl.pallas_call(functools.partial(fit_other_kernel, owned, half, groups),...]
    ppermute x3, waiting for transfers between devices: 8.21 us -> 7.41 us  [ahead_by(): lax.ppermute(array, axis, [(i, (i + distance) % count) for i in range(cou...]
  transfers between devices with their start and end apart: 18 -> 18, of which waited for: 10 -> 9; matrix products, arithmetic and copies ran while one was open for 0% -> 0% of each run, Pallas kernels for 6% -> 9%
where the time goes in v6:
time: 53 us; the launch traced here: 52.9 us
  waiting for transfers between devices  23.7 us (45%)
  starting transfers between devices  18.4 us (35%)
  Pallas kernels  9.51 us (18%)
  other arithmetic  1.01 us (2%)
    ppermute x13, waiting for transfers between devices, exchange(): lax.ppermute(array, axis, [(i, i ^ distance) for i in range(lax.axis_size...  12.7 us
    ppermute x13, starting transfers between devices, exchange(): lax.ppermute(array, axis, [(i, i ^ distance) for i in range(lax.axis_size...  11.4 us
    ppermute x3, waiting for transfers between devices, ahead_by(): lax.ppermute(array, axis, [(i, (i + distance) % count) for i in range(cou...  7.41 us
    ppermute x3, starting transfers between devices, ahead_by(): lax.ppermute(array, axis, [(i, (i + distance) % count) for i in range(cou...  4.04 us
    ppermute x2, waiting for transfers between devices, pairs_from(): return lax.ppermute(array, axis, swaps)  3.65 us
    pallas_call x1, Pallas kernels, fit_other(): pl.pallas_call(functools.partial(fit_other_kernel, owned, half, groups),...  3.39 us
    pallas_call x2, Pallas kernels, build(): pl.pallas_call(functools.partial(build_kernel, parts, order), in_specs=[S...  3.23 us
    ppermute x2, starting transfers between devices, pairs_from(): return lax.ppermute(array, axis, swaps)  2.95 us
  transfers between devices with their start and end apart: 18, of which 9 were waited for; matrix products, arithmetic and copies ran while one was open for 0% of the time, Pallas kernels for 9%

profile of v6, /device:TPU:0, one launch (start us, length us, event | category | flops | bytes accessed | tf_op | source)
XLA Modules:
  0.0 52.9 jit_solution(12575876323434240132)
XLA Ops:
  0.0 3.4 %fit_other.1 = (bf16[12,128,128]{2,1,0:T(8,128)(2,1)S(1)}, s32[8,12]{1,0:T(8,128)S(1)}, bf16[8,128,128]{2,1,0:T(8,128)(2,1)S(1)}, bf16[8,12,128,128]{3,2,1,0:T(8,128)(2,1)S(1)}) custom-call(s32[8,12]{1,0:T(8,128)} %tile_hbm.1, s32[32]{0:T(128)} %bitcast.36, s32[32]{0:T(128)} %bitcast.37, bf16[8,128,256]{2,1,0:T(8,128)(2,1)} %d_hbm.1, ...), custom_call_target="tpu_custom_call" | custom-call | flops 402653184 | bytes 3670016 | tf_op jit(solution)/shard_map/fit_other/pallas_call | solution.py:77
  3.9 1.7 %fit_own.1 = bf16[12,128,128]{2,1,0:T(8,128)(2,1)S(1)} custom-call(s32[8,12]{1,0:T(8,128)S(1)} %get-tuple-element.17.slot_any.slot_ref, bf16[8,128,128]{2,1,0:T(8,128)(2,1)S(1)} %get-tuple-element.19.own_ref, bf16[8,12,128,128]{3,2,1,0:T(8,128)(2,1)S(1)} %get-tuple-element.18.t_ref), custom_call_target="tpu_custom_call" | custom-call | flops 402653184 | bytes 3407872 | tf_op jit(solution)/shard_map/fit_own/pallas_call | solution.py:123
  5.9 5.1 %collective-permute-start.1 = (bf16[3,128,128]{2,1,0:T(8,128)(2,1)S(1)}, bf16[3,128,128]{2,1,0:T(8,128)(2,1)S(1)}, u32[]{:S(2)}, u32[]{:S(2)}) collective-permute-start(bf16[3,128,128]{2,1,0:T(8,128)(2,1)S(1)} %get-tuple-element.33), channel_id=1, source_target_pairs={{0,12},{4,8},{8,4},{12,0},{1,13},{5,9},{9,5},{13,1},{2,14},{6,10},... | collective-permute-start | bytes 294920 | tf_op jit(solution)/shard_map/ppermute | solution.py:230
  11.7 1.2 %collective-permute-done.5.peer_cols = s32[3,4]{1,0:T(4,128)S(1)} collective-permute-done((s32[3,4]{1,0:T(4,128)S(1)}, s32[3,4]{1,0:T(4,128)S(1)}, u32[]{:S(2)}, u32[]{:S(2)}) %collective-permute-start.5) | collective-permute-done | bytes 80 | tf_op jit(solution)/shard_map/ppermute | solution.py:230
  12.8 1.9 %collective-permute-done.1 = bf16[3,128,128]{2,1,0:T(8,128)(2,1)S(1)} collective-permute-done((bf16[3,128,128]{2,1,0:T(8,128)(2,1)S(1)}, bf16[3,128,128]{2,1,0:T(8,128)(2,1)S(1)}, u32[]{:S(2)}, u32[]{:S(2)}) %collective-permute-start.1) | collective-permute-done | bytes 98336 | tf_op jit(solution)/shard_map/ppermute | solution.py:230
  14.7 4.8 %collective-permute-done.2 = bf16[3,128,128]{2,1,0:T(8,128)(2,1)S(1)} collective-permute-done((bf16[3,128,128]{2,1,0:T(8,128)(2,1)S(1)}, bf16[3,128,128]{2,1,0:T(8,128)(2,1)S(1)}, u32[]{:S(2)}, u32[]{:S(2)}) %collective-permute-start.2) | collective-permute-done | bytes 98336 | tf_op jit(solution)/shard_map/ppermute | solution.py:230
  19.6 1.6 %collective-permute-start.6 = (bf16[3,128,128]{2,1,0:T(8,128)(2,1)S(1)}, bf16[3,128,128]{2,1,0:T(8,128)(2,1)S(1)}, u32[]{:S(2)}, u32[]{:S(2)}) collective-permute-start(bf16[3,128,128]{2,1,0:T(8,128)(2,1)S(1)} %fusion.4), channel_id=1, source_target_pairs={{0,2},{2,0},{1,3},{3,1},{4,6},{6,4},{5,7},{7,5},{8,10},{10,8},{9,1... | collective-permute-start | bytes 294920 | tf_op jit(solution)/shard_map/ppermute | solution.py:235
  21.1 3.1 %collective-permute-done.6 = bf16[3,128,128]{2,1,0:T(8,128)(2,1)S(1)} collective-permute-done((bf16[3,128,128]{2,1,0:T(8,128)(2,1)S(1)}, bf16[3,128,128]{2,1,0:T(8,128)(2,1)S(1)}, u32[]{:S(2)}, u32[]{:S(2)}) %collective-permute-start.6) | collective-permute-done | bytes 98336 | tf_op jit(solution)/shard_map/ppermute | solution.py:235
  24.3 0.7 %collective-permute-start.7 = (bf16[6,128,128]{2,1,0:T(8,128)(2,1)S(1)}, bf16[6,128,128]{2,1,0:T(8,128)(2,1)S(1)}, u32[]{:S(2)}, u32[]{:S(2)}) collective-permute-start(bf16[6,128,128]{2,1,0:T(8,128)(2,1)S(1)} %pad_maximum_fusion.1.near_ref), channel_id=1, source_target_pairs={{4,8},{8,4},{5,9},{9,5},{6,10},{10,6},{7,11},{11,7},{20,24},{24,20... | collective-permute-start | bytes 589832 | tf_op jit(solution)/shard_map/ppermute | solution.py:242
  24.9 2.3 %collective-permute-start.8 = (bf16[6,128,128]{2,1,0:T(8,128)(2,1)S(1)}, bf16[6,128,128]{2,1,0:T(8,128)(2,1)S(1)}, u32[]{:S(2)}, u32[]{:S(2)}) collective-permute-start(bf16[6,128,128]{2,1,0:T(8,128)(2,1)S(1)} %pad_maximum_fusion.1.near_ref), channel_id=1, source_target_pairs={{0,4},{4,0},{8,12},{12,8},{1,5},{5,1},{9,13},{13,9},{2,6},{6,2},{1... | collective-permute-start | bytes 589832 | tf_op jit(solution)/shard_map/ppermute | solution.py:242
  27.2 3.6 %collective-permute-done.8.even_ref = bf16[6,128,128]{2,1,0:T(8,128)(2,1)S(1)} collective-permute-done((bf16[6,128,128]{2,1,0:T(8,128)(2,1)S(1)}, bf16[6,128,128]{2,1,0:T(8,128)(2,1)S(1)}, u32[]{:S(2)}, u32[]{:S(2)}) %collective-permute-start.8) | collective-permute-done | bytes 196640 | tf_op jit(solution)/shard_map/ppermute | solution.py:242
  30.9 1.2 %metric.1.rest_0_ = bf16[3,128,128]{2,1,0:T(8,128)(2,1)S(1)} custom-call(s32[3,4]{1,0:T(4,128)S(1)} %copy-done.1, s32[3,4]{1,0:T(4,128)S(1)} %collective-permute-done.5.peer_cols, bf16[6,128,128]{2,1,0:T(8,128)(2,1)S(1)} %pad_maximum_fusion.1.near_ref, bf16[6,128,128]{2,1,0:T(8,128)(2,1)S(1)} %collective-permute-done.7.odd_ref, ...), custom_call_target="tpu_custom_call" | custom-call | flops 100663296 | bytes 1376256 | tf_op jit(solution)/shard_map/metric/pallas_call | solution.py:176
  32.1 2.5 %collective-permute-start.9 = (bf16[3,128,128]{2,1,0:T(8,128)(2,1)S(1)}, bf16[3,128,128]{2,1,0:T(8,128)(2,1)S(1)}, u32[]{:S(2)}, u32[]{:S(2)}) collective-permute-start(bf16[3,128,128]{2,1,0:T(8,128)(2,1)S(1)} %metric.1.rest_0_), channel_id=1, source_target_pairs={{0,12},{4,8},{8,4},{12,0},{1,13},{5,9},{9,5},{13,1},{2,14},{6,10},... | collective-permute-start | bytes 294920 | tf_op jit(solution)/shard_map/ppermute | solution.py:230
  34.6 1.0 %collective-permute-start.10 = (bf16[3,128,128]{2,1,0:T(8,128)(2,1)S(1)}, bf16[3,128,128]{2,1,0:T(8,128)(2,1)S(1)}, u32[]{:S(2)}, u32[]{:S(2)}) collective-permute-start(bf16[3,128,128]{2,1,0:T(8,128)(2,1)S(1)} %metric.1.rest_0_), channel_id=1, source_target_pairs={{0,8},{4,12},{8,0},{12,4},{1,9},{5,13},{9,1},{13,5},{2,10},{6,14},... | collective-permute-start | bytes 294920 | tf_op jit(solution)/shard_map/ppermute | solution.py:230
  35.6 0.9 %collective-permute-start.11 = (bf16[3,128,128]{2,1,0:T(8,128)(2,1)S(1)}, bf16[3,128,128]{2,1,0:T(8,128)(2,1)S(1)}, u32[]{:S(2)}, u32[]{:S(2)}) collective-permute-start(bf16[3,128,128]{2,1,0:T(8,128)(2,1)S(1)} %metric.1.rest_0_), channel_id=1, source_target_pairs={{0,4},{4,0},{8,12},{12,8},{1,5},{5,1},{9,13},{13,9},{2,6},{6,2},{1... | collective-permute-start | bytes 294920 | tf_op jit(solution)/shard_map/ppermute | solution.py:230
  36.5 2.1 %collective-permute-done.9.rest_1_ = bf16[3,128,128]{2,1,0:T(8,128)(2,1)S(1)} collective-permute-done((bf16[3,128,128]{2,1,0:T(8,128)(2,1)S(1)}, bf16[3,128,128]{2,1,0:T(8,128)(2,1)S(1)}, u32[]{:S(2)}, u32[]{:S(2)}) %collective-permute-start.9) | collective-permute-done | bytes 98336 | tf_op jit(solution)/shard_map/ppermute | solution.py:230
  38.7 2.7 %collective-permute-done.10.rest_2_ = bf16[3,128,128]{2,1,0:T(8,128)(2,1)S(1)} collective-permute-done((bf16[3,128,128]{2,1,0:T(8,128)(2,1)S(1)}, bf16[3,128,128]{2,1,0:T(8,128)(2,1)S(1)}, u32[]{:S(2)}, u32[]{:S(2)}) %collective-permute-start.10) | collective-permute-done | bytes 98336 | tf_op jit(solution)/shard_map/ppermute | solution.py:230
  41.4 1.6 %build_own.1 = bf16[2,8,64,128]{3,2,1,0:T(8,128)(2,1)S(1)} custom-call(s32[8,12]{1,0:T(8,128)S(1)} %get-tuple-element.17.slot_any.slot_ref, bf16[8,12,128,128]{3,2,1,0:T(8,128)(2,1)S(1)} %get-tuple-element.18.t_ref, bf16[3,128,128]{2,1,0:T(8,128)(2,1)S(1)} %metric.1.rest_0_, bf16[3,128,128]{2,1,0:T(8,128)(2,1)S(1)} %collective-permute-done.9.rest_1_, ...), custom_call_target="tpu_custom_call" | custom-call | flops 402653184 | bytes 3407872 | tf_op jit(solution)/shard_map/build_own/pallas_call | solution.py:213
  43.6 1.6 %collective-permute-start.12 = (bf16[8,64,128]{2,1,0:T(8,128)(2,1)S(1)}, bf16[8,64,128]{2,1,0:T(8,128)(2,1)S(1)}, u32[]{:S(2)}, u32[]{:S(2)}) collective-permute-start(bf16[8,64,128]{2,1,0:T(8,128)(2,1)S(1)} %slice_bitcast_fusion.2), channel_id=1, source_target_pairs={{0,2},{2,0},{1,3},{3,1},{4,6},{6,4},{5,7},{7,5},{8,10},{10,8},{9,1... | collective-permute-start | bytes 393224 | tf_op jit(solution)/shard_map/ppermute | solution.py:235
  45.2 1.6 %build_other.1 = bf16[2,8,64,128]{3,2,1,0:T(8,128)(2,1)S(1)} custom-call(s32[8,12]{1,0:T(8,128)S(1)} %get-tuple-element.17.slot_any.slot_ref, bf16[8,12,128,128]{3,2,1,0:T(8,128)(2,1)S(1)} %get-tuple-element.18.t_ref, bf16[3,128,128]{2,1,0:T(8,128)(2,1)S(1)} %collective-permute-done.13.rest_0_, bf16[3,128,128]{2,1,0:T(8,128)(2,1)S(1)} %collective-permute-done.14.rest_1_, ...), custom_call_target="tpu_custom_call" | custom-call | flops 402653184 | bytes 3407872 | tf_op jit(solution)/shard_map/build_other/pallas_call | solution.py:213
  46.8 0.9 %collective-permute-start.17 = (bf16[8,64,128]{2,1,0:T(8,128)(2,1)S(1)}, bf16[8,64,128]{2,1,0:T(8,128)(2,1)S(1)}, u32[]{:S(2)}, u32[]{:S(2)}) collective-permute-start(bf16[8,64,128]{2,1,0:T(8,128)(2,1)S(1)} %slice_bitcast_fusion), channel_id=1, source_target_pairs={{0,2},{2,0},{1,3},{3,1},{4,6},{6,4},{5,7},{7,5},{8,10},{10,8},{9,1... | collective-permute-start | bytes 393224 | tf_op jit(solution)/shard_map/ppermute | solution.py:235
  47.8 1.3 %collective-permute-done.12 = bf16[8,64,128]{2,1,0:T(8,128)(2,1)S(1)} collective-permute-done((bf16[8,64,128]{2,1,0:T(8,128)(2,1)S(1)}, bf16[8,64,128]{2,1,0:T(8,128)(2,1)S(1)}, u32[]{:S(2)}, u32[]{:S(2)}) %collective-permute-start.12) | collective-permute-done | bytes 131104 | tf_op jit(solution)/shard_map/ppermute | solution.py:235
  49.1 2.9 %collective-permute-done.17 = bf16[8,64,128]{2,1,0:T(8,128)(2,1)S(1)} collective-permute-done((bf16[8,64,128]{2,1,0:T(8,128)(2,1)S(1)}, bf16[8,64,128]{2,1,0:T(8,128)(2,1)S(1)}, u32[]{:S(2)}, u32[]{:S(2)}) %collective-permute-start.17) | collective-permute-done | bytes 131104 | tf_op jit(solution)/shard_map/ppermute | solution.py:235
  52.1 0.7 %pad_maximum_fusion = bf16[8,64,256]{2,1,0:T(8,128)(2,1)} fusion(bf16[8,64,128]{2,1,0:T(8,128)(2,1)S(1)} %get-tuple-element.30, bf16[8,64,128]{2,1,0:T(8,128)(2,1)S(1)} %get-tuple-element.29), kind=kLoop, calls=%fused_computation.1 | loop fusion | flops 524288 | bytes 524288 | tf_op jit(solution)/shard_map/concatenate | solution.py:293
  (29 shorter events, 2.2 us)
Async XLA Ops:
  3.4 2.4 %copy-start = (bf16[3,4,128,128]{3,2,1,0:T(8,128)(2,1)S(1)}, bf16[3,4,128,128]{3,2,1,0:T(8,128)(2,1)}, u32[]{:S(2)}) copy-start(bf16[3,4,128,128]{3,2,1,0:T(8,128)(2,1)} %m_ref.1) | copy-start | bytes 1179652
  3.4 8.3 %copy-start.1 = (s32[3,4]{1,0:T(4,128)S(1)}, s32[3,4]{1,0:T(4,128)}, u32[]{:S(2)}) copy-start(s32[3,4]{1,0:T(4,128)} %mine_cols.1) | copy-start | bytes 148
  3.4 2.2 %collective-permute-start = (bf16[12,128,128]{2,1,0:T(8,128)(2,1)S(1)}, bf16[12,128,128]{2,1,0:T(8,128)(2,1)S(1)}, u32[]{:S(2)}, u32[]{:S(2)}) collective-permute-start(bf16[12,128,128]{2,1,0:T(8,128)(2,1)S(1)} %get-tuple-element.20), channel_id=1, source_target_pairs={{0,1},{1,0},{2,3},{3,2},{4,5},{5,4},{6,7},{7,6},{8,9},{9,8},{10,11... | collective-permute-start | bytes 1179656 | tf_op jit(solution)/shard_map/ppermute | solution.py:230
  5.8 13.7 %collective-permute-start.4 = (bf16[3,4,128,128]{3,2,1,0:T(8,128)(2,1)S(1)}, bf16[3,4,128,128]{3,2,1,0:T(8,128)(2,1)S(1)}, u32[]{:S(2)}, u32[]{:S(2)}) collective-permute-start(bf16[3,4,128,128]{3,2,1,0:T(8,128)(2,1)S(1)} %copy-done), channel_id=1, source_target_pairs={{0,1},{1,0},{2,3},{3,2},{4,5},{5,4},{6,7},{7,6},{8,9},{9,8},{10,11... | collective-permute-start | bytes 1179656 | tf_op jit(solution)/shard_map/ppermute | solution.py:230
  5.9 8.8 %collective-permute-start.1 = (bf16[3,128,128]{2,1,0:T(8,128)(2,1)S(1)}, bf16[3,128,128]{2,1,0:T(8,128)(2,1)S(1)}, u32[]{:S(2)}, u32[]{:S(2)}) collective-permute-start(bf16[3,128,128]{2,1,0:T(8,128)(2,1)S(1)} %get-tuple-element.33), channel_id=1, source_target_pairs={{0,12},{4,8},{8,4},{12,0},{1,13},{5,9},{9,5},{13,1},{2,14},{6,10},... | collective-permute-start | bytes 294920 | tf_op jit(solution)/shard_map/ppermute | solution.py:230
  11.0 8.5 %collective-permute-start.2 = (bf16[3,128,128]{2,1,0:T(8,128)(2,1)S(1)}, bf16[3,128,128]{2,1,0:T(8,128)(2,1)S(1)}, u32[]{:S(2)}, u32[]{:S(2)}) collective-permute-start(bf16[3,128,128]{2,1,0:T(8,128)(2,1)S(1)} %get-tuple-element.32), channel_id=1, source_target_pairs={{0,8},{4,12},{8,0},{12,4},{1,9},{5,13},{9,1},{13,5},{2,10},{6,14},... | collective-permute-start | bytes 294920 | tf_op jit(solution)/shard_map/ppermute | solution.py:230
  11.0 8.5 %collective-permute-start.3 = (bf16[3,128,128]{2,1,0:T(8,128)(2,1)S(1)}, bf16[3,128,128]{2,1,0:T(8,128)(2,1)S(1)}, u32[]{:S(2)}, u32[]{:S(2)}) collective-permute-start(bf16[3,128,128]{2,1,0:T(8,128)(2,1)S(1)} %get-tuple-element.31), channel_id=1, source_target_pairs={{0,4},{4,0},{8,12},{12,8},{1,5},{5,1},{9,13},{13,9},{2,6},{6,2},{1... | collective-permute-start | bytes 294920 | tf_op jit(solution)/shard_map/ppermute | solution.py:230
  11.7 1.2 %collective-permute-start.5 = (s32[3,4]{1,0:T(4,128)S(1)}, s32[3,4]{1,0:T(4,128)S(1)}, u32[]{:S(2)}, u32[]{:S(2)}) collective-permute-start(s32[3,4]{1,0:T(4,128)S(1)} %copy-done.1), channel_id=1, source_target_pairs={{0,1},{1,0},{2,3},{3,2},{4,5},{5,4},{6,7},{7,6},{8,9},{9,8},{10,11... | collective-permute-start | bytes 152 | tf_op jit(solution)/shard_map/ppermute | solution.py:230
  19.6 4.7 %collective-permute-start.6 = (bf16[3,128,128]{2,1,0:T(8,128)(2,1)S(1)}, bf16[3,128,128]{2,1,0:T(8,128)(2,1)S(1)}, u32[]{:S(2)}, u32[]{:S(2)}) collective-permute-start(bf16[3,128,128]{2,1,0:T(8,128)(2,1)S(1)} %fusion.4), channel_id=1, source_target_pairs={{0,2},{2,0},{1,3},{3,1},{4,6},{6,4},{5,7},{7,5},{8,10},{10,8},{9,1... | collective-permute-start | bytes 294920 | tf_op jit(solution)/shard_map/ppermute | solution.py:235
  24.3 3.0 %collective-permute-start.7 = (bf16[6,128,128]{2,1,0:T(8,128)(2,1)S(1)}, bf16[6,128,128]{2,1,0:T(8,128)(2,1)S(1)}, u32[]{:S(2)}, u32[]{:S(2)}) collective-permute-start(bf16[6,128,128]{2,1,0:T(8,128)(2,1)S(1)} %pad_maximum_fusion.1.near_ref), channel_id=1, source_target_pairs={{4,8},{8,4},{5,9},{9,5},{6,10},{10,6},{7,11},{11,7},{20,24},{24,20... | collective-permute-start | bytes 589832 | tf_op jit(solution)/shard_map/ppermute | solution.py:242
  24.9 5.9 %collective-permute-start.8 = (bf16[6,128,128]{2,1,0:T(8,128)(2,1)S(1)}, bf16[6,128,128]{2,1,0:T(8,128)(2,1)S(1)}, u32[]{:S(2)}, u32[]{:S(2)}) collective-permute-start(bf16[6,128,128]{2,1,0:T(8,128)(2,1)S(1)} %pad_maximum_fusion.1.near_ref), channel_id=1, source_target_pairs={{0,4},{4,0},{8,12},{12,8},{1,5},{5,1},{9,13},{13,9},{2,6},{6,2},{1... | collective-permute-start | bytes 589832 | tf_op jit(solution)/shard_map/ppermute | solution.py:242
  32.1 6.6 %collective-permute-start.9 = (bf16[3,128,128]{2,1,0:T(8,128)(2,1)S(1)}, bf16[3,128,128]{2,1,0:T(8,128)(2,1)S(1)}, u32[]{:S(2)}, u32[]{:S(2)}) collective-permute-start(bf16[3,128,128]{2,1,0:T(8,128)(2,1)S(1)} %metric.1.rest_0_), channel_id=1, source_target_pairs={{0,12},{4,8},{8,4},{12,0},{1,13},{5,9},{9,5},{13,1},{2,14},{6,10},... | collective-permute-start | bytes 294920 | tf_op jit(solution)/shard_map/ppermute | solution.py:230
  34.6 6.8 %collective-permute-start.10 = (bf16[3,128,128]{2,1,0:T(8,128)(2,1)S(1)}, bf16[3,128,128]{2,1,0:T(8,128)(2,1)S(1)}, u32[]{:S(2)}, u32[]{:S(2)}) collective-permute-start(bf16[3,128,128]{2,1,0:T(8,128)(2,1)S(1)} %metric.1.rest_0_), channel_id=1, source_target_pairs={{0,8},{4,12},{8,0},{12,4},{1,9},{5,13},{9,1},{13,5},{2,10},{6,14},... | collective-permute-start | bytes 294920 | tf_op jit(solution)/shard_map/ppermute | solution.py:230
  35.6 5.8 %collective-permute-start.11 = (bf16[3,128,128]{2,1,0:T(8,128)(2,1)S(1)}, bf16[3,128,128]{2,1,0:T(8,128)(2,1)S(1)}, u32[]{:S(2)}, u32[]{:S(2)}) collective-permute-start(bf16[3,128,128]{2,1,0:T(8,128)(2,1)S(1)} %metric.1.rest_0_), channel_id=1, source_target_pairs={{0,4},{4,0},{8,12},{12,8},{1,5},{5,1},{9,13},{13,9},{2,6},{6,2},{1... | collective-permute-start | bytes 294920 | tf_op jit(solution)/shard_map/ppermute | solution.py:230
  36.5 8.6 %collective-permute-start.13 = (bf16[3,128,128]{2,1,0:T(8,128)(2,1)S(1)}, bf16[3,128,128]{2,1,0:T(8,128)(2,1)S(1)}, u32[]{:S(2)}, u32[]{:S(2)}) collective-permute-start(bf16[3,128,128]{2,1,0:T(8,128)(2,1)S(1)} %metric.1.rest_0_), channel_id=1, source_target_pairs={{0,1},{1,0},{2,3},{3,2},{4,5},{5,4},{6,7},{7,6},{8,9},{9,8},{10,11... | collective-permute-start | bytes 294920 | tf_op jit(solution)/shard_map/ppermute | solution.py:230
  38.7 6.5 %collective-permute-start.14 = (bf16[3,128,128]{2,1,0:T(8,128)(2,1)S(1)}, bf16[3,128,128]{2,1,0:T(8,128)(2,1)S(1)}, u32[]{:S(2)}, u32[]{:S(2)}) collective-permute-start(bf16[3,128,128]{2,1,0:T(8,128)(2,1)S(1)} %collective-permute-done.9.rest_1_), channel_id=1, source_target_pairs={{0,1},{1,0},{2,3},{3,2},{4,5},{5,4},{6,7},{7,6},{8,9},{9,8},{10,11... | collective-permute-start | bytes 294920 | tf_op jit(solution)/shard_map/ppermute | solution.py:230
  41.4 3.8 %collective-permute-start.15 = (bf16[3,128,128]{2,1,0:T(8,128)(2,1)S(1)}, bf16[3,128,128]{2,1,0:T(8,128)(2,1)S(1)}, u32[]{:S(2)}, u32[]{:S(2)}) collective-permute-start(bf16[3,128,128]{2,1,0:T(8,128)(2,1)S(1)} %collective-permute-done.10.rest_2_), channel_id=1, source_target_pairs={{0,1},{1,0},{2,3},{3,2},{4,5},{5,4},{6,7},{7,6},{8,9},{9,8},{10,11... | collective-permute-start | bytes 294920 | tf_op jit(solution)/shard_map/ppermute | solution.py:230
  43.0 2.2 %collective-permute-start.16 = (bf16[3,128,128]{2,1,0:T(8,128)(2,1)S(1)}, bf16[3,128,128]{2,1,0:T(8,128)(2,1)S(1)}, u32[]{:S(2)}, u32[]{:S(2)}) collective-permute-start(bf16[3,128,128]{2,1,0:T(8,128)(2,1)S(1)} %collective-permute-done.11.rest_3_), channel_id=1, source_target_pairs={{0,1},{1,0},{2,3},{3,2},{4,5},{5,4},{6,7},{7,6},{8,9},{9,8},{10,11... | collective-permute-start | bytes 294920 | tf_op jit(solution)/shard_map/ppermute | solution.py:230
  43.6 5.5 %collective-permute-start.12 = (bf16[8,64,128]{2,1,0:T(8,128)(2,1)S(1)}, bf16[8,64,128]{2,1,0:T(8,128)(2,1)S(1)}, u32[]{:S(2)}, u32[]{:S(2)}) collective-permute-start(bf16[8,64,128]{2,1,0:T(8,128)(2,1)S(1)} %slice_bitcast_fusion.2), channel_id=1, source_target_pairs={{0,2},{2,0},{1,3},{3,1},{4,6},{6,4},{5,7},{7,5},{8,10},{10,8},{9,1... | collective-permute-start | bytes 393224 | tf_op jit(solution)/shard_map/ppermute | solution.py:235
  46.8 5.2 %collective-permute-start.17 = (bf16[8,64,128]{2,1,0:T(8,128)(2,1)S(1)}, bf16[8,64,128]{2,1,0:T(8,128)(2,1)S(1)}, u32[]{:S(2)}, u32[]{:S(2)}) collective-permute-start(bf16[8,64,128]{2,1,0:T(8,128)(2,1)S(1)} %slice_bitcast_fusion), channel_id=1, source_target_pairs={{0,2},{2,0},{1,3},{3,1},{4,6},{6,4},{5,7},{7,5},{8,10},{10,8},{9,1... | collective-permute-start | bytes 393224 | tf_op jit(solution)/shard_map/ppermute | solution.py:235

commit v7 on v6

--- a/solution.py
+++ b/solution.py
@@ -140,13 +140,16 @@
     )(slots, own_rows, three_centre)
 
 
-def metric_kernel(owned, count, mine_cols, peer_cols, near_ref, odd_ref, even_ref, m_ref, pm_ref, out_ref, window):
+def metric_kernel(owned, count, mine_cols, peer_cols, near_ref, *rest):
+    odd_refs, even_refs, (m_ref, pm_ref, out_ref, window) = rest[:2], rest[2:-4], rest[-4:]
     me = lax.axis_index("space")
     aux = lax.axis_index("aux")
     own = owned * count
     window[:own] = near_ref[...]
-    window[own : 2 * own] = even_ref[...]
-    window[2 * own :] = odd_ref[...]
+    for begin, refs in ((own, even_refs), (2 * own, odd_refs)):
+        for ref in refs:
+            window[begin : begin + ref.shape[0]] = ref[...]
+            begin += ref.shape[0]
 
     def place(column):
         zone = column // own
@@ -175,7 +178,7 @@
     half = near.shape[1]
     return pl.pallas_call(
         functools.partial(metric_kernel, owned, count),
-        in_specs=[SMEM] * 2 + [VMEM] * 5,
+        in_specs=[SMEM] * 2 + [VMEM] * (3 + len(odd) + len(even)),
         out_specs=VMEM,
         out_shape=jax.ShapeDtypeStruct((owned, half, width), BF16),
         scratch_shapes=[pltpu.VMEM((3 * owned * count, half, width), BF16)],
@@ -186,7 +189,7 @@
             transcendentals=0,
         ),
         name="metric",
-    )(mine_cols, peer_cols, near, odd, even, m, pm)
+    )(mine_cols, peer_cols, near, *odd, *even, m, pm)
 
 
 def build_kernel(parts, order, slot_ref, t_ref, *rest):
@@ -270,11 +273,13 @@
         total = total + piece.astype(F32)
     fitted = total.astype(BF16)
 
-    near = jnp.concatenate(
-        [fitted] + [ahead_by(fitted, "aux", aux_count - k) for k in range(1, aux_count)]
-    )
-    odd = pairs_from(near, "space", 1)
-    even = pairs_from(near, "space", 0)
+    odd = [pairs_from(fitted, "space", 1)]
+    even = [pairs_from(fitted, "space", 0)]
+    rest = [ahead_by(fitted, "aux", aux_count - k) for k in range(1, aux_count)]
+    rest = jnp.concatenate(rest) if aux_count > 2 else rest[0]
+    odd.append(pairs_from(rest, "space", 1))
+    even.append(pairs_from(rest, "space", 0))
+    near = jnp.concatenate([fitted, rest])
     coefficients = metric(
         metric_columns, peer_columns, near, odd, even, metric_inverse, peer_metric, aux_count
     )

time: 53 us -> 52.9 us (level)
  waiting for transfers between devices: 23.7 us -> 20.8 us
  starting transfers between devices: 18.4 us -> 21.2 us
    ppermute x2 -> x4, starting transfers between devices: 2.95 us -> 6.34 us  [pairs_from(): return lax.ppermute(array, axis, swaps)]
    ppermute x3, waiting for transfers between devices: 7.41 us -> 4.74 us  [ahead_by(): lax.ppermute(array, axis, [(i, (i + distance) % count) for i in range(cou...]
    ppermute x2 -> x4, waiting for transfers between devices: 3.65 us -> 2.55 us  [pairs_from(): return lax.ppermute(array, axis, swaps)]
    ppermute x13, waiting for transfers between devices: 12.7 us -> 13.5 us  [exchange(): lax.ppermute(array, axis, [(i, i ^ distance) for i in range(lax.axis_size...]
    ppermute x3, starting transfers between devices: 4.04 us -> 3.39 us  [ahead_by(): lax.ppermute(array, axis, [(i, (i + distance) % count) for i in range(cou...]
  transfers between devices with their start and end apart: 18 -> 20, of which waited for: 9 -> 10; matrix products, arithmetic and copies ran while one was open for 0% -> 0% of each run, Pallas kernels for 9% -> 9%
where the time goes in v7:
time: 52.9 us; the launch traced here: 52.7 us
  starting transfers between devices  21.2 us (40%)
  waiting for transfers between devices  20.8 us (39%)
  Pallas kernels  9.52 us (18%)
  other arithmetic  1.01 us (2%)
    ppermute x13, waiting for transfers between devices, exchange(): lax.ppermute(array, axis, [(i, i ^ distance) for i in range(lax.axis_size...  13.5 us
    ppermute x13, starting transfers between devices, exchange(): lax.ppermute(array, axis, [(i, i ^ distance) for i in range(lax.axis_size...  11.4 us
    ppermute x4, starting transfers between devices, pairs_from(): return lax.ppermute(array, axis, swaps)  6.34 us
    ppermute x3, waiting for transfers between devices, ahead_by(): lax.ppermute(array, axis, [(i, (i + distance) % count) for i in range(cou...  4.74 us
    ppermute x3, starting transfers between devices, ahead_by(): lax.ppermute(array, axis, [(i, (i + distance) % count) for i in range(cou...  3.39 us
    pallas_call x1, Pallas kernels, fit_other(): pl.pallas_call(functools.partial(fit_other_kernel, owned, half, groups),...  3.39 us
    pallas_call x2, Pallas kernels, build(): pl.pallas_call(functools.partial(build_kernel, parts, order), in_specs=[S...  3.22 us
    ppermute x4, waiting for transfers between devices, pairs_from(): return lax.ppermute(array, axis, swaps)  2.55 us
  transfers between devices with their start and end apart: 20, of which 10 were waited for; matrix products, arithmetic and copies ran while one was open for 0% of the time, Pallas kernels for 9%

profile of v7, /device:TPU:0, one launch (start us, length us, event | category | flops | bytes accessed | tf_op | source)
XLA Modules:
  0.0 52.7 jit_solution(507179302523376254)
XLA Ops:
  0.0 3.4 %fit_other.1 = (bf16[12,128,128]{2,1,0:T(8,128)(2,1)S(1)}, s32[8,12]{1,0:T(8,128)S(1)}, bf16[8,128,128]{2,1,0:T(8,128)(2,1)S(1)}, bf16[8,12,128,128]{3,2,1,0:T(8,128)(2,1)S(1)}) custom-call(s32[8,12]{1,0:T(8,128)} %tile_hbm.1, s32[32]{0:T(128)} %bitcast.36, s32[32]{0:T(128)} %bitcast.37, bf16[8,128,256]{2,1,0:T(8,128)(2,1)} %d_hbm.1, ...), custom_call_target="tpu_custom_call" | custom-call | flops 402653184 | bytes 3670016 | tf_op jit(solution)/shard_map/fit_other/pallas_call | solution.py:77
  3.9 1.7 %fit_own.1 = bf16[12,128,128]{2,1,0:T(8,128)(2,1)S(1)} custom-call(s32[8,12]{1,0:T(8,128)S(1)} %get-tuple-element.17.slot_any.slot_ref, bf16[8,128,128]{2,1,0:T(8,128)(2,1)S(1)} %get-tuple-element.19.own_ref, bf16[8,12,128,128]{3,2,1,0:T(8,128)(2,1)S(1)} %get-tuple-element.18.t_ref), custom_call_target="tpu_custom_call" | custom-call | flops 402653184 | bytes 3407872 | tf_op jit(solution)/shard_map/fit_own/pallas_call | solution.py:123
  5.9 5.1 %collective-permute-start.1 = (bf16[3,128,128]{2,1,0:T(8,128)(2,1)S(1)}, bf16[3,128,128]{2,1,0:T(8,128)(2,1)S(1)}, u32[]{:S(2)}, u32[]{:S(2)}) collective-permute-start(bf16[3,128,128]{2,1,0:T(8,128)(2,1)S(1)} %get-tuple-element.33), channel_id=1, source_target_pairs={{0,12},{4,8},{8,4},{12,0},{1,13},{5,9},{9,5},{13,1},{2,14},{6,10},... | collective-permute-start | bytes 294920 | tf_op jit(solution)/shard_map/ppermute | solution.py:233
  11.7 1.2 %collective-permute-done.5.peer_cols = s32[3,4]{1,0:T(4,128)S(1)} collective-permute-done((s32[3,4]{1,0:T(4,128)S(1)}, s32[3,4]{1,0:T(4,128)S(1)}, u32[]{:S(2)}, u32[]{:S(2)}) %collective-permute-start.5) | collective-permute-done | bytes 80 | tf_op jit(solution)/shard_map/ppermute | solution.py:233
  12.8 1.9 %collective-permute-done.1 = bf16[3,128,128]{2,1,0:T(8,128)(2,1)S(1)} collective-permute-done((bf16[3,128,128]{2,1,0:T(8,128)(2,1)S(1)}, bf16[3,128,128]{2,1,0:T(8,128)(2,1)S(1)}, u32[]{:S(2)}, u32[]{:S(2)}) %collective-permute-start.1) | collective-permute-done | bytes 98336 | tf_op jit(solution)/shard_map/ppermute | solution.py:233
  14.7 4.8 %collective-permute-done.2 = bf16[3,128,128]{2,1,0:T(8,128)(2,1)S(1)} collective-permute-done((bf16[3,128,128]{2,1,0:T(8,128)(2,1)S(1)}, bf16[3,128,128]{2,1,0:T(8,128)(2,1)S(1)}, u32[]{:S(2)}, u32[]{:S(2)}) %collective-permute-start.2) | collective-permute-done | bytes 98336 | tf_op jit(solution)/shard_map/ppermute | solution.py:233
  19.6 1.6 %collective-permute-start.6 = (bf16[3,128,128]{2,1,0:T(8,128)(2,1)S(1)}, bf16[3,128,128]{2,1,0:T(8,128)(2,1)S(1)}, u32[]{:S(2)}, u32[]{:S(2)}) collective-permute-start(bf16[3,128,128]{2,1,0:T(8,128)(2,1)S(1)} %fusion.4), channel_id=1, source_target_pairs={{0,2},{2,0},{1,3},{3,1},{4,6},{6,4},{5,7},{7,5},{8,10},{10,8},{9,1... | collective-permute-start | bytes 294920 | tf_op jit(solution)/shard_map/ppermute | solution.py:238
  21.1 0.7 %collective-permute-start.7 = (bf16[3,128,128]{2,1,0:T(8,128)(2,1)S(1)}, bf16[3,128,128]{2,1,0:T(8,128)(2,1)S(1)}, u32[]{:S(2)}, u32[]{:S(2)}) collective-permute-start(bf16[3,128,128]{2,1,0:T(8,128)(2,1)S(1)} %fusion.4), channel_id=1, source_target_pairs={{4,8},{8,4},{5,9},{9,5},{6,10},{10,6},{7,11},{11,7},{20,24},{24,20... | collective-permute-start | bytes 294920 | tf_op jit(solution)/shard_map/ppermute | solution.py:245
  21.8 2.3 %collective-permute-start.9 = (bf16[3,128,128]{2,1,0:T(8,128)(2,1)S(1)}, bf16[3,128,128]{2,1,0:T(8,128)(2,1)S(1)}, u32[]{:S(2)}, u32[]{:S(2)}) collective-permute-start(bf16[3,128,128]{2,1,0:T(8,128)(2,1)S(1)} %fusion.4), channel_id=1, source_target_pairs={{0,4},{4,0},{8,12},{12,8},{1,5},{5,1},{9,13},{13,9},{2,6},{6,2},{1... | collective-permute-start | bytes 294920 | tf_op jit(solution)/shard_map/ppermute | solution.py:245
  24.2 0.7 %collective-permute-start.8 = (bf16[3,128,128]{2,1,0:T(8,128)(2,1)S(1)}, bf16[3,128,128]{2,1,0:T(8,128)(2,1)S(1)}, u32[]{:S(2)}, u32[]{:S(2)}) collective-permute-start(bf16[3,128,128]{2,1,0:T(8,128)(2,1)S(1)} %collective-permute-done.6), channel_id=1, source_target_pairs={{4,8},{8,4},{5,9},{9,5},{6,10},{10,6},{7,11},{11,7},{20,24},{24,20... | collective-permute-start | bytes 294920 | tf_op jit(solution)/shard_map/ppermute | solution.py:245
  24.9 2.7 %collective-permute-start.10 = (bf16[3,128,128]{2,1,0:T(8,128)(2,1)S(1)}, bf16[3,128,128]{2,1,0:T(8,128)(2,1)S(1)}, u32[]{:S(2)}, u32[]{:S(2)}) collective-permute-start(bf16[3,128,128]{2,1,0:T(8,128)(2,1)S(1)} %collective-permute-done.6), channel_id=1, source_target_pairs={{0,4},{4,0},{8,12},{12,8},{1,5},{5,1},{9,13},{13,9},{2,6},{6,2},{1... | collective-permute-start | bytes 294920 | tf_op jit(solution)/shard_map/ppermute | solution.py:245
  27.7 2.5 %collective-permute-done.10.rest_3_ = bf16[3,128,128]{2,1,0:T(8,128)(2,1)S(1)} collective-permute-done((bf16[3,128,128]{2,1,0:T(8,128)(2,1)S(1)}, bf16[3,128,128]{2,1,0:T(8,128)(2,1)S(1)}, u32[]{:S(2)}, u32[]{:S(2)}) %collective-permute-start.10) | collective-permute-done | bytes 98336 | tf_op jit(solution)/shard_map/ppermute | solution.py:245
  30.2 1.2 %metric.1.rest_0_ = bf16[3,128,128]{2,1,0:T(8,128)(2,1)S(1)} custom-call(s32[3,4]{1,0:T(4,128)S(1)} %copy-done.1, s32[3,4]{1,0:T(4,128)S(1)} %collective-permute-done.5.peer_cols, bf16[6,128,128]{2,1,0:T(8,128)(2,1)S(1)} %pad_maximum_fusion.1.near_ref, bf16[3,128,128]{2,1,0:T(8,128)(2,1)S(1)} %collective-permute-done.7.rest_0_, ...), custom_call_target="tpu_custom_call" | custom-call | flops 100663296 | bytes 1376256 | tf_op jit(solution)/shard_map/metric/pallas_call | solution.py:179
  31.5 2.1 %collective-permute-start.11 = (bf16[3,128,128]{2,1,0:T(8,128)(2,1)S(1)}, bf16[3,128,128]{2,1,0:T(8,128)(2,1)S(1)}, u32[]{:S(2)}, u32[]{:S(2)}) collective-permute-start(bf16[3,128,128]{2,1,0:T(8,128)(2,1)S(1)} %metric.1.rest_0_), channel_id=1, source_target_pairs={{0,12},{4,8},{8,4},{12,0},{1,13},{5,9},{9,5},{13,1},{2,14},{6,10},... | collective-permute-start | bytes 294920 | tf_op jit(solution)/shard_map/ppermute | solution.py:233
  33.5 1.5 %collective-permute-start.12 = (bf16[3,128,128]{2,1,0:T(8,128)(2,1)S(1)}, bf16[3,128,128]{2,1,0:T(8,128)(2,1)S(1)}, u32[]{:S(2)}, u32[]{:S(2)}) collective-permute-start(bf16[3,128,128]{2,1,0:T(8,128)(2,1)S(1)} %metric.1.rest_0_), channel_id=1, source_target_pairs={{0,8},{4,12},{8,0},{12,4},{1,9},{5,13},{9,1},{13,5},{2,10},{6,14},... | collective-permute-start | bytes 294920 | tf_op jit(solution)/shard_map/ppermute | solution.py:233
  35.0 0.9 %collective-permute-start.13 = (bf16[3,128,128]{2,1,0:T(8,128)(2,1)S(1)}, bf16[3,128,128]{2,1,0:T(8,128)(2,1)S(1)}, u32[]{:S(2)}, u32[]{:S(2)}) collective-permute-start(bf16[3,128,128]{2,1,0:T(8,128)(2,1)S(1)} %metric.1.rest_0_), channel_id=1, source_target_pairs={{0,4},{4,0},{8,12},{12,8},{1,5},{5,1},{9,13},{13,9},{2,6},{6,2},{1... | collective-permute-start | bytes 294920 | tf_op jit(solution)/shard_map/ppermute | solution.py:233
  35.9 2.5 %collective-permute-done.11.rest_1_ = bf16[3,128,128]{2,1,0:T(8,128)(2,1)S(1)} collective-permute-done((bf16[3,128,128]{2,1,0:T(8,128)(2,1)S(1)}, bf16[3,128,128]{2,1,0:T(8,128)(2,1)S(1)}, u32[]{:S(2)}, u32[]{:S(2)}) %collective-permute-start.11) | collective-permute-done | bytes 98336 | tf_op jit(solution)/shard_map/ppermute | solution.py:233
  38.4 2.9 %collective-permute-done.12.rest_2_ = bf16[3,128,128]{2,1,0:T(8,128)(2,1)S(1)} collective-permute-done((bf16[3,128,128]{2,1,0:T(8,128)(2,1)S(1)}, bf16[3,128,128]{2,1,0:T(8,128)(2,1)S(1)}, u32[]{:S(2)}, u32[]{:S(2)}) %collective-permute-start.12) | collective-permute-done | bytes 98336 | tf_op jit(solution)/shard_map/ppermute | solution.py:233
  41.3 1.6 %build_own.1 = bf16[2,8,64,128]{3,2,1,0:T(8,128)(2,1)S(1)} custom-call(s32[8,12]{1,0:T(8,128)S(1)} %get-tuple-element.17.slot_any.slot_ref, bf16[8,12,128,128]{3,2,1,0:T(8,128)(2,1)S(1)} %get-tuple-element.18.t_ref, bf16[3,128,128]{2,1,0:T(8,128)(2,1)S(1)} %metric.1.rest_0_, bf16[3,128,128]{2,1,0:T(8,128)(2,1)S(1)} %collective-permute-done.11.rest_1_, ...), custom_call_target="tpu_custom_call" | custom-call | flops 402653184 | bytes 3407872 | tf_op jit(solution)/shard_map/build_own/pallas_call | solution.py:216
  44.4 1.6 %build_other.1 = bf16[2,8,64,128]{3,2,1,0:T(8,128)(2,1)S(1)} custom-call(s32[8,12]{1,0:T(8,128)S(1)} %get-tuple-element.17.slot_any.slot_ref, bf16[8,12,128,128]{3,2,1,0:T(8,128)(2,1)S(1)} %get-tuple-element.18.t_ref, bf16[3,128,128]{2,1,0:T(8,128)(2,1)S(1)} %collective-permute-done.15.rest_0_, bf16[3,128,128]{2,1,0:T(8,128)(2,1)S(1)} %collective-permute-done.16.rest_1_, ...), custom_call_target="tpu_custom_call" | custom-call | flops 402653184 | bytes 3407872 | tf_op jit(solution)/shard_map/build_other/pallas_call | solution.py:216
  46.1 1.3 %collective-permute-start.19 = (bf16[8,64,128]{2,1,0:T(8,128)(2,1)S(1)}, bf16[8,64,128]{2,1,0:T(8,128)(2,1)S(1)}, u32[]{:S(2)}, u32[]{:S(2)}) collective-permute-start(bf16[8,64,128]{2,1,0:T(8,128)(2,1)S(1)} %slice_bitcast_fusion), channel_id=1, source_target_pairs={{0,2},{2,0},{1,3},{3,1},{4,6},{6,4},{5,7},{7,5},{8,10},{10,8},{9,1... | collective-permute-start | bytes 393224 | tf_op jit(solution)/shard_map/ppermute | solution.py:238
  47.3 1.7 %collective-permute-done.14 = bf16[8,64,128]{2,1,0:T(8,128)(2,1)S(1)} collective-permute-done((bf16[8,64,128]{2,1,0:T(8,128)(2,1)S(1)}, bf16[8,64,128]{2,1,0:T(8,128)(2,1)S(1)}, u32[]{:S(2)}, u32[]{:S(2)}) %collective-permute-start.14) | collective-permute-done | bytes 131104 | tf_op jit(solution)/shard_map/ppermute | solution.py:238
  49.0 2.9 %collective-permute-done.19 = bf16[8,64,128]{2,1,0:T(8,128)(2,1)S(1)} collective-permute-done((bf16[8,64,128]{2,1,0:T(8,128)(2,1)S(1)}, bf16[8,64,128]{2,1,0:T(8,128)(2,1)S(1)}, u32[]{:S(2)}, u32[]{:S(2)}) %collective-permute-start.19) | collective-permute-done | bytes 131104 | tf_op jit(solution)/shard_map/ppermute | solution.py:238
  52.0 0.7 %pad_maximum_fusion = bf16[8,64,256]{2,1,0:T(8,128)(2,1)} fusion(bf16[8,64,128]{2,1,0:T(8,128)(2,1)S(1)} %get-tuple-element.30, bf16[8,64,128]{2,1,0:T(8,128)(2,1)S(1)} %get-tuple-element.29), kind=kLoop, calls=%fused_computation.1 | loop fusion | flops 524288 | bytes 524288 | tf_op jit(solution)/shard_map/concatenate | solution.py:298
  (33 shorter events, 3.3 us)
Async XLA Ops:
  3.4 2.4 %copy-start = (bf16[3,4,128,128]{3,2,1,0:T(8,128)(2,1)S(1)}, bf16[3,4,128,128]{3,2,1,0:T(8,128)(2,1)}, u32[]{:S(2)}) copy-start(bf16[3,4,128,128]{3,2,1,0:T(8,128)(2,1)} %rest_4_.1) | copy-start | bytes 1179652
  3.4 8.3 %copy-start.1 = (s32[3,4]{1,0:T(4,128)S(1)}, s32[3,4]{1,0:T(4,128)}, u32[]{:S(2)}) copy-start(s32[3,4]{1,0:T(4,128)} %mine_cols.1) | copy-start | bytes 148
  3.4 2.2 %collective-permute-start = (bf16[12,128,128]{2,1,0:T(8,128)(2,1)S(1)}, bf16[12,128,128]{2,1,0:T(8,128)(2,1)S(1)}, u32[]{:S(2)}, u32[]{:S(2)}) collective-permute-start(bf16[12,128,128]{2,1,0:T(8,128)(2,1)S(1)} %get-tuple-element.20), channel_id=1, source_target_pairs={{0,1},{1,0},{2,3},{3,2},{4,5},{5,4},{6,7},{7,6},{8,9},{9,8},{10,11... | collective-permute-start | bytes 1179656 | tf_op jit(solution)/shard_map/ppermute | solution.py:233
  5.8 13.7 %collective-permute-start.4 = (bf16[3,4,128,128]{3,2,1,0:T(8,128)(2,1)S(1)}, bf16[3,4,128,128]{3,2,1,0:T(8,128)(2,1)S(1)}, u32[]{:S(2)}, u32[]{:S(2)}) collective-permute-start(bf16[3,4,128,128]{3,2,1,0:T(8,128)(2,1)S(1)} %copy-done), channel_id=1, source_target_pairs={{0,1},{1,0},{2,3},{3,2},{4,5},{5,4},{6,7},{7,6},{8,9},{9,8},{10,11... | collective-permute-start | bytes 1179656 | tf_op jit(solution)/shard_map/ppermute | solution.py:233
  5.9 8.8 %collective-permute-start.1 = (bf16[3,128,128]{2,1,0:T(8,128)(2,1)S(1)}, bf16[3,128,128]{2,1,0:T(8,128)(2,1)S(1)}, u32[]{:S(2)}, u32[]{:S(2)}) collective-permute-start(bf16[3,128,128]{2,1,0:T(8,128)(2,1)S(1)} %get-tuple-element.33), channel_id=1, source_target_pairs={{0,12},{4,8},{8,4},{12,0},{1,13},{5,9},{9,5},{13,1},{2,14},{6,10},... | collective-permute-start | bytes 294920 | tf_op jit(solution)/shard_map/ppermute | solution.py:233
  11.0 8.5 %collective-permute-start.2 = (bf16[3,128,128]{2,1,0:T(8,128)(2,1)S(1)}, bf16[3,128,128]{2,1,0:T(8,128)(2,1)S(1)}, u32[]{:S(2)}, u32[]{:S(2)}) collective-permute-start(bf16[3,128,128]{2,1,0:T(8,128)(2,1)S(1)} %get-tuple-element.32), channel_id=1, source_target_pairs={{0,8},{4,12},{8,0},{12,4},{1,9},{5,13},{9,1},{13,5},{2,10},{6,14},... | collective-permute-start | bytes 294920 | tf_op jit(solution)/shard_map/ppermute | solution.py:233
  11.0 8.5 %collective-permute-start.3 = (bf16[3,128,128]{2,1,0:T(8,128)(2,1)S(1)}, bf16[3,128,128]{2,1,0:T(8,128)(2,1)S(1)}, u32[]{:S(2)}, u32[]{:S(2)}) collective-permute-start(bf16[3,128,128]{2,1,0:T(8,128)(2,1)S(1)} %get-tuple-element.31), channel_id=1, source_target_pairs={{0,4},{4,0},{8,12},{12,8},{1,5},{5,1},{9,13},{13,9},{2,6},{6,2},{1... | collective-permute-start | bytes 294920 | tf_op jit(solution)/shard_map/ppermute | solution.py:233
  11.7 1.2 %collective-permute-start.5 = (s32[3,4]{1,0:T(4,128)S(1)}, s32[3,4]{1,0:T(4,128)S(1)}, u32[]{:S(2)}, u32[]{:S(2)}) collective-permute-start(s32[3,4]{1,0:T(4,128)S(1)} %copy-done.1), channel_id=1, source_target_pairs={{0,1},{1,0},{2,3},{3,2},{4,5},{5,4},{6,7},{7,6},{8,9},{9,8},{10,11... | collective-permute-start | bytes 152 | tf_op jit(solution)/shard_map/ppermute | solution.py:233
  19.6 4.7 %collective-permute-start.6 = (bf16[3,128,128]{2,1,0:T(8,128)(2,1)S(1)}, bf16[3,128,128]{2,1,0:T(8,128)(2,1)S(1)}, u32[]{:S(2)}, u32[]{:S(2)}) collective-permute-start(bf16[3,128,128]{2,1,0:T(8,128)(2,1)S(1)} %fusion.4), channel_id=1, source_target_pairs={{0,2},{2,0},{1,3},{3,1},{4,6},{6,4},{5,7},{7,5},{8,10},{10,8},{9,1... | collective-permute-start | bytes 294920 | tf_op jit(solution)/shard_map/ppermute | solution.py:238
  21.1 6.6 %collective-permute-start.7 = (bf16[3,128,128]{2,1,0:T(8,128)(2,1)S(1)}, bf16[3,128,128]{2,1,0:T(8,128)(2,1)S(1)}, u32[]{:S(2)}, u32[]{:S(2)}) collective-permute-start(bf16[3,128,128]{2,1,0:T(8,128)(2,1)S(1)} %fusion.4), channel_id=1, source_target_pairs={{4,8},{8,4},{5,9},{9,5},{6,10},{10,6},{7,11},{11,7},{20,24},{24,20... | collective-permute-start | bytes 294920 | tf_op jit(solution)/shard_map/ppermute | solution.py:245
  21.8 5.9 %collective-permute-start.9 = (bf16[3,128,128]{2,1,0:T(8,128)(2,1)S(1)}, bf16[3,128,128]{2,1,0:T(8,128)(2,1)S(1)}, u32[]{:S(2)}, u32[]{:S(2)}) collective-permute-start(bf16[3,128,128]{2,1,0:T(8,128)(2,1)S(1)} %fusion.4), channel_id=1, source_target_pairs={{0,4},{4,0},{8,12},{12,8},{1,5},{5,1},{9,13},{13,9},{2,6},{6,2},{1... | collective-permute-start | bytes 294920 | tf_op jit(solution)/shard_map/ppermute | solution.py:245
  24.2 3.4 %collective-permute-start.8 = (bf16[3,128,128]{2,1,0:T(8,128)(2,1)S(1)}, bf16[3,128,128]{2,1,0:T(8,128)(2,1)S(1)}, u32[]{:S(2)}, u32[]{:S(2)}) collective-permute-start(bf16[3,128,128]{2,1,0:T(8,128)(2,1)S(1)} %collective-permute-done.6), channel_id=1, source_target_pairs={{4,8},{8,4},{5,9},{9,5},{6,10},{10,6},{7,11},{11,7},{20,24},{24,20... | collective-permute-start | bytes 294920 | tf_op jit(solution)/shard_map/ppermute | solution.py:245
  24.9 5.3 %collective-permute-start.10 = (bf16[3,128,128]{2,1,0:T(8,128)(2,1)S(1)}, bf16[3,128,128]{2,1,0:T(8,128)(2,1)S(1)}, u32[]{:S(2)}, u32[]{:S(2)}) collective-permute-start(bf16[3,128,128]{2,1,0:T(8,128)(2,1)S(1)} %collective-permute-done.6), channel_id=1, source_target_pairs={{0,4},{4,0},{8,12},{12,8},{1,5},{5,1},{9,13},{13,9},{2,6},{6,2},{1... | collective-permute-start | bytes 294920 | tf_op jit(solution)/shard_map/ppermute | solution.py:245
  31.5 7.0 %collective-permute-start.11 = (bf16[3,128,128]{2,1,0:T(8,128)(2,1)S(1)}, bf16[3,128,128]{2,1,0:T(8,128)(2,1)S(1)}, u32[]{:S(2)}, u32[]{:S(2)}) collective-permute-start(bf16[3,128,128]{2,1,0:T(8,128)(2,1)S(1)} %metric.1.rest_0_), channel_id=1, source_target_pairs={{0,12},{4,8},{8,4},{12,0},{1,13},{5,9},{9,5},{13,1},{2,14},{6,10},... | collective-permute-start | bytes 294920 | tf_op jit(solution)/shard_map/ppermute | solution.py:233
  33.5 7.8 %collective-permute-start.12 = (bf16[3,128,128]{2,1,0:T(8,128)(2,1)S(1)}, bf16[3,128,128]{2,1,0:T(8,128)(2,1)S(1)}, u32[]{:S(2)}, u32[]{:S(2)}) collective-permute-start(bf16[3,128,128]{2,1,0:T(8,128)(2,1)S(1)} %metric.1.rest_0_), channel_id=1, source_target_pairs={{0,8},{4,12},{8,0},{12,4},{1,9},{5,13},{9,1},{13,5},{2,10},{6,14},... | collective-permute-start | bytes 294920 | tf_op jit(solution)/shard_map/ppermute | solution.py:233
  35.0 6.3 %collective-permute-start.13 = (bf16[3,128,128]{2,1,0:T(8,128)(2,1)S(1)}, bf16[3,128,128]{2,1,0:T(8,128)(2,1)S(1)}, u32[]{:S(2)}, u32[]{:S(2)}) collective-permute-start(bf16[3,128,128]{2,1,0:T(8,128)(2,1)S(1)} %metric.1.rest_0_), channel_id=1, source_target_pairs={{0,4},{4,0},{8,12},{12,8},{1,5},{5,1},{9,13},{13,9},{2,6},{6,2},{1... | collective-permute-start | bytes 294920 | tf_op jit(solution)/shard_map/ppermute | solution.py:233
  35.9 8.2 %collective-permute-start.15 = (bf16[3,128,128]{2,1,0:T(8,128)(2,1)S(1)}, bf16[3,128,128]{2,1,0:T(8,128)(2,1)S(1)}, u32[]{:S(2)}, u32[]{:S(2)}) collective-permute-start(bf16[3,128,128]{2,1,0:T(8,128)(2,1)S(1)} %metric.1.rest_0_), channel_id=1, source_target_pairs={{0,1},{1,0},{2,3},{3,2},{4,5},{5,4},{6,7},{7,6},{8,9},{9,8},{10,11... | collective-permute-start | bytes 294920 | tf_op jit(solution)/shard_map/ppermute | solution.py:233
  38.4 5.7 %collective-permute-start.16 = (bf16[3,128,128]{2,1,0:T(8,128)(2,1)S(1)}, bf16[3,128,128]{2,1,0:T(8,128)(2,1)S(1)}, u32[]{:S(2)}, u32[]{:S(2)}) collective-permute-start(bf16[3,128,128]{2,1,0:T(8,128)(2,1)S(1)} %collective-permute-done.11.rest_1_), channel_id=1, source_target_pairs={{0,1},{1,0},{2,3},{3,2},{4,5},{5,4},{6,7},{7,6},{8,9},{9,8},{10,11... | collective-permute-start | bytes 294920 | tf_op jit(solution)/shard_map/ppermute | solution.py:233
  41.3 2.8 %collective-permute-start.17 = (bf16[3,128,128]{2,1,0:T(8,128)(2,1)S(1)}, bf16[3,128,128]{2,1,0:T(8,128)(2,1)S(1)}, u32[]{:S(2)}, u32[]{:S(2)}) collective-permute-start(bf16[3,128,128]{2,1,0:T(8,128)(2,1)S(1)} %collective-permute-done.12.rest_2_), channel_id=1, source_target_pairs={{0,1},{1,0},{2,3},{3,2},{4,5},{5,4},{6,7},{7,6},{8,9},{9,8},{10,11... | collective-permute-start | bytes 294920 | tf_op jit(solution)/shard_map/ppermute | solution.py:233
  42.9 1.5 %collective-permute-start.18 = (bf16[3,128,128]{2,1,0:T(8,128)(2,1)S(1)}, bf16[3,128,128]{2,1,0:T(8,128)(2,1)S(1)}, u32[]{:S(2)}, u32[]{:S(2)}) collective-permute-start(bf16[3,128,128]{2,1,0:T(8,128)(2,1)S(1)} %collective-permute-done.13.rest_3_), channel_id=1, source_target_pairs={{0,1},{1,0},{2,3},{3,2},{4,5},{5,4},{6,7},{7,6},{8,9},{9,8},{10,11... | collective-permute-start | bytes 294920 | tf_op jit(solution)/shard_map/ppermute | solution.py:233
  43.5 5.5 %collective-permute-start.14 = (bf16[8,64,128]{2,1,0:T(8,128)(2,1)S(1)}, bf16[8,64,128]{2,1,0:T(8,128)(2,1)S(1)}, u32[]{:S(2)}, u32[]{:S(2)}) collective-permute-start(bf16[8,64,128]{2,1,0:T(8,128)(2,1)S(1)} %slice_bitcast_fusion.2), channel_id=1, source_target_pairs={{0,2},{2,0},{1,3},{3,1},{4,6},{6,4},{5,7},{7,5},{8,10},{10,8},{9,1... | collective-permute-start | bytes 393224 | tf_op jit(solution)/shard_map/ppermute | solution.py:238
  46.1 5.8 %collective-permute-start.19 = (bf16[8,64,128]{2,1,0:T(8,128)(2,1)S(1)}, bf16[8,64,128]{2,1,0:T(8,128)(2,1)S(1)}, u32[]{:S(2)}, u32[]{:S(2)}) collective-permute-start(bf16[8,64,128]{2,1,0:T(8,128)(2,1)S(1)} %slice_bitcast_fusion), channel_id=1, source_target_pairs={{0,2},{2,0},{1,3},{3,1},{4,6},{6,4},{5,7},{7,5},{8,10},{10,8},{9,1... | collective-permute-start | bytes 393224 | tf_op jit(solution)/shard_map/ppermute | solution.py:238
